TPU v7x, 32 devices: a whole 2x2x4 slice. The times are simulated.
32 devices in a mesh: dp: 8 (over z, x), mp: 4 (over y, core).
Axes of the slice: x: 2, y: 2, z: 4, core: 2. Of those that a mesh axis runs over, the one named last changes fastest.
Arguments:
- tokens: bfloat16 [16384, 512], P('dp'), may hold values from -6 to 6
- item_kind: int32 [8], P('dp'), may hold values from 0 to 1
- first_gain: float32 [512], replicated, may hold values from 0.1 to 1.9
- first_shift: float32 [512], replicated, may hold values from -1.75 to 1.75
- query_weight: bfloat16 [512, 512], P(None, 'mp'), may hold values from -0.25 to 0.25
- key_weight: bfloat16 [512, 512], P(None, 'mp'), may hold values from -0.25 to 0.25
- value_weight: bfloat16 [512, 512], P(None, 'mp'), may hold values from -0.25 to 0.25
- position_weight: bfloat16 [512, 512], P(None, 'mp'), may hold values from -0.25 to 0.25
- content_bias: float32 [512], P('mp'), may hold values from -3 to 3
- position_bias: float32 [512], P('mp'), may hold values from -3 to 3
- output_weight: bfloat16 [512, 512], P('mp'), may hold values from -1 to 1
- second_gain: float32 [512], replicated, may hold values from 0.1 to 1.9
- second_shift: float32 [512], replicated, may hold values from -1.75 to 1.75
- inner_weight: bfloat16 [512, 2048], P(None, 'mp'), may hold values from -0.25 to 0.25
- inner_bias: float32 [2048], P('mp'), may hold values from -1.75 to 1.75
- outer_weight: bfloat16 [2048, 512], P('mp'), may hold values from -0.125 to 0.125
- outer_bias: float32 [512], replicated, may hold values from -1.75 to 1.75
- cotangent: bfloat16 [16384, 512], P('dp'), may hold values from -6 to 6
Outputs:
- mixed: bfloat16 [16384, 512], P('dp')
- tokens_grad: bfloat16 [16384, 512], P('dp')
- first_gain_grad: float32 [512], replicated
- first_shift_grad: float32 [512], replicated
- query_grad: float32 [512, 512], P(None, 'mp')
- key_grad: float32 [512, 512], P(None, 'mp')
- value_grad: float32 [512, 512], P(None, 'mp')
- position_grad: float32 [512, 512], P(None, 'mp')
- content_bias_grad: float32 [512], P('mp')
- position_bias_grad: float32 [512], P('mp')
- output_grad: float32 [512, 512], P('mp')
- second_gain_grad: float32 [512], replicated
- second_shift_grad: float32 [512], replicated
- inner_grad: float32 [512, 2048], P(None, 'mp')
- inner_bias_grad: float32 [2048], P('mp')
- outer_grad: float32 [2048, 512], P('mp')
- outer_bias_grad: float32 [512], replicated
Inputs may be any that keep to these rules, and one draw needn't show every extreme that they name: `item_kind`: 0: the group's 2048 bytes are one item; 1: they are two items of 1024 bytes.
All inputs are finite; a program needn't handle non-finite values.
Results may differ from a plain program's by a relative error of at most 0.017.
Values may be sent and summed in bfloat16 or wider, within the bound.
No kernel may reach another device: no remote copies, remote signals or barrier semaphores. Data moves between devices by JAX's collectives and lax.ppermute only.
A program may use at most 128 MiB of HBM per device.

v0:
```python
import math

import jax
import jax.numpy as jnp
from jax import lax
from jax.sharding import PartitionSpec as P

DH = 64


EPS = 1e-05
NEG = -1e30


def sinusoid(count, model_width):
    distance = jnp.arange(count, dtype=jnp.float32)[:, None]
    freqs = jnp.exp(
        jnp.arange(model_width // 2, dtype=jnp.float32) * (-2.0 * math.log(10000.0) / model_width)
    )
    angles = distance * freqs[None, :]
    return jnp.concatenate([jnp.sin(angles), jnp.cos(angles)], axis=1)


def norm_parts(values):
    center = values - jnp.mean(values, axis=-1, keepdims=True)
    spread = jnp.mean(center * center, axis=-1, keepdims=True)
    scale = lax.rsqrt(spread + EPS)
    return (center * scale, scale)


def norm_back(upstream, normed, scale, gain_row):
    scaled = upstream * gain_row
    inner_term = (
        scaled
        - jnp.mean(scaled, axis=-1, keepdims=True)
        - normed * jnp.mean(scaled * normed, axis=-1, keepdims=True)
    )
    return (scale * inner_term, jnp.sum(upstream * normed, axis=0), jnp.sum(upstream, axis=0))


def head_major(rows, head_count):
    return rows.reshape(rows.shape[0], head_count, DH).transpose(1, 0, 2)


def row_major(heads):
    return heads.transpose(1, 0, 2).reshape(heads.shape[1], heads.shape[0] * heads.shape[2])


def blocks_to_rows(stacked):
    blocks, head_count, row_block, width = stacked.shape
    return row_major(stacked.transpose(1, 0, 2, 3).reshape(head_count, blocks * row_block, width))


def shear(wide, row_block, length):
    head_count = wide.shape[0]
    span = length + row_block - 1
    flat = wide.reshape(head_count, row_block * span)
    taken = flat[:, row_block - 1 : row_block - 1 + row_block * (span - 1)]
    return taken.reshape(head_count, row_block, span - 1)[:, :, :length]


def unshear(upstream, row_block, length):
    head_count = upstream.shape[0]
    span = length + row_block - 1
    padded = jnp.pad(upstream, ((0, 0), (0, 0), (0, span - 1 - length)))
    flat = padded.reshape(head_count, row_block * (span - 1))
    flat = jnp.pad(flat, ((0, 0), (row_block - 1, 1)))
    return flat.reshape(head_count, row_block, span)


def join_heads(acts, weight_rows, base):
    share = acts.shape[0] // lax.axis_size("mp")
    summed = lax.psum_scatter(
        jnp.dot(acts, weight_rows, preferred_element_type=jnp.float32),
        "mp",
        scatter_dimension=0,
        tiled=True,
    )
    summed = summed + lax.dynamic_slice_in_dim(base, lax.axis_index("mp") * share, share, 0)
    return lax.all_gather(summed, "mp", axis=0, tiled=True)


def shards(
    tokens,
    item_kind,
    first_gain,
    first_shift,
    query_weight,
    key_weight,
    value_weight,
    position_weight,
    content_bias,
    position_bias,
    output_weight,
    second_gain,
    second_shift,
    inner_weight,
    inner_bias,
    outer_weight,
    outer_bias,
    cotangent,
):
    length, model_width = tokens.shape
    columns = query_weight.shape[1]
    head_count = columns // DH
    row_block = min(512, length)
    blocks = length // row_block
    item_half = length // 2
    item_type = item_kind[0]
    inputs = tokens.astype(jnp.float32)
    normed_one, scale_one = norm_parts(inputs)
    hidden_one = (normed_one * first_gain + first_shift).astype(jnp.bfloat16)
    queries = jnp.dot(hidden_one, query_weight, preferred_element_type=jnp.float32)
    key_rows = jnp.dot(hidden_one, key_weight, preferred_element_type=jnp.float32).astype(
        jnp.bfloat16
    )
    value_rows = jnp.dot(hidden_one, value_weight, preferred_element_type=jnp.float32).astype(
        jnp.bfloat16
    )
    query_content = (queries + content_bias).astype(jnp.bfloat16)
    query_position = (queries + position_bias).astype(jnp.bfloat16)
    table_rows = sinusoid(length, model_width).astype(jnp.bfloat16)
    positions = jnp.dot(table_rows, position_weight, preferred_element_type=jnp.float32).astype(
        jnp.bfloat16
    )
    shifted = jnp.concatenate(
        [jnp.flip(positions, 0), jnp.zeros((length - 1, columns), jnp.bfloat16)], axis=0
    )
    key_heads = head_major(key_rows, head_count)
    value_heads = head_major(value_rows, head_count)
    content_heads = head_major(query_content, head_count)
    position_query_heads = head_major(query_position, head_count)
    shifted_heads = head_major(shifted, head_count)
    starts = jnp.arange(blocks, dtype=jnp.int32) * row_block
    column_ids = jnp.arange(length)

    def scores(offset, content_rows, position_rows):
        direct = jnp.einsum(
            "hqd,hkd->hqk", content_rows, key_heads, preferred_element_type=jnp.float32
        )
        relative_heads = lax.dynamic_slice_in_dim(
            shifted_heads, length - row_block - offset, length + row_block - 1, 1
        )
        wide = jnp.einsum(
            "hqd,hcd->hqc", position_rows, relative_heads, preferred_element_type=jnp.float32
        )
        logits = (direct + shear(wide, row_block, length)) * 0.125
        row_ids = offset + jnp.arange(row_block)
        allowed = (column_ids[None, :] <= row_ids[:, None]) & (
            (item_type == 0) | (row_ids[:, None] // item_half == column_ids[None, :] // item_half)
        )
        return (jnp.where(allowed[None], logits, NEG), relative_heads)

    def forward_block(offset):
        content_rows = lax.dynamic_slice_in_dim(content_heads, offset, row_block, 1)
        position_rows = lax.dynamic_slice_in_dim(position_query_heads, offset, row_block, 1)
        masked, unused_rel = scores(offset, content_rows, position_rows)
        peak = jnp.max(masked, axis=-1, keepdims=True)
        powers = jnp.exp(masked - peak)
        denominator = jnp.sum(powers, axis=-1, keepdims=True)
        probabilities = (powers / denominator).astype(jnp.bfloat16)
        mixed_rows = jnp.einsum(
            "hqk,hkd->hqd", probabilities, value_heads, preferred_element_type=jnp.float32
        )
        return (mixed_rows, (peak + jnp.log(denominator))[:, :, 0])

    attended_blocks, logsum = lax.map(forward_block, starts)
    attended = blocks_to_rows(attended_blocks).astype(jnp.bfloat16)
    residual_one = join_heads(attended, output_weight, inputs)
    normed_two, scale_two = norm_parts(residual_one)
    hidden_two = (normed_two * second_gain + second_shift).astype(jnp.bfloat16)
    preact = jnp.dot(hidden_two, inner_weight, preferred_element_type=jnp.float32) + inner_bias
    activated, gelu_pull = jax.vjp(jax.nn.gelu, preact)
    activated = activated.astype(jnp.bfloat16)
    output = join_heads(activated, outer_weight, residual_one + outer_bias)
    outer_grad = jnp.einsum("tf,td->fd", activated, cotangent, preferred_element_type=jnp.float32)
    outer_bias_grad = jnp.sum(cotangent.astype(jnp.float32), axis=0)
    activated_grad = jnp.dot(cotangent, outer_weight.T, preferred_element_type=jnp.float32)
    preact_grad = gelu_pull(activated_grad)[0].astype(jnp.bfloat16)
    inner_bias_grad = jnp.sum(preact_grad.astype(jnp.float32), axis=0)
    inner_grad = jnp.einsum(
        "td,tf->df", hidden_two, preact_grad, preferred_element_type=jnp.float32
    )
    hidden_two_grad = join_heads(
        preact_grad, inner_weight.T, jnp.zeros((length, model_width), jnp.float32)
    )
    second_term, second_gain_grad, second_shift_grad = norm_back(
        hidden_two_grad, normed_two, scale_two, second_gain
    )
    residual_grad = cotangent.astype(jnp.float32) + second_term
    branch_grad = residual_grad.astype(jnp.bfloat16)
    output_grad = jnp.einsum("tc,td->cd", attended, branch_grad, preferred_element_type=jnp.float32)
    attended_grad = jnp.dot(
        branch_grad, output_weight.T, preferred_element_type=jnp.float32
    ).astype(jnp.bfloat16)
    delta_heads_all = head_major(attended_grad, head_count)

    def backward_block(totals, pieces):
        key_total, value_total, table_total = totals
        offset, lse_rows = pieces
        content_rows = lax.dynamic_slice_in_dim(content_heads, offset, row_block, 1)
        position_rows = lax.dynamic_slice_in_dim(position_query_heads, offset, row_block, 1)
        delta_heads = lax.dynamic_slice_in_dim(delta_heads_all, offset, row_block, 1)
        masked, relative_heads = scores(offset, content_rows, position_rows)
        probabilities = jnp.exp(masked - lse_rows[:, :, None])
        value_total = value_total + jnp.einsum(
            "hqk,hqd->hkd",
            probabilities.astype(jnp.bfloat16),
            delta_heads,
            preferred_element_type=jnp.float32,
        )
        prob_grad = jnp.einsum(
            "hqd,hkd->hqk", delta_heads, value_heads, preferred_element_type=jnp.float32
        )
        score_grad = probabilities * (
            prob_grad - jnp.sum(prob_grad * probabilities, axis=-1, keepdims=True)
        )
        score_grad = score_grad.astype(jnp.bfloat16) * 0.125
        content_grad = jnp.einsum(
            "hqk,hkd->hqd", score_grad, key_heads, preferred_element_type=jnp.float32
        )
        key_total = key_total + jnp.einsum(
            "hqk,hqd->hkd", score_grad, content_rows, preferred_element_type=jnp.float32
        )
        wide_grad = unshear(score_grad, row_block, length)
        position_grad_rows = jnp.einsum(
            "hqc,hcd->hqd", wide_grad, relative_heads, preferred_element_type=jnp.float32
        )
        relative_grad = jnp.einsum(
            "hqc,hqd->hcd", wide_grad, position_rows, preferred_element_type=jnp.float32
        )
        first_row = length - row_block - offset
        current = lax.dynamic_slice_in_dim(table_total, first_row, length + row_block - 1, 1)
        table_total = lax.dynamic_update_slice_in_dim(
            table_total, current + relative_grad, first_row, 1
        )
        return ((key_total, value_total, table_total), (content_grad, position_grad_rows))

    zeros_rows = jnp.zeros((head_count, length, DH), jnp.float32)
    zeros_table = jnp.zeros((head_count, 2 * length - 1, DH), jnp.float32)
    (key_total, value_total, table_total), (content_blocks, position_blocks) = lax.scan(
        backward_block, (zeros_rows, zeros_rows, zeros_table), (starts, logsum)
    )
    content_grad = blocks_to_rows(content_blocks)
    position_query_grad = blocks_to_rows(position_blocks)
    content_bias_grad = jnp.sum(content_grad, axis=0)
    position_bias_grad = jnp.sum(position_query_grad, axis=0)
    query_low = (content_grad + position_query_grad).astype(jnp.bfloat16)
    key_low = row_major(key_total).astype(jnp.bfloat16)
    value_low = row_major(value_total).astype(jnp.bfloat16)
    positions_low = jnp.flip(row_major(table_total)[:length], 0).astype(jnp.bfloat16)
    query_grad = jnp.einsum("td,tc->dc", hidden_one, query_low, preferred_element_type=jnp.float32)
    key_grad = jnp.einsum("td,tc->dc", hidden_one, key_low, preferred_element_type=jnp.float32)
    value_grad = jnp.einsum("td,tc->dc", hidden_one, value_low, preferred_element_type=jnp.float32)
    position_grad = jnp.einsum(
        "td,tc->dc", table_rows, positions_low, preferred_element_type=jnp.float32
    )
    stacked_grads = jnp.concatenate([query_low, key_low, value_low], axis=1)
    stacked_weights = jnp.concatenate([query_weight, key_weight, value_weight], axis=1).T
    hidden_one_grad = join_heads(
        stacked_grads, stacked_weights, jnp.zeros((length, model_width), jnp.float32)
    )
    first_term, first_gain_grad, first_shift_grad = norm_back(
        hidden_one_grad, normed_one, scale_one, first_gain
    )
    tokens_grad = (residual_grad + first_term).astype(jnp.bfloat16)
    (
        first_gain_grad,
        first_shift_grad,
        query_grad,
        key_grad,
        value_grad,
        position_grad,
        content_bias_grad,
        position_bias_grad,
        output_grad,
        second_gain_grad,
        second_shift_grad,
        inner_grad,
        inner_bias_grad,
        outer_grad,
        outer_bias_grad,
    ) = lax.psum(
        (
            first_gain_grad,
            first_shift_grad,
            query_grad,
            key_grad,
            value_grad,
            position_grad,
            content_bias_grad,
            position_bias_grad,
            output_grad,
            second_gain_grad,
            second_shift_grad,
            inner_grad,
            inner_bias_grad,
            outer_grad,
            outer_bias_grad,
        ),
        "dp",
    )
    return (
        output.astype(jnp.bfloat16),
        tokens_grad,
        first_gain_grad,
        first_shift_grad,
        query_grad,
        key_grad,
        value_grad,
        position_grad,
        content_bias_grad,
        position_bias_grad,
        output_grad,
        second_gain_grad,
        second_shift_grad,
        inner_grad,
        inner_bias_grad,
        outer_grad,
        outer_bias_grad,
    )


def solution(mesh):
    return jax.shard_map(
        shards,
        mesh=mesh,
        in_specs=(
            P("dp", None),
            P("dp"),
            P(),
            P(),
            P(None, "mp"),
            P(None, "mp"),
            P(None, "mp"),
            P(None, "mp"),
            P("mp"),
            P("mp"),
            P("mp", None),
            P(),
            P(),
            P(None, "mp"),
            P("mp"),
            P("mp", None),
            P(),
            P("dp", None),
        ),
        out_specs=(
            P("dp", None),
            P("dp", None),
            P(),
            P(),
            P(None, "mp"),
            P(None, "mp"),
            P(None, "mp"),
            P(None, "mp"),
            P("mp"),
            P("mp"),
            P("mp", None),
            P(),
            P(),
            P(None, "mp"),
            P("mp"),
            P("mp", None),
            P(),
        ),
        check_vma=False,
    )
```

profile of v0, /device:TPU:0, one launch (start us, length us, event | category | flops | bytes accessed | tf_op | source)
XLA Modules:
  0.0 1759.1 jit_solution(6975366361293698121)
XLA Ops:
  40.3 462.2 %while.42 = (s32[]{:T(128)}, bf16[4,2,512,64]{2,3,1,0:T(8,128)(2,1)S(1)}, f32[4,2,512]{2,1,0:T(2,128)S(1)}, s32[4]{0:T(128)S(1)}, pred[]{:T(512)}, /*index=5*/bf...) while((s32[]{:T(128)}, ...), condition=%wide.region_5.6_spmd.clone.clone.clone, body=%wide.region_2.5_spmd.clone.clone.sunk.clone | while | flops 895376384 | bytes 153215200 | solution.py:167
  75.2 15.0 reshape.577
  90.1 16.5 reshape.578
  106.6 13.8 slice.69
  120.5 24.3 %reshape.579 = f32[2619392]{0:T(1024)} reshape(f32[2,1309696]{1,0:T(2,128)} %slice.69) | data formatting | bytes 20955136 | tf_op jit(solution)/shard_map/while
  144.8 16.4 reshape.580
  183.3 15.0 reshape.577
  198.3 16.5 reshape.578
  214.8 13.8 slice.69
  228.6 24.3 %reshape.579 = f32[2619392]{0:T(1024)} reshape(f32[2,1309696]{1,0:T(2,128)} %slice.69) | data formatting | bytes 20955136 | tf_op jit(solution)/shard_map/while
  252.9 16.4 reshape.580
  291.5 15.0 reshape.577
  306.4 16.5 reshape.578
  336.8 24.3 %reshape.579 = f32[2619392]{0:T(1024)} reshape(f32[2,1309696]{1,0:T(2,128)} %slice.69) | data formatting | bytes 20955136 | tf_op jit(solution)/shard_map/while
  361.1 16.4 reshape.580
  399.6 15.0 reshape.577
  414.6 16.5 reshape.578
  444.9 24.3 %reshape.579 = f32[2619392]{0:T(1024)} reshape(f32[2,1309696]{1,0:T(2,128)} %slice.69) | data formatting | bytes 20955136 | tf_op jit(solution)/shard_map/while
  469.2 16.4 reshape.580
  510.4 43.1 %reduce-scatter.5.cloned.1.call-done = f32[512,512]{1,0:T(8,128)} async-done(((f32[2048,512]{1,0:T(8,128)}), f32[512,512]{1,0:T(8,128)}) %reduce-scatter.5.cloned.1.call-update) | async-done | bytes 1048592 | tf_op jit(solution)/shard_map/reduce_scatter | solution.py:73
  556.3 34.6 %all-gather.5.cloned.1.call-done = f32[2048,512]{1,0:T(8,128)} async-done(((f32[512,512]{1,0:T(8,128)}), f32[2048,512]{1,0:T(8,128)}) %all-gather.5.cloned.1.call-update) | async-done | bytes 4194320 | tf_op jit(solution)/shard_map/all_gather | solution.py:80
  610.6 44.6 %reduce-scatter.9.cloned.1.call-done = f32[512,512]{1,0:T(8,128)} async-done(((f32[2048,512]{1,0:T(8,128)}), f32[512,512]{1,0:T(8,128)}) %reduce-scatter.9.cloned.1.call-update) | async-done | bytes 1048592 | tf_op jit(solution)/shard_map/reduce_scatter | solution.py:73
  660.2 30.9 %all-gather.9.cloned.1.call-done = f32[2048,512]{1,0:T(8,128)} async-done(((f32[512,512]{1,0:T(8,128)}), f32[2048,512]{1,0:T(8,128)}) %all-gather.9.cloned.1.call-update) | async-done | bytes 4194320 | tf_op jit(solution)/shard_map/all_gather | solution.py:80
  705.8 777.6 %while.43 = (s32[]{:T(128)}, f32[2,2048,64]{1,2,0:T(8,128)}, f32[2,2048,64]{1,2,0:T(8,128)}, f32[2,4095,64]{1,2,0:T(8,128)}, f32[4,2,512,64]{2,3,1,0:T(8,128)}, ...) while((s32[]{:T(128)}, f32[2,2048,64]{1,2,0:T(8,128)}, ...), condition=%wide.region_15.16_spmd.clone.clone.clone, body=%wide.region_13.15_spmd.clone.clone.sunk.clone | while | flops 2649713664 | bytes 329834336 | solution.py:241
  719.0 15.2 reshape.581
  734.2 16.6 reshape.582
  750.8 13.9 slice.71
  764.7 24.1 %reshape.583 = f32[2619392]{0:T(1024)} reshape(f32[2,1309696]{1,0:T(2,128)} %slice.71) | data formatting | bytes 20955136 | tf_op jit(solution)/shard_map/while
  788.8 17.0 reshape.584
  910.0 15.1 reshape.581
  925.1 16.6 reshape.582
  941.7 13.9 slice.71
  955.6 24.1 %reshape.583 = f32[2619392]{0:T(1024)} reshape(f32[2,1309696]{1,0:T(2,128)} %slice.71) | data formatting | bytes 20955136 | tf_op jit(solution)/shard_map/while
  979.7 17.0 reshape.584
  1102.9 15.1 reshape.581
  1118.0 16.6 reshape.582
  1134.6 13.9 slice.71
  1148.5 24.1 %reshape.583 = f32[2619392]{0:T(1024)} reshape(f32[2,1309696]{1,0:T(2,128)} %slice.71) | data formatting | bytes 20955136 | tf_op jit(solution)/shard_map/while
  1172.6 17.0 reshape.584
  1296.0 15.1 reshape.581
  1311.0 16.6 reshape.582
  1327.6 13.9 slice.71
  1341.5 24.1 %reshape.583 = f32[2619392]{0:T(1024)} reshape(f32[2,1309696]{1,0:T(2,128)} %slice.71) | data formatting | bytes 20955136 | tf_op jit(solution)/shard_map/while
  1365.7 17.0 reshape.584
  1496.7 41.5 %reduce-scatter.11.cloned.1.call-done = f32[512,512]{1,0:T(8,128)} async-done(((f32[2048,512]{1,0:T(8,128)}), f32[512,512]{1,0:T(8,128)}) %reduce-scatter.11.cloned.1.call-update) | async-done | bytes 1048592 | tf_op jit(solution)/shard_map/reduce_scatter | solution.py:73
  1562.5 35.9 %all-gather.11.cloned.1.call-done = f32[2048,512]{1,0:T(8,128)} async-done(((f32[512,512]{1,0:T(8,128)}), f32[2048,512]{1,0:T(8,128)}) %all-gather.11.cloned.1.call-update) | async-done | bytes 4194320 | tf_op jit(solution)/shard_map/all_gather | solution.py:80
  1602.3 39.4 %all-reduce.3 = (f32[512]{0:T(512)}, f32[512]{0:T(512)}, f32[128]{0:T(128)}, f32[128]{0:T(128)}, f32[512]{0:T(512)}, /*index=5*/f32[512]{0:T(512)}, f32[512]{0:T(512)}, f32[512]{0:T(512)}) all-reduce(f32[512]{0:T(512)S(1)} %get-tuple-element.644, f32[512]{0:T(512)S(1)} %get-tuple-element.649, ...), channel_id=1, replica_groups=mesh['dp'=8,'mp'=4] {'dp'}, use_global_device_ids=true, to_apply=%region_20.21 | all-reduce | flops 3328 | bytes 26624 | tf_op jit(solution)/shard_map/psum | solution.py:283
  1647.0 96.7 %all-reduce.7.cloned.1.call-done = (f32[512,128]{1,0:T(8,128)}, f32[512,128]{1,0:T(8,128)}, f32[512,128]{1,0:T(8,128)}, f32[512,128]{1,0:T(8,128)}, f32[128,512]...) async-done(((f32[512,128]{1,0:T(8,128)}, f32[512,128]{1,0:T(8,128)}, f32[512,128]{1,0:T(8,128)}, f32[512,128]{1,0:T(8,128)}, f32[128,512]{1,0:T(8,128)}, ...) | async-done | bytes 3407888 | tf_op jit(solution)/shard_map/psum | solution.py:283
  (357 shorter events, 648.7 us)
Async XLA Ops:
  7.2 593.1 %copy-start = (bf16[512,512]{1,0:T(8,128)(2,1)S(1)}, bf16[512,512]{1,0:T(8,128)(2,1)}, u32[]{:S(2)}) copy-start(bf16[512,512]{1,0:T(8,128)(2,1)} %param.37) | copy-start | bytes 1572868
  7.2 14.7 copy-start.60
  7.2 546.3 %reduce-scatter.5.cloned.1.call-start = ((), (), s32[]{:S(2)}) async-start(), calls=%async_computation.4 | async-start | bytes 5242880 | tf_op jit(solution)/shard_map/reduce_scatter | solution.py:73
  9.9 23.9 %copy-start.38 = (f32[2048]{0:T(1024)}, f32[2048]{0:T(1024)S(1)}, u32[]{:S(2)}) copy-start(f32[2048]{0:T(1024)S(1)} %broadcast_multiply_fusion.5) | copy-start | bytes 24580
  12.5 21.4 %copy-start.46 = (f32[2048]{0:T(1024)}, f32[2048]{0:T(1024)S(1)}, u32[]{:S(2)}) copy-start(f32[2048]{0:T(1024)S(1)} %add_rsqrt_fusion.1) | copy-start | bytes 24580
  12.5 21.4 %copy-start.9 = (bf16[2048,512]{1,0:T(8,128)(2,1)S(1)}, bf16[2048,512]{1,0:T(8,128)(2,1)}, u32[]{:S(2)}) copy-start(bf16[2048,512]{1,0:T(8,128)(2,1)} %param.22) | copy-start | bytes 6291460
  12.5 21.3 %copy-start.49 = (f32[512]{0:T(512)S(1)}, f32[512]{0:T(512)}, u32[]{:S(2)}) copy-start(f32[512]{0:T(512)} %param.24) | copy-start | bytes 6148
  12.5 21.3 %copy-start.54 = (f32[512]{0:T(512)S(1)}, f32[512]{0:T(512)}, u32[]{:S(2)}) copy-start(f32[512]{0:T(512)} %param.25) | copy-start | bytes 6148
  23.4 11.4 copy-start.44
  31.7 4.8 copy-start.42
  34.8 5.5 copy-start.7
  40.3 463.1 %copy-start.32 = (bf16[128,512]{1,0:T(8,128)(2,1)S(1)}, bf16[128,512]{1,0:T(8,128)(2,1)}, u32[]{:S(2)}) copy-start(bf16[128,512]{1,0:T(8,128)(2,1)} %param.32) | copy-start | bytes 393220
  506.1 84.7 %all-gather.5.cloned.1.call-start = ((), (), s32[]{:S(2)}) async-start(), calls=%async_computation.5 | async-start | bytes 5242880 | tf_op jit(solution)/shard_map/all_gather | solution.py:80
  556.2 40.3 %copy-start.48 = (f32[512]{0:T(512)S(1)}, f32[512]{0:T(512)}, u32[]{:S(2)}) copy-start(f32[512]{0:T(512)} %param.33) | copy-start | bytes 6148
  556.2 40.3 %copy-start.55 = (f32[512]{0:T(512)S(1)}, f32[512]{0:T(512)}, u32[]{:S(2)}) copy-start(f32[512]{0:T(512)} %param.34) | copy-start | bytes 6148
  556.2 99.0 %reduce-scatter.9.cloned.1.call-start = ((), (), s32[]{:S(2)}) async-start(), calls=%async_computation.8 | async-start | bytes 5242880 | tf_op jit(solution)/shard_map/reduce_scatter | solution.py:73
  610.6 80.6 %all-gather.9.cloned.1.call-start = ((), (), s32[]{:S(2)}) async-start(), calls=%async_computation.9 | async-start | bytes 5242880 | tf_op jit(solution)/shard_map/all_gather | solution.py:80
  655.3 838.2 %reduce-scatter.7.cloned.1.call-start = ((), (), s32[]{:S(2)}) async-start(), calls=%async_computation.6 | async-start | bytes 5242880 | tf_op jit(solution)/shard_map/reduce_scatter | solution.py:73
  660.2 878.0 %reduce-scatter.11.cloned.1.call-start = ((), (), s32[]{:S(2)}) async-start(), calls=%async_computation.10 | async-start | bytes 5242880 | tf_op jit(solution)/shard_map/reduce_scatter | solution.py:73
  691.2 5.5 copy-start.6
  691.2 5.9 copy-start.13
  884.0 5.2 copy-start.4
  1076.4 5.2 copy-start.4
  1269.4 5.2 copy-start.4
  1462.4 5.2 copy-start.4
  1484.7 5.2 copy-start.41
  1484.7 5.2 copy-start.43
  1484.8 5.2 copy-start.45
  1487.4 5.9 copy-start.21
  1493.3 44.9 %copy-start.15 = (bf16[2048,512]{1,0:T(8,128)(2,1)S(1)}, bf16[2048,512]{1,0:T(8,128)(2,1)}, u32[]{:S(2)}) copy-start(bf16[2048,512]{1,0:T(8,128)(2,1)} %copy-done.14) | copy-start | bytes 6291460
  1493.3 69.0 %all-gather.7.cloned.1.call-start = ((), (), s32[]{:S(2)}) async-start(), calls=%async_computation.7 | async-start | bytes 2621440 | tf_op jit(solution)/shard_map/all_gather | solution.py:80
  1496.7 101.8 %all-gather.11.cloned.1.call-start = ((), (), s32[]{:S(2)}) async-start(), calls=%async_computation.11 | async-start | bytes 5242880 | tf_op jit(solution)/shard_map/all_gather | solution.py:80
  1538.2 205.5 %all-reduce.7.cloned.1.call-start = ((), (), s32[]{:S(2)}) async-start(), calls=%async_computation.12 | async-start | bytes 6815744 | tf_op jit(solution)/shard_map/psum | solution.py:283
  1544.5 10.4 copy-start.8
  1551.7 6.1 copy-start.27
  1559.3 39.1 %copy-start.10 = (bf16[2048,512]{1,0:T(8,128)(2,1)S(1)}, bf16[2048,512]{1,0:T(8,128)(2,1)}, u32[]{:S(2)}) copy-start(bf16[2048,512]{1,0:T(8,128)(2,1)} %param.22) | copy-start | bytes 6291460
  1559.3 39.1 %copy-start.39 = (f32[2048]{0:T(1024)S(1)}, f32[2048]{0:T(1024)}, u32[]{:S(2)}) copy-start(f32[2048]{0:T(1024)} %copy-done.38) | copy-start | bytes 24580
  1559.3 39.1 %copy-start.47 = (f32[2048]{0:T(1024)S(1)}, f32[2048]{0:T(1024)}, u32[]{:S(2)}) copy-start(f32[2048]{0:T(1024)} %copy-done.46) | copy-start | bytes 24580
  1559.3 39.1 %copy-start.50 = (f32[512]{0:T(512)S(1)}, f32[512]{0:T(512)}, u32[]{:S(2)}) copy-start(f32[512]{0:T(512)} %param.24) | copy-start | bytes 6148
  1560.6 41.7 %copy-start.51 = (f32[512]{0:T(512)S(1)}, f32[512]{0:T(512)}, u32[]{:S(2)}) copy-start(f32[512]{0:T(512)} %get-tuple-element.642) | copy-start | bytes 6148
  1560.6 41.8 %copy-start.52 = (f32[512]{0:T(512)S(1)}, f32[512]{0:T(512)}, u32[]{:S(2)}) copy-start(f32[512]{0:T(512)} %get-tuple-element.648) | copy-start | bytes 6148
  1560.6 41.8 %copy-start.53 = (f32[512]{0:T(512)S(1)}, f32[512]{0:T(512)}, u32[]{:S(2)}) copy-start(f32[512]{0:T(512)} %get-tuple-element.724) | copy-start | bytes 6148
  1560.6 41.8 %copy-start.57 = (f32[512]{0:T(512)S(1)}, f32[512]{0:T(512)}, u32[]{:S(2)}) copy-start(f32[512]{0:T(512)} %get-tuple-element.715) | copy-start | bytes 6148
  1743.7 5.4 copy-start.34
  1743.7 6.1 copy-start.33
  1743.7 6.8 copy-start.29
  1743.7 7.7 copy-start.28
  1743.7 8.7 copy-start.1
  (32 other events, 97.4 us)
Sparse Core Ops, SparseCore 0:
  506.2 47.2 reduce-scatter.4
  556.3 34.4 all-gather.4
  610.7 44.4 reduce-scatter.8
  656.6 34.4 all-gather.8
  693.5 44.5 reduce-scatter.6
  1493.5 44.6 reduce-scatter.10
  1539.7 22.5 all-gather.6
  1563.9 34.4 all-gather.10
  1604.2 139.3 all-reduce.6
where the time goes:
time: 1770 us; the launch traced here: 1760 us
  local copies, waits for them, and re-layouts  977 us (55%)
  waiting for transfers between devices  329 us (19%)
  matrix products  261 us (15%)
  other arithmetic  72.1 us (4%)
  loops' own time  65.1 us (4%)
  blocking collectives  39.4 us (2%)
    while x48, local copies, waits for them, and re-layouts  406 us
    reshape x8, local copies, waits for them, and re-layouts, shear(): return taken.reshape(head_count, row_block, span - 1)[:, :, :length]  134 us
    reshape x8, local copies, waits for them, and re-layouts, shear(): flat = wide.reshape(head_count, row_block * span)  132 us
    reduce_scatter x4, waiting for transfers between devices, join_heads(): lax.psum_scatter(jnp.dot(acts, weight_rows, preferred_element_type=jnp.fl...  129 us
    slice x8, local copies, waits for them, and re-layouts, shear(): taken = flat[:, row_block - 1:row_block - 1 + row_block * (span - 1)]  111 us
    all_gather x4, waiting for transfers between devices, join_heads(): return lax.all_gather(summed, 'mp', axis=0, tiled=True)  103 us
    psum x1, waiting for transfers between devices, shards(): lax.psum((first_gain_grad, first_shift_grad, query_grad, key_grad, value_...  96.7 us
    dot_general x8, matrix products, scores(): jnp.einsum('hqd,hcd->hqc', position_rows, relative_heads, preferred_eleme...  54.6 us
  transfers between devices with their start and end apart: 9, of which 8 were waited for; matrix products, arithmetic and copies ran while one was open for 46% of the time, Pallas kernels for 0%

commit v1 on v0

v1 whole, which is shorter than its diff:
```python
import functools
import math

import jax
import jax.numpy as jnp
import numpy as np
from jax import lax
from jax.experimental import pallas as pl
from jax.experimental.pallas import tpu as pltpu
from jax.sharding import PartitionSpec as P

DH = 64
EPS = 1e-05
NEG = -1e30
LOG2E = 1.4426950408889634
GELU_A = 0.7978845608028654
GELU_B = 0.044715

f32 = jnp.float32
bf16 = jnp.bfloat16


def sinusoid(count, model_width):
    freqs = np.exp(np.arange(model_width // 2) * (-2.0 * math.log(10000.0) / model_width))
    angles = np.arange(count)[:, None] * freqs[None, :]
    return np.sin(angles), np.cos(angles)


def dot(left, right):
    return jnp.dot(left, right, preferred_element_type=f32)


def dot_nt(left, right):
    return lax.dot_general(left, right, (((1,), (1,)), ((), ())), preferred_element_type=f32)


def whole(shape):
    return pl.BlockSpec(shape, lambda *ids: (0,) * len(shape))


def params(mib=60):
    return pltpu.CompilerParams(
        vmem_limit_bytes=mib * 2**20, dimension_semantics=("arbitrary",)
    )


def cost(microseconds):
    return pl.CostEstimate(
        flops=int(microseconds * 1.1e9), bytes_accessed=1 << 10, transcendentals=0
    )


def keep_rows(values, head):
    ids = lax.broadcasted_iota(jnp.int32, values.shape, 0)
    return jnp.where(ids // DH == head, values, jnp.zeros_like(values))


def keep_cols(values, head):
    ids = lax.broadcasted_iota(jnp.int32, values.shape, 1)
    return jnp.where(ids // DH == head, values, jnp.zeros_like(values))


def norm_parts(values):
    center = values - jnp.mean(values, axis=-1, keepdims=True)
    spread = jnp.mean(center * center, axis=-1, keepdims=True)
    scale = lax.rsqrt(spread + EPS)
    return center * scale, scale


def forward_body(
    block, half_rows,
    kind, place, tokens, cot, gain, shift, wq, wk, wv, cbias, pbias, wp, st, ct, table, table_t,
    tokens_own, cot_own, normed_out, qc_out, qp_out, v_out, ktt_out, p_out, ot_out, att_out,
    linv_out,
    wcat, kcat, vt, qa, s_scr, m_scr, l_scr, acc,
):
    ib = pl.program_id(0)
    here = pl.multiple_of(ib * block, block)
    width, cols = wp.shape
    half = width // 2
    mid = block // 2
    own = tokens_own.shape[0]

    @pl.when(ib == 0)
    def start():
        for n, ref in enumerate((wq, wk, wv)):
            wcat[:, n * cols : (n + 1) * cols] = ref[...]

    at = pl.multiple_of(place[1] * own, own)
    tokens_own[...] = tokens[pl.ds(at, own), :]
    cot_own[...] = cot[pl.ds(at, own), :]
    normed, _ = norm_parts(tokens[...].astype(f32))
    normed_out[...] = normed.astype(bf16)
    hidden = (normed * gain[...] + shift[...]).astype(bf16)
    qkv = dot(hidden, wcat[...])
    queries, keys, values = (qkv[:, n * cols : (n + 1) * cols] for n in range(3))
    qc_out[...] = ((queries + cbias[...]) * 0.125).astype(bf16)
    qp_out[...] = ((queries + pbias[...]) * 0.125).astype(bf16)
    v_out[...] = values.astype(bf16)
    kcat[pl.ds(here, block), :width] = table[...]
    kcat[pl.ds(here, block), width:] = keys.astype(bf16)
    vt[:, pl.ds(here, block)] = values.T.astype(bf16)
    keys_t = keys.T.astype(bf16)
    ktt_out[:DH] = keys_t[:DH]
    ktt_out[DH : DH + width] = table_t[...]
    ktt_out[DH + width :] = keys_t[DH:]
    queries_t = queries.T
    column = lambda row: jnp.broadcast_to(row, (8, row.shape[1])).T[:, :1]
    content = ((queries_t + column(cbias[...])) * (0.125 * LOG2E)).astype(bf16)
    position = ((queries_t + column(pbias[...])) * (0.125 * LOG2E)).astype(bf16)
    for h in range(2):
        u = dot(wp[...], keep_rows(position, h))
        us, uc = u[:half], u[half:]
        to = slice(h * block, (h + 1) * block)
        qa[:half, to] = (uc * st[...] - us * ct[...]).astype(bf16)
        qa[half:width, to] = (us * st[...] + uc * ct[...]).astype(bf16)
        qa[width:, to] = keep_rows(content, h)
    lo = jnp.where((kind[0] == 1) & (ib * block >= half_rows), half_rows // block, 0)
    fold = lambda x, op: op(x.reshape(x.shape[0] // 8, 8, x.shape[1]), axis=0)
    rj = lax.broadcasted_iota(jnp.int32, (mid, block), 0)
    ri = lax.broadcasted_iota(jnp.int32, (mid, block), 1)
    first = pl.ds(here, mid)
    second = pl.ds(pl.multiple_of(here + mid, mid), mid)

    s = dot(kcat[first, :], qa[...])
    s = jnp.where(jnp.concatenate([rj <= ri] * 2, axis=1), s, NEG)
    s_scr[first, :] = s
    m_scr[...] = fold(s, jnp.max)
    for h in range(2):
        to = slice(h * block + mid, (h + 1) * block)
        s = dot(kcat[second, :], qa[:, to])
        s = jnp.where(rj[:, :mid] <= ri[:, :mid], s, NEG)
        s_scr[second, to] = s
        m_scr[:, to] = jnp.maximum(m_scr[:, to], fold(s, jnp.max))

    def score_loop(c, carry):
        rows = pl.ds(pl.multiple_of(c * block, block), block)
        s = dot(kcat[rows, :], qa[...])
        s_scr[rows, :] = s
        m_scr[...] = jnp.maximum(m_scr[...], fold(s, jnp.max))
        return carry

    lax.fori_loop(lo, ib, score_loop, 0)
    m_scr[...] = jnp.broadcast_to(jnp.max(m_scr[...], axis=0, keepdims=True), m_scr.shape)

    p = jnp.exp2(s_scr[first, :] - m_scr[0:1])
    l_scr[...] = fold(p, jnp.sum)
    low = p.astype(bf16)
    p_out[first, :] = low
    for h in range(2):
        rows = slice(DH * h, DH * h + DH)
        to = slice(h * block + mid, (h + 1) * block)
        acc[rows] = dot(vt[rows, first], low[:, h * block : (h + 1) * block])
        p = jnp.exp2(s_scr[second, to] - m_scr[0:1, to])
        l_scr[:, to] += fold(p, jnp.sum)
        part = p.astype(bf16)
        p_out[second, to] = part
        acc[rows, mid:] += dot(vt[rows, second], part)

    def prob_loop(c, carry):
        rows = pl.ds(pl.multiple_of(c * block, block), block)
        p = jnp.exp2(s_scr[rows, :] - m_scr[0:1])
        l_scr[...] += fold(p, jnp.sum)
        low = p.astype(bf16)
        p_out[rows, :] = low
        for h in range(2):
            heads = slice(DH * h, DH * h + DH)
            acc[heads] += dot(vt[heads, rows], low[:, h * block : (h + 1) * block])
        return carry

    lax.fori_loop(lo, ib, prob_loop, 0)
    inverse = 1.0 / jnp.sum(l_scr[...], axis=0, keepdims=True)
    linv_out[...] = inverse
    attended = jnp.concatenate(
        [acc[DH * h : DH * h + DH] * inverse[:, h * block : (h + 1) * block] for h in range(2)],
        axis=0,
    )
    ot_out[...] = attended
    att_out[...] = attended.T.astype(bf16)


def attention_forward(
    kind, place, tokens, cot, gain, shift, wq, wk, wv, cbias, pbias, wp, st, ct, table, table_t,
    block,
):
    length, width = table.shape
    cols = wp.shape[1]
    count = length // block
    row = lambda n, w: pl.BlockSpec((n, w), lambda i: (i, 0))
    col = lambda n, w: pl.BlockSpec((n, w), lambda i: (0, i))
    smem = pl.BlockSpec(memory_space=pltpu.SMEM)
    shape = jax.ShapeDtypeStruct
    return pl.pallas_call(
        functools.partial(forward_body, block, length // 2),
        grid=(count,),
        in_specs=[
            smem, smem, row(block, width), row(block, width),
            whole((1, width)), whole((1, width)), *[whole((width, cols))] * 3,
            whole((1, cols)), whole((1, cols)), whole((width, cols)),
            col(width // 2, block), col(width // 2, block), row(block, width), col(width, block),
        ],
        out_specs=[
            row(block // 2, width), row(block // 2, width), row(block, width),
            row(block, cols), row(block, cols), row(block, cols), col(cols + width, block),
            col(length, 2 * block), col(cols, block), row(block, cols), col(1, 2 * block),
        ],
        out_shape=[
            shape((length // 2, width), bf16), shape((length // 2, width), bf16),
            shape((length, width), bf16),
            shape((length, cols), bf16), shape((length, cols), bf16), shape((length, cols), bf16),
            shape((cols + width, length), bf16),
            shape((length, 2 * length), bf16), shape((cols, length), f32),
            shape((length, cols), bf16), shape((1, 2 * length), f32),
        ],
        scratch_shapes=[
            pltpu.VMEM((width, 3 * cols), bf16),
            pltpu.VMEM((length, width + cols), bf16),
            pltpu.VMEM((cols, length), bf16),
            pltpu.VMEM((width + cols, 2 * block), bf16),
            pltpu.VMEM((length, 2 * block), f32),
            pltpu.VMEM((8, 2 * block), f32),
            pltpu.VMEM((8, 2 * block), f32),
            pltpu.VMEM((cols, block), f32),
        ],
        compiler_params=params(),
        cost_estimate=cost(25),
        name="attention_forward",
    )(
        kind, place, tokens, cot, gain, shift, wq, wk, wv, cbias, pbias, wp, st, ct, table, table_t
    )


def backward_body(
    count, block, half_rows,
    kind, place, p, d0, d1, d2, d3, ot, linv, qc, qp, v, ktt, wp, st, ct,
    wq, wk, wv, normed, gain, shift, sums,
    last, near, mine,
    wcat, acc, dk, dv, low, low_t, d_scr, dcat, dstack, qstack, delta, mom, colsum, dwp, cb, pb,
):
    step = pl.program_id(0)
    ib = count - 1 - step
    width, cols = wp.shape
    half = width // 2
    mid = block // 2
    own = d0.shape[0] // 2

    @pl.when(step == 0)
    def start():
        for ref in (dk, dv, dwp, cb, pb, mom, colsum):
            ref[...] = jnp.zeros(ref.shape, f32)
        for n, ref in enumerate((wq, wk, wv)):
            wcat[:, n * cols : (n + 1) * cols] = ref[...]
        for n, ref in enumerate((d0, d1, d2, d3)):
            for part in range(2):
                at = pl.multiple_of((4 * part + (place[0] ^ n)) * own, own)
                d_scr[pl.ds(at, own), :] = ref[part * own : (part + 1) * own]

    lo = jnp.where((kind[0] == 1) & (ib * block >= half_rows), half_rows // block, 0)
    here = pl.multiple_of(ib * block, block)
    dt = d_scr[pl.ds(here, block), :].astype(f32).T
    scaled = jnp.concatenate(
        [
            dt[DH * h : DH * h + DH] * linv[:, h * block : (h + 1) * block]
            for h in range(2)
        ],
        axis=0,
    )
    scaled_rows = scaled.T.astype(bf16)
    scaled = scaled.astype(bf16)
    product = scaled.astype(f32) * ot[...]
    for h in range(2):
        to = slice(h * block, (h + 1) * block)
        dcat[:, to] = keep_rows(scaled, h)
        dstack[to] = keep_cols(scaled_rows, h)
        qstack[to] = keep_cols(qc[...], h)
        delta[:, to] = jnp.sum(product[DH * h : DH * h + DH], axis=0, keepdims=True)

    first = pl.ds(here, mid)
    second = pl.ds(pl.multiple_of(here + mid, mid), mid)
    pt = p[first, :]
    dp = dot(v[first, :], dcat[...])
    ds = (pt.astype(f32) * (dp - delta[...])).astype(bf16)
    dv[first, :] += dot(pt, dstack[...])
    dk[first, :] += dot(ds, qstack[...])
    for h in range(2):
        to = slice(h * block + mid, (h + 1) * block)
        rows = slice(DH * h, DH * h + DH + width)
        acc[h] = dot(ktt[rows, first], ds[:, h * block : (h + 1) * block])
        pt2 = p[second, to]
        dp2 = dot(v[second, :], dcat[:, to])
        ds2 = (pt2.astype(f32) * (dp2 - delta[:, to])).astype(bf16)
        dv[second, :] += dot(pt2, dstack[to])
        dk[second, :] += dot(ds2, qstack[to])
        acc[h, :, mid:] += dot(ktt[rows, second], ds2)

    def loop(c, carry):
        rows = pl.ds(pl.multiple_of(c * block, block), block)
        pt = p[rows, :]
        dp = dot(v[rows, :], dcat[...])
        ds = (pt.astype(f32) * (dp - delta[...])).astype(bf16)
        dv[rows, :] += dot(pt, dstack[...])
        dk[rows, :] += dot(ds, qstack[...])
        for h in range(2):
            acc[h] += dot(
                ktt[DH * h : DH * h + DH + width, rows], ds[:, h * block : (h + 1) * block]
            )
        return carry

    lax.fori_loop(lo, ib, loop, 0)
    wpt = wp[...].astype(f32).T.astype(bf16)
    dqs = []
    for h in range(2):
        base = DH * (1 - h)
        gs = acc[h, base : base + half]
        gc = acc[h, base + half : base + width]
        rs = (st[...] * gc - ct[...] * gs).astype(bf16)
        rc = (ct[...] * gc + st[...] * gs).astype(bf16)
        wh = wpt[DH * h : DH * h + DH]
        by_position = (dot(wh[:, :half], rs) + dot(wh[:, half:], rc)) * 0.125
        by_content = acc[h, width * h : width * h + DH] * 0.125
        qph = keep_cols(qp[...], h)
        dwp[:half] += dot(rs, qph)
        dwp[half:] += dot(rc, qph)
        cb[DH * h : DH * h + DH] += by_content
        pb[DH * h : DH * h + DH] += by_position
        dqs.append(by_content + by_position)
    dqt = jnp.concatenate(dqs, axis=0)
    rows = pl.ds(here, block)
    for n, (value, value_t) in enumerate(
        ((dqt.T, dqt), (dk[rows, :], dk[rows, :].T), (dv[rows, :], dv[rows, :].T))
    ):
        to = slice(n * cols, (n + 1) * cols)
        low[:, to] = value.astype(bf16)
        low_t[to] = value_t.astype(bf16)
    mom[...] += dot(low_t[...], normed[...])
    colsum[...] += jnp.sum(low[...].astype(f32), axis=0, keepdims=True)
    for ref, core in ((near, 1 - place[1]), (mine, place[1])):
        at = pl.multiple_of(core * own, own)
        ref[...] = dot_nt(low[pl.ds(at, own), :], wcat[...]).astype(ref.dtype)

    @pl.when(step == count - 1)
    def finish():
        as_row = lambda values: jnp.broadcast_to(
            jnp.sum(values, axis=1, keepdims=True), (values.shape[0], 128)
        ).T[:1]
        parts = last.shape[0]
        share = width // parts
        extra = cols // parts
        column = jnp.broadcast_to(colsum[...], (8, 3 * cols)).T[:, :1]
        weights = wcat[...].astype(f32).T
        by_gain = jnp.sum(mom[...] * weights, axis=0, keepdims=True)
        by_shift = jnp.sum(column * weights, axis=0, keepdims=True)
        full = (gain[...] * mom[...] + shift[...] * column).T.astype(bf16)
        biases = jnp.concatenate(
            [as_row(cb[...]), as_row(pb[...]), jnp.zeros((1, width - 2 * cols), f32)], axis=1
        )
        tail = jnp.concatenate(
            [by_gain, by_shift, sums[...], biases, jnp.zeros((10, width), f32)], axis=0
        ).astype(bf16)
        by_table = dwp[...].astype(bf16)
        for r in range(parts):
            at = slice(r * share, (r + 1) * share)
            last[r, :extra] = jnp.zeros((extra, width), bf16)
            last[r, extra : extra + share, : 3 * cols] = full[at]
            last[r, extra : extra + share, 3 * cols :] = by_table[at]
            last[r, extra + share :] = tail


def attention_backward(
    kind, place, p, grads, ot, linv, qc, qp, v, ktt, wp, st, ct, wq, wk, wv, normed,
    gain, shift, sums, block,
):
    length, width = normed.shape
    cols = qc.shape[1]
    count = length // block
    quarter = length // 4
    col = lambda n, w: pl.BlockSpec((n, w), lambda i: (0, count - 1 - i))
    row = lambda n, w: pl.BlockSpec((n, w), lambda i: (count - 1 - i, 0))
    smem = pl.BlockSpec(memory_space=pltpu.SMEM)
    parts = first_parts()
    message = (parts, (width + cols) // parts + 16, width)
    return pl.pallas_call(
        functools.partial(backward_body, count, block, length // 2),
        grid=(count,),
        in_specs=[
            smem, smem, col(length, 2 * block),
            *[whole((quarter, cols))] * 4,
            col(cols, block), col(1, 2 * block), row(block, cols), row(block, cols),
            whole(v.shape), whole(ktt.shape), whole(wp.shape),
            col(width // 2, block), col(width // 2, block),
            *[whole((width, cols))] * 3, row(block, width),
            whole(gain.shape), whole(shift.shape), whole(sums.shape),
        ],
        out_specs=[whole(message), row(block // 2, width), row(block // 2, width)],
        out_shape=[
            jax.ShapeDtypeStruct(message, bf16),
            jax.ShapeDtypeStruct((length // 2, width), bf16),
            jax.ShapeDtypeStruct((length // 2, width), f32),
        ],
        scratch_shapes=[
            pltpu.VMEM((width, 3 * cols), bf16),
            pltpu.VMEM((2, DH + width, block), f32),
            pltpu.VMEM((length, cols), f32),
            pltpu.VMEM((length, cols), f32),
            pltpu.VMEM((block, 3 * cols), bf16),
            pltpu.VMEM((3 * cols, block), bf16),
            pltpu.VMEM((length, cols), bf16),
            pltpu.VMEM((cols, 2 * block), bf16),
            pltpu.VMEM((2 * block, cols), bf16),
            pltpu.VMEM((2 * block, cols), bf16),
            pltpu.VMEM((1, 2 * block), f32),
            pltpu.VMEM((3 * cols, width), f32),
            pltpu.VMEM((1, 3 * cols), f32),
            pltpu.VMEM((width, cols), f32),
            pltpu.VMEM((cols, block), f32),
            pltpu.VMEM((cols, block), f32),
        ],
        compiler_params=params(),
        cost_estimate=cost(100),
        name="attention_backward",
    )(
        kind, place, p, *grads, ot, linv, qc, qp, v, ktt, wp, st, ct, wq, wk, wv, normed,
        gain, shift, sums,
    )


def feed_body(
    place, tokens, cot, own_att, a1, a2, a3, w0, w1, w2, w3, i0, i1, u0, u1, b0, b1,
    bu, gain, shift,
    back_keep, back_send, out_keep, out_send, res_own, grad0, grad1,
    back_scr, res_scr, sum0, sum1,
):
    step = pl.program_id(0)
    own, width = res_own.shape
    cols = a1.shape[1]
    share = i0.shape[1]
    c = cot[...]
    residual = tokens[...].astype(f32)
    residual = residual + dot(own_att[...].reshape(2 * own, cols), w0[...])
    for att, wo in ((a1, w1), (a2, w2), (a3, w3)):
        residual = residual + dot(att[...], wo[...])
    res_scr[...] = residual
    normed, _ = norm_parts(residual)
    hidden = (normed * gain[...] + shift[...]).astype(bf16)
    hidden_t = hidden.T
    mixed = None
    back = None
    for n, wi, wu, bi, total in ((0, i0, u0, b0, sum0), (1, i1, u1, b1, sum1)):
        x = dot(hidden, wi[...]) + bi[...]
        square = x * x
        t = jnp.tanh(GELU_A * x * (1.0 + GELU_B * square))
        act = (0.5 * x * (1.0 + t)).astype(bf16)
        slope = 0.5 * (1.0 + t) + (0.5 * GELU_A) * x * (1.0 - t * t) * (
            1.0 + (3.0 * GELU_B) * square
        )
        out_n = dot(act, wu[...])
        pre = (dot_nt(c, wu[...]) * slope).astype(bf16)
        back_n = dot_nt(pre, wi[...])
        mixed = out_n if mixed is None else mixed + out_n
        back = back_n if back is None else back + back_n
        inner = dot(hidden_t, pre)
        outer = dot(act.T, c)
        bias = jnp.sum(pre.astype(f32), axis=0, keepdims=True)
        bias = jnp.broadcast_to(bias, (16, share))

        @pl.when(step == 0)
        def first(total=total, inner=inner, outer=outer, bias=bias):
            total[:width] = inner
            total[width : width + share] = outer
            total[width + share :] = bias

        @pl.when(step > 0)
        def later(total=total, inner=inner, outer=outer, bias=bias):
            total[:width] += inner
            total[width : width + share] += outer
            total[width + share :] += bias

    back_scr[...] = back
    mine = pl.multiple_of(place[2] * own, own)
    other = pl.multiple_of((1 - place[2]) * own, own)
    res_own[...] = res_scr[pl.ds(mine, own), :]
    back_keep[...] = back_scr[pl.ds(mine, own), :]
    back_send[...] = back_scr[pl.ds(other, own), :].astype(bf16)
    out_keep[...] = mixed + residual + bu[...]
    out_send[...] = mixed.astype(bf16)

    @pl.when(step == pl.num_programs(0) - 1)
    def finish():
        parts = grad0.shape[0]
        mid = width // parts
        end = mid + share // parts
        for total, grad in ((sum0, grad0), (sum1, grad1)):
            bias = total[width + share :].astype(bf16)
            for r in range(parts):
                grad[r, :mid] = total[r * mid : (r + 1) * mid].astype(bf16)
                at = width + r * (end - mid)
                grad[r, mid:end] = total[at : at + end - mid].astype(bf16)
                grad[r, end:] = bias


def feed(place, tokens, cot, own_att, atts, wos, wis, wus, bis, bu, gain, shift):
    rows, width = tokens.shape
    cols = own_att.shape[1]
    share = wis[0].shape[1]
    own = rows // 4
    spec = lambda s: pl.BlockSpec(s, lambda i, place: (0,) * len(s))
    step = lambda n, w: pl.BlockSpec((n, w), lambda i, place: (i, 0))
    parts = first_parts()
    grad_shape = (parts, (width + share) // parts + 16, width)
    att = pl.BlockSpec((1, 2, 1, own, cols), lambda i, place: (i, 0, place[1], 0, 0))
    others = (*wos, *wis, *wus, *bis, bu, gain, shift)
    shape = jax.ShapeDtypeStruct
    return pl.pallas_call(
        feed_body,
        grid_spec=pltpu.PrefetchScalarGridSpec(
            num_scalar_prefetch=1,
            grid=(2,),
            in_specs=[step(2 * own, width), step(2 * own, width), att]
            + [step(2 * own, cols)] * 3
            + [spec(o.shape) for o in others],
            out_specs=[
                step(own, width), step(own, width), step(2 * own, width), step(2 * own, width),
                step(own, width), spec(grad_shape), spec(grad_shape),
            ],
            scratch_shapes=[pltpu.VMEM((2 * own, width), f32)] * 2
            + [pltpu.VMEM((width + share + 16, width), f32)] * 2,
        ),
        out_shape=[
            shape((2 * own, width), f32), shape((2 * own, width), bf16),
            shape((rows, width), f32), shape((rows, width), bf16),
            shape((2 * own, width), f32), shape(grad_shape, bf16), shape(grad_shape, bf16),
        ],
        compiler_params=params(),
        cost_estimate=cost(13),
        name="feed",
    )(place, tokens, cot, own_att.reshape(2, 2, 2, own, cols), *atts, *others)


def turn_body(
    place, keep, got, residual, cot, a0, a1, a2, a3, w0, w1, w2, w3, gain,
    res_out, sums_out, g0, g1, g2, g3, o0, o1, o2, o3, total,
):
    step = pl.program_id(0)
    back = keep[...] + got[...].astype(f32)
    c = cot[...].astype(f32)
    normed, scale = norm_parts(residual[...])
    fold = lambda values: jnp.sum(values, axis=0, keepdims=True)
    sums = jnp.concatenate([fold(back * normed), fold(back), fold(c)], axis=0)
    e = back * gain[...]
    inner = (
        e
        - jnp.mean(e, axis=-1, keepdims=True)
        - normed * jnp.mean(e * normed, axis=-1, keepdims=True)
    )
    res = c + scale * inner
    res_out[...] = res
    branch = res.astype(bf16)
    for wo, out in ((w0, g0), (w1, g1), (w2, g2), (w3, g3)):
        out[...] = dot_nt(branch, wo[...]).astype(bf16)
    products = [dot(att[...].T, branch) for att in (a0, a1, a2, a3)]

    @pl.when(step == 0)
    def first():
        sums_out[...] = sums
        for n in range(4):
            total[n] = products[n]

    @pl.when(step == 1)
    def second():
        sums_out[...] += sums
        for n, out in enumerate((o0, o1, o2, o3)):
            out[...] = (total[n] + products[n]).astype(out.dtype)


def turn(place, keep, got, residual, cot, own_att, others, wos, gain):
    rows, width = keep.shape
    own = rows // 2
    cols = wos[0].shape[0]
    spec = lambda s: pl.BlockSpec(s, lambda i, place: (0,) * len(s))
    step = lambda w: pl.BlockSpec((own, w), lambda i, place: (i, 0))
    half = lambda w: pl.BlockSpec((own, w), lambda i, place: (2 * i + place[2], 0))
    shapes = [((rows, width), f32), ((3, width), f32)]
    shapes = shapes + [((rows, cols), bf16)] * 4
    shapes = shapes + [((cols, width), t) for t in (f32, bf16, bf16, bf16)]
    return pl.pallas_call(
        turn_body,
        grid_spec=pltpu.PrefetchScalarGridSpec(
            num_scalar_prefetch=1,
            grid=(2,),
            in_specs=[step(width), step(width), step(width), half(width)]
            + [pl.BlockSpec((own, cols), lambda i, place: (4 * i + place[0], 0))]
            + [half(cols)] * 3
            + [spec(w.shape) for w in wos]
            + [spec(gain.shape)],
            out_specs=[step(width), spec((3, width))]
            + [step(cols)] * 4
            + [spec((cols, width))] * 4,
            scratch_shapes=[pltpu.VMEM((4, cols, width), f32)],
        ),
        out_shape=[jax.ShapeDtypeStruct(s, t) for s, t in shapes],
        compiler_params=params(),
        cost_estimate=cost(60),
        name="turn",
    )(place, keep, got, residual, cot, own_att, *others, *wos, gain)


def close_body(place, keep0, keep1, near0, near1, got, t0, t1, res, gain, out):
    own = t0.shape[0]
    for part, keep, near, tokens in ((0, keep0, near0, t0), (1, keep1, near1, t1)):
        rows = slice(part * own, (part + 1) * own)
        total = keep[...] + near[...].astype(f32) + got[rows].astype(f32)
        normed, scale = norm_parts(tokens[...].astype(f32))
        e = total * gain[...]
        inner = (
            e
            - jnp.mean(e, axis=-1, keepdims=True)
            - normed * jnp.mean(e * normed, axis=-1, keepdims=True)
        )
        out[rows] = (res[rows] + scale * inner).astype(bf16)


def close(place, keep, near, got, tokens, res, gain):
    rows, width = got.shape
    own = rows // 2
    spec = pl.BlockSpec((rows, width), lambda i, place: (0, 0))
    at = lambda part: pl.BlockSpec((own, width), lambda i, place: (2 * part + place[2], 0))
    return pl.pallas_call(
        close_body,
        grid_spec=pltpu.PrefetchScalarGridSpec(
            num_scalar_prefetch=1,
            grid=(1,),
            in_specs=[
                at(0), at(1), at(0), at(1), spec, at(0), at(1), spec,
                pl.BlockSpec((1, width), lambda i, place: (0, 0)),
            ],
            out_specs=spec,
        ),
        out_shape=jax.ShapeDtypeStruct((rows, width), bf16),
        compiler_params=params(),
        cost_estimate=cost(2),
        name="close",
    )(place, keep, keep, near, near, got, tokens, tokens, res, gain)


def collect_body(place, m0, m1, g0, g1, g2, g3, mixed, grad):
    own = g0.shape[0] // 2
    core, high = place[1], place[2]
    for part in range(2):
        for flip, ref in ((0, m0), (1, m1)):
            for at_high in range(2):
                put = pl.multiple_of((4 * part + 2 * at_high + (core ^ flip)) * own, own)
                mixed[pl.ds(put, own), :] = ref[(2 * part + at_high) * own :][:own]
        for n, ref in enumerate((g0, g1, g2, g3)):
            put = pl.multiple_of((4 * part + (place[0] ^ n)) * own, own)
            grad[pl.ds(put, own), :] = ref[part * own : (part + 1) * own]


def collect(place, mixed, grads):
    rows, width = grads[0].shape
    vmem = pl.BlockSpec(memory_space=pltpu.VMEM)
    shape = jax.ShapeDtypeStruct((4 * rows, width), bf16)
    return pl.pallas_call(
        collect_body,
        in_specs=[pl.BlockSpec(memory_space=pltpu.SMEM)] + [vmem] * 6,
        out_specs=[vmem] * 2,
        out_shape=[shape] * 2,
        compiler_params=pltpu.CompilerParams(vmem_limit_bytes=60 * 2**20),
        cost_estimate=cost(3),
        name="collect",
    )(place, *mixed, *grads)


def swap(value, axis, mask):
    size = lax.axis_size(axis)
    return lax.ppermute(value, axis, [(i, i ^ mask) for i in range(size)])


def block_of(value, index, count):
    return lax.dynamic_slice_in_dim(value, index * count, count, 0)


def gather_mp(value):
    beyond = swap(value, "mp", 2)
    return [value, swap(value, "mp", 1), beyond, swap(beyond, "mp", 1)]


def levels(size):
    bits = size.bit_length() - 1
    out = []
    shift = 0
    while shift < bits:
        wide = min(3, bits - shift)
        out.append((shift, wide))
        shift += wide
    return out


def groups_of(shift, wide):
    size = lax.axis_size("dp")
    count = 1 << wide
    return [
        [base + (n << shift) for n in range(count)]
        for base in range(size)
        if not (base >> shift) & (count - 1)
    ]


def exchange(value, shift, wide):
    return lax.all_to_all(
        value, "dp", split_axis=0, concat_axis=0, tiled=True,
        axis_index_groups=None if 1 << wide == lax.axis_size("dp") else groups_of(shift, wide),
    )


def gather_dp(value):
    sizes = [1 << wide for _, wide in levels(lax.axis_size("dp"))]
    whole_value = lax.all_gather(value, "dp", axis=0)
    if len(sizes) > 1:
        whole_value = whole_value.reshape(*sizes[::-1], *value.shape)
        whole_value = whole_value.transpose(
            *reversed(range(len(sizes))), len(sizes), len(sizes) + 1
        )
    return whole_value.reshape(sizes[0], -1, value.shape[1])


def first_parts():
    return 1 << levels(lax.axis_size("dp"))[0][1]


def reduce_dp(parts, before=None):
    for at, (shift, wide) in enumerate(levels(lax.axis_size("dp"))):
        if at:
            count = 1 << wide
            small = jnp.broadcast_to(total[None, -16:], (count, 16, total.shape[1]))
            rows = total[:-16].reshape(count, -1, total.shape[1])
            parts = jnp.concatenate([rows, small], axis=1).astype(bf16)
        got = exchange(parts, shift, wide)
        if before is not None:
            got, before = lax.optimization_barrier((got, before))
        total = jnp.sum(got.astype(f32), axis=0)
    return total[:-16].astype(bf16), total[-16:], before


def spread_dp(value):
    for shift, wide in reversed(levels(lax.axis_size("dp"))):
        count = 1 << wide
        parts = jnp.broadcast_to(value[None], (count,) + value.shape)
        value = exchange(parts, shift, wide).reshape((count * value.shape[0],) + value.shape[1:])
    return value.reshape(first_parts(), -1, value.shape[1])


def shards(
    tokens, item_kind, first_gain, first_shift, query_weight, key_weight, value_weight,
    position_weight, content_bias, position_bias, output_weight, second_gain, second_shift,
    inner_weight, inner_bias, outer_weight, outer_bias, cotangent,
):
    length, width = tokens.shape
    cols = query_weight.shape[1]
    share = inner_weight.shape[1]
    mp = lax.axis_index("mp").astype(jnp.int32)
    core, high = mp & 1, mp >> 1
    place = jnp.stack([mp, core, high])
    half = length // 2
    block = min(512, half)
    per_half = half // block
    own = half // 4
    sin_table, cos_table = sinusoid(length, width)
    table = jnp.asarray(np.concatenate([sin_table, cos_table], axis=1), bf16)
    table_t = jnp.asarray(np.concatenate([sin_table, cos_table], axis=1).T, bf16)
    st = jnp.asarray(sin_table.T, f32)
    ct = jnp.asarray(cos_table.T, f32)
    gain1, shift1, gain2, shift2, bu = (
        v[None] for v in (first_gain, first_shift, second_gain, second_shift, outer_bias)
    )

    tie = lax.optimization_barrier
    wos = [output_weight] + [swap(output_weight, "mp", n) for n in (1, 2, 3)]
    wis = [inner_weight, swap(inner_weight, "mp", 1)]
    wus = [outer_weight, swap(outer_weight, "mp", 1)]
    bis = [inner_bias[None], swap(inner_bias[None], "mp", 1)]

    projections = (query_weight, key_weight, value_weight)
    tokens_own, cot_own, normed, qc, qp, v, ktt, p, ot, attended, linv = attention_forward(
        item_kind, place, tokens, cotangent, gain1, shift1, *projections, content_bias[None],
        position_bias[None], position_weight, st, ct, table, table_t, block,
    )
    blocks = attended.reshape(4, 2, own, cols)
    pick = lambda c: lax.dynamic_index_in_dim(blocks, c, 1, False).reshape(4 * own, cols)
    near, far = pick(1 - core), pick(core)
    atts = [swap(near, "mp", 1), swap(far, "mp", 2), swap(near, "mp", 3)]
    back_keep, back_send, out_keep, out_send, residual, keep, near = feed(
        place, tokens_own, cot_own, attended, atts, wos, wis, wus, bis, bu, gain2, shift2
    )
    back_got = swap(back_send, "mp", 2)
    near_got = swap(near, "mp", 1)
    feed_sum = (keep.astype(f32) + near_got.astype(f32)).astype(bf16)
    feed_part, feed_small, _ = reduce_dp(feed_sum)

    res, sums, *turned = turn(
        place, back_keep, back_got, residual, cot_own, attended, atts, wos, gain2
    )
    grads, weight_parts = turned[:4], turned[4:]
    grads = [grads[0]] + [swap(grads[n], "mp", n) for n in (1, 2, 3)]
    grads, weight_parts, out_send, feed_part = tie(
        (grads, weight_parts, out_send, feed_part)
    )
    feed_total = spread_dp(feed_part)
    weight_parts = [weight_parts[0]] + [swap(weight_parts[n], "mp", n) for n in (1, 2, 3)]
    out_got = swap(out_send, "mp", 2)

    last, near, keep = attention_backward(
        item_kind, place, p, grads, ot, linv, qc, qp, v, ktt, position_weight,
        st, ct, *projections, normed, gain1, shift1, sums, block,
    )
    last, near, keep, weight_parts, out_got, feed_total = tie(
        (last, near, keep, weight_parts, out_got, feed_total)
    )
    near = swap(near, "mp", 1)
    parts = first_parts()
    out_sum = sum(x.astype(f32) for x in weight_parts).astype(bf16)
    last = lax.dynamic_update_slice(
        last, out_sum.reshape(parts, cols // parts, width), (0, 0, 0)
    )
    pick = lambda x: lax.dynamic_index_in_dim(x.reshape(2, 2, own, width), 1 - high, 1, False)
    far = (pick(keep) + pick(near).astype(f32)).astype(bf16).reshape(2 * own, width)
    far = swap(far, "mp", 2)
    mixed = (out_keep + out_got.astype(f32)).astype(bf16)
    mixed = [mixed, swap(mixed, "mp", 1)]
    grad = close(place, keep, near, far, tokens_own, res, gain1)
    last_part, last_small, grad = reduce_dp(last, grad)
    tokens_grad = gather_mp(grad)
    last_total = spread_dp(last_part).astype(f32)
    mixed, tokens_grad = collect(place, mixed, tokens_grad)

    summed = last_small[:5]
    summed = summed + swap(summed, "mp", 1)
    summed = summed + swap(summed, "mp", 2)
    feed_total = feed_total.astype(f32)
    split = width // parts
    begin = cols // parts
    inner_grad = feed_total[:, :split].reshape(width, share)
    outer_grad = feed_total[:, split:].reshape(share, width)
    whole_grad = last_total[:, begin:].reshape(width, width)

    return (
        mixed,
        tokens_grad,
        summed[0],
        summed[1],
        whole_grad[:, :cols],
        whole_grad[:, cols : 2 * cols],
        whole_grad[:, 2 * cols : 3 * cols],
        whole_grad[:, 3 * cols :],
        last_small[5, :cols],
        last_small[5, cols : 2 * cols],
        last_total[:, :begin].reshape(cols, width),
        summed[2],
        summed[3],
        inner_grad,
        feed_small[0],
        outer_grad,
        summed[4],
    )


def solution(mesh):
    return jax.shard_map(
        shards,
        mesh=mesh,
        in_specs=(
            P("dp", None), P("dp"), P(), P(), P(None, "mp"), P(None, "mp"), P(None, "mp"),
            P(None, "mp"), P("mp"), P("mp"), P("mp", None), P(), P(), P(None, "mp"), P("mp"),
            P("mp", None), P(), P("dp", None),
        ),
        out_specs=(
            P("dp", None), P("dp", None), P(), P(), P(None, "mp"), P(None, "mp"), P(None, "mp"),
            P(None, "mp"), P("mp"), P("mp"), P("mp", None), P(), P(), P(None, "mp"), P("mp"),
            P("mp", None), P(),
        ),
        check_vma=False,
    )
```

time: 1770 us -> 201 us (0.11)
  local copies, waits for them, and re-layouts: 977 us -> 14.8 us
  waiting for transfers between devices: 329 us -> 54.4 us
  matrix products: 261 us -> 0 us
  Pallas kernels: 0 us -> 84.9 us
  loops' own time: 65.1 us -> 0 us
  other arithmetic: 72.1 us -> 9.7 us
  blocking collectives: 39.4 us -> 0 us
  starting transfers between devices: 0.36 us -> 33.9 us
    while x48 -> x0, local copies, waits for them, and re-layouts: 406 us -> none
    reshape x26 -> x0, local copies, waits for them, and re-layouts: 345 us -> none  [the longest x8 134 us: shear(): return taken.reshape(head_count, row_block, span - 1)[:, :, :length]]
    dot_general x58 -> x0, matrix products: 220 us -> none  [the longest x8 54.6 us: scores(): jnp.einsum('hqd,hcd->hqc', position_rows, relative_heads, preferred_eleme...]
    reduce_scatter x4 -> x0, waiting for transfers between devices: 129 us -> none  [join_heads(): lax.psum_scatter(jnp.dot(acts, weight_rows, preferred_element_type=jnp.fl...]
    slice x9, local copies, waits for them, and re-layouts: 112 us -> 4.66 us  [the longest x1 1.6 us: shards(): outer_grad = feed_total[:, split:].reshape(share, width)]
    all_gather x4 -> x0, waiting for transfers between devices: 103 us -> none  [join_heads(): return lax.all_gather(summed, 'mp', axis=0, tiled=True)]
    psum x1 -> x0, waiting for transfers between devices: 96.7 us -> none  [shards(): lax.psum((first_gain_grad, first_shift_grad, query_grad, key_grad, value_...]
    pallas_call x0 -> x6, Pallas kernels: none -> 84.9 us  [the longest x1 28.6 us: attention_backward(): pl.pallas_call(functools.partial(backward_body, count, block, length // 2...]
  transfers between devices with their start and end apart: 9 -> 30, of which waited for: 8 -> 10; matrix products, arithmetic and copies ran while one was open for 46% -> 8% of each run, Pallas kernels for 0% -> 34%
where the time goes in v1:
time: 201 us; the launch traced here: 199 us
  Pallas kernels  84.9 us (42%)
  waiting for transfers between devices  54.4 us (27%)
  starting transfers between devices  33.9 us (17%)
  local copies, waits for them, and re-layouts  14.8 us (7%)
  other arithmetic  9.7 us (5%)
    ppermute x26, waiting for transfers between devices, swap(): return lax.ppermute(value, axis, [(i, i ^ mask) for i in range(size)])  34.3 us
    pallas_call x1, Pallas kernels, attention_backward(): pl.pallas_call(functools.partial(backward_body, count, block, length // 2...  28.6 us
    pallas_call x1, Pallas kernels, attention_forward(): pl.pallas_call(functools.partial(forward_body, block, length // 2), grid=...  23.9 us
    all_to_all x4, waiting for transfers between devices, exchange(): lax.all_to_all(value, 'dp', split_axis=0, concat_axis=0, tiled=True, axis...  20.1 us
    pallas_call x1, Pallas kernels, feed(): pl.pallas_call(feed_body, grid_spec=pltpu.PrefetchScalarGridSpec(num_scal...  17.9 us
    all_to_all x4, starting transfers between devices, exchange(): lax.all_to_all(value, 'dp', split_axis=0, concat_axis=0, tiled=True, axis...  17.2 us
    ppermute x26, starting transfers between devices, swap(): return lax.ppermute(value, axis, [(i, i ^ mask) for i in range(size)])  16.6 us
    unnamed x46, local copies, waits for them, and re-layouts  5.87 us
  transfers between devices with their start and end apart: 30, of which 10 were waited for; matrix products, arithmetic and copies ran while one was open for 8% of the time, Pallas kernels for 34%

profile of v1, /device:TPU:0, one launch (start us, length us, event | category | flops | bytes accessed | tf_op | source)
XLA Modules:
  0.0 199.3 jit_solution(1648303899539370651)
XLA Ops:
  1.2 2.6 %collective-permute-start.4 = (bf16[128,512]{1,0:T(8,128)(2,1)}, bf16[128,512]{1,0:T(8,128)(2,1)S(1)}, u32[]{:S(2)}, u32[]{:S(2)}) collective-permute-start(bf16[128,512]{1,0:T(8,128)(2,1)} %w0.3), channel_id=1, source_target_pairs={{0,2},{1,3},{2,0},{3,1},{4,6},{5,7},{6,4},{7,5},{8,10},{9,11},{10,... | collective-permute-start | bytes 393224 | tf_op jit(solution)/shard_map/ppermute | solution.py:675
  4.3 0.6 pad_add_fusion.place
  5.9 23.9 %attention_forward.1 = (bf16[1024,512]{1,0:T(8,128)(2,1)}, bf16[1024,512]{1,0:T(8,128)(2,1)}, bf16[2048,512]{1,0:T(8,128)(2,1)}, bf16[2048,128]{1,0:T(8,128)(2,1...) custom-call(s32[1]{0:T(128)S(6)} %copy.48.kind, ...), custom_call_target="tpu_custom_call" | custom-call | flops 27499999232 | bytes 1024 | tf_op jit(solution)/shard_map/attention_forward/pallas_call | solution.py:193
  29.8 1.1 constant_dynamic-slice_fusion
  31.3 1.7 collective-permute-start.2
  33.1 6.5 %collective-permute-done.2.a3 = bf16[1024,128]{1,0:T(8,128)(2,1)S(1)} collective-permute-done((bf16[1024,128]{1,0:T(8,128)(2,1)S(1)}, bf16[1024,128]{1,0:T(8,128)(2,1)S(1)}, u32[]{:S(2)}, u32[]{:S(2)}) %collective-permute-start.2) | collective-permute-done | bytes 262176 | tf_op jit(solution)/shard_map/ppermute | solution.py:675
  39.6 5.9 %collective-permute-done.1.a2 = bf16[1024,128]{1,0:T(8,128)(2,1)S(1)} collective-permute-done((bf16[1024,128]{1,0:T(8,128)(2,1)S(1)}, bf16[1024,128]{1,0:T(8,128)(2,1)S(1)}, u32[]{:S(2)}, u32[]{:S(2)}) %collective-permute-start.1) | collective-permute-done | bytes 262176 | tf_op jit(solution)/shard_map/ppermute | solution.py:675
  45.6 0.6 copy-done.15
  46.6 17.9 %feed.1 = (f32[512,512]{1,0:T(8,128)}, bf16[512,512]{1,0:T(8,128)(2,1)}, f32[1024,512]{1,0:T(8,128)}, bf16[1024,512]{1,0:T(8,128)(2,1)}, f32[512,512]{1,0:T(8,12...) custom-call(s32[3]{0:T(128)} %pad_add_fusion.place, bf16[1024,512]{1,0:T(8,128)(2,1)} %get-tuple-element.71.tokens.t0.t1, ...), custom_call_target="tpu_custom_call" | custom-call | flops 14300000256 | bytes 1024 | tf_op jit(solution)/shard_map/feed/pallas_call | solution.py:513
  64.5 1.8 collective-permute-start.9
  66.3 1.3 collective-permute-done.13
  67.6 2.6 %add_convert_fusion = bf16[8,144,512]{2,1,0:T(8,128)(2,1)} fusion(bf16[8,144,512]{2,1,0:T(8,128)(2,1)S(1)} %collective-permute-done.13, bf16[8,144,512]{2,1,0:T(8,128)(2,1)} %get-tuple-element.88), kind=kLoop, calls=%fused_computation.1 | loop fusion | flops 2359296 | bytes 3538944 | tf_op jit(solution)/shard_map/convert_element_type | solution.py:796
  70.2 4.0 %all-to-all-start = ((bf16[8,144,512]{2,1,0:T(8,128)(2,1)}), bf16[8,144,512]{2,1,0:T(8,128)(2,1)S(1)}, u32[]{:S(2)}, u32[]{:S(2)}) async-start(bf16[8,144,512]{2,1,0:T(8,128)(2,1)} %add_convert_fusion), calls=%async_computation | async-start | bytes 2359296 | tf_op jit(solution)/shard_map/all_to_all | solution.py:709
  74.2 4.9 %collective-permute-done.9.got = bf16[512,512]{1,0:T(8,128)(2,1)S(1)} collective-permute-done((bf16[512,512]{1,0:T(8,128)(2,1)}, bf16[512,512]{1,0:T(8,128)(2,1)S(1)}, u32[]{:S(2)}, u32[]{:S(2)}) %collective-permute-start.9) | collective-permute-done | bytes 524320 | tf_op jit(solution)/shard_map/ppermute | solution.py:675
  79.1 0.8 copy-done.12
  79.9 5.8 %turn.1 = (f32[512,512]{1,0:T(8,128)}, f32[3,512]{1,0:T(4,128)}, bf16[512,128]{1,0:T(8,128)(2,1)}, bf16[512,128]{1,0:T(8,128)(2,1)}, bf16[512,128]{1,0:T(8,128)(...) custom-call(s32[3]{0:T(128)} %pad_add_fusion.place, ...), custom_call_target="tpu_custom_call" | custom-call | flops 65999998976 | bytes 1024 | tf_op jit(solution)/shard_map/turn/pallas_call | solution.py:585
  85.7 1.8 collective-permute-start.11
  87.6 15.5 %all-to-all-done = bf16[8,144,512]{2,1,0:T(8,128)(2,1)S(1)} async-done(((bf16[8,144,512]{2,1,0:T(8,128)(2,1)}), bf16[8,144,512]{2,1,0:T(8,128)(2,1)S(1)}, u32[]{:S(2)}, u32[]{:S(2)}) %all-to-all-start) | async-done | bytes 1179680 | tf_op jit(solution)/shard_map/all_to_all | solution.py:709
  103.3 1.1 broadcast_in_dim.45
  104.5 3.7 %all-to-all-start.1 = ((bf16[8,128,512]{2,1,0:T(8,128)(2,1)}), bf16[8,128,512]{2,1,0:T(8,128)(2,1)S(1)}, u32[]{:S(2)}, u32[]{:S(2)}) async-start(bf16[8,128,512]{2,1,0:T(8,128)(2,1)} %broadcast_in_dim.45), calls=%async_computation.1 | async-start | bytes 2097152 | tf_op jit(solution)/shard_map/all_to_all | solution.py:709
  108.2 1.6 collective-permute-start.17
  110.3 1.4 collective-permute-start.16
  111.6 28.6 %attention_backward.1 = (bf16[8,96,512]{2,1,0:T(8,128)(2,1)}, bf16[1024,512]{1,0:T(8,128)(2,1)}, f32[1024,512]{1,0:T(8,128)}) custom-call(s32[1]{0:T(128)S(6)} %copy.48.kind, s32[3]{0:T(128)} %pad_add_fusion.place, bf16[2048,4096]{1,0:T(8,128)(2,1)} %get-tuple-element.75.p, bf16[512,128]{1,0:T(8,128)(2,1)} %get-tuple-element.90.d0, ...), custom_call_target="tpu_custom_call" | custom-call | flops 109999996928 | bytes 1024 | tf_op jit(solution)/shard_map/attention_backward/pallas_call | solution.py:382
  140.3 0.6 copy-done.4
  141.0 0.7 copy-done.6
  142.0 1.2 add_convert_fusion.2
  143.1 0.7 constant_dynamic-update-slice_fusion
  143.8 4.2 %all-to-all-start.2 = ((bf16[8,96,512]{2,1,0:T(8,128)(2,1)}), bf16[8,96,512]{2,1,0:T(8,128)(2,1)}, u32[]{:S(2)}, u32[]{:S(2)}) async-start(bf16[8,96,512]{2,1,0:T(8,128)(2,1)} %constant_dynamic-update-slice_fusion), calls=%async_computation.2 | async-start | bytes 1572864 | tf_op jit(solution)/shard_map/all_to_all | solution.py:709
  148.0 1.2 fusion
  149.8 0.6 slice.100
  150.4 13.0 %collective-permute-done.20.got = bf16[512,512]{1,0:T(8,128)(2,1)S(1)} collective-permute-done((bf16[512,512]{1,0:T(8,128)(2,1)S(1)}, bf16[512,512]{1,0:T(8,128)(2,1)S(1)}, u32[]{:S(2)}, u32[]{:S(2)}) %collective-permute-start.20) | collective-permute-done | bytes 524320 | tf_op jit(solution)/shard_map/ppermute | solution.py:675
  163.4 0.8 copy-done.3
  164.2 4.4 %close.1.g0 = bf16[512,512]{1,0:T(8,128)(2,1)} custom-call(s32[3]{0:T(128)} %pad_add_fusion.place, f32[1024,512]{1,0:T(8,128)} %get-tuple-element.117.keep0.keep1, f32[1024,512]{1,0:T(8,128)} %get-tuple-element.117.keep0.keep1, bf16[1024,512]{1,0:T(8,128)(2,1)} %collective-permute-done.19.near0.near1, bf16[1024,512]{1,0:T(8,128)(2,1)} %collective-permute-done.19.near0.near1, ...), custom_call_target="tpu_custom_call" | custom-call | flops 2200000000 | bytes 1024 | tf_op jit(solution)/shard_map/close/pallas_call | solution.py:627
  169.3 2.6 %add_convert_fusion.1.m0 = bf16[1024,512]{1,0:T(8,128)(2,1)} fusion(f32[1024,512]{1,0:T(8,128)S(1)} %copy-done.1, bf16[1024,512]{1,0:T(8,128)(2,1)} %collective-permute-done.17), kind=kLoop, calls=%fused_computation.2 | loop fusion | flops 1572864 | bytes 4194304 | tf_op jit(solution)/shard_map/convert_element_type | solution.py:827
  171.9 1.3 convert_reduce_fusion.1
  173.8 0.9 broadcast_in_dim.46
  174.7 5.3 %all-to-all-start.3 = ((bf16[8,80,512]{2,1,0:T(8,128)(2,1)}), bf16[8,80,512]{2,1,0:T(8,128)(2,1)S(1)}, u32[]{:S(2)}, u32[]{:S(2)}) async-start(bf16[8,80,512]{2,1,0:T(8,128)(2,1)} %broadcast_in_dim.46), calls=%async_computation.3 | async-start | bytes 1310720 | tf_op jit(solution)/shard_map/all_to_all | solution.py:709
  180.0 1.6 fusion.1
  181.6 0.8 collective-permute-done.22.g2
  182.4 1.3 collective-permute-start.25
  184.2 2.0 collective-permute-done.25
  186.2 0.6 fusion.3
  186.8 1.0 copy-done.7
  187.9 0.8 copy-done.11
  188.8 4.4 %collect.1 = (bf16[2048,512]{1,0:T(8,128)(2,1)}, bf16[2048,512]{1,0:T(8,128)(2,1)}) custom-call(s32[3]{0:T(128)} %pad_add_fusion.place, bf16[1024,512]{1,0:T(8,128)(2,1)} %add_convert_fusion.1.m0, bf16[1024,512]{1,0:T(8,128)(2,1)} %copy-done.7, bf16[512,512]{1,0:T(8,128)(2,1)} %close.1.g0, bf16[512,512]{1,0:T(8,128)(2,1)} %copy-done.10, ...), custom_call_target="tpu_custom_call" | custom-call | flops 3300000000 | bytes 1024 | tf_op jit(solution)/shard_map/collect/pallas_call | solution.py:662
  193.2 4.3 %all-to-all-done.3 = bf16[8,80,512]{2,1,0:T(8,128)(2,1)S(1)} async-done(((bf16[8,80,512]{2,1,0:T(8,128)(2,1)}), bf16[8,80,512]{2,1,0:T(8,128)(2,1)S(1)}, u32[]{:S(2)}, u32[]{:S(2)}) %all-to-all-start.3) | async-done | bytes 655392 | tf_op jit(solution)/shard_map/all_to_all | solution.py:709
  197.6 1.0 fusion.2
  198.6 0.7 slice.96
  (87 shorter events, 6.3 us)
Async XLA Ops:
  0.7 30.2 %collective-permute-start.3 = (bf16[128,512]{1,0:T(8,128)(2,1)}, bf16[128,512]{1,0:T(8,128)(2,1)S(1)}, u32[]{:S(2)}, u32[]{:S(2)}) collective-permute-start(bf16[128,512]{1,0:T(8,128)(2,1)} %w0.3), channel_id=1, source_target_pairs={{0,1},{1,0},{2,3},{3,2},{4,5},{5,4},{6,7},{7,6},{8,9},{9,8},{10,11... | collective-permute-start | bytes 393224 | tf_op jit(solution)/shard_map/ppermute | solution.py:675
  1.2 30.1 %collective-permute-start.4 = (bf16[128,512]{1,0:T(8,128)(2,1)}, bf16[128,512]{1,0:T(8,128)(2,1)S(1)}, u32[]{:S(2)}, u32[]{:S(2)}) collective-permute-start(bf16[128,512]{1,0:T(8,128)(2,1)} %w0.3), channel_id=1, source_target_pairs={{0,2},{1,3},{2,0},{3,1},{4,6},{5,7},{6,4},{7,5},{8,10},{9,11},{10,... | collective-permute-start | bytes 393224 | tf_op jit(solution)/shard_map/ppermute | solution.py:675
  3.8 29.2 %collective-permute-start.5 = (bf16[128,512]{1,0:T(8,128)(2,1)}, bf16[128,512]{1,0:T(8,128)(2,1)S(1)}, u32[]{:S(2)}, u32[]{:S(2)}) collective-permute-start(bf16[128,512]{1,0:T(8,128)(2,1)} %w0.3), channel_id=1, source_target_pairs={{0,3},{1,2},{2,1},{3,0},{4,7},{5,6},{6,5},{7,4},{8,11},{9,10},{10,... | collective-permute-start | bytes 393224 | tf_op jit(solution)/shard_map/ppermute | solution.py:675
  3.8 1.8 collective-permute-start.8
  4.0 41.5 %collective-permute-start.6 = (bf16[512,512]{1,0:T(8,128)(2,1)}, bf16[512,512]{1,0:T(8,128)(2,1)S(1)}, u32[]{:S(2)}, u32[]{:S(2)}) collective-permute-start(bf16[512,512]{1,0:T(8,128)(2,1)} %i0.1), channel_id=1, source_target_pairs={{0,1},{1,0},{2,3},{3,2},{4,5},{5,4},{6,7},{7,6},{8,9},{9,8},{10,11... | collective-permute-start | bytes 1572872 | tf_op jit(solution)/shard_map/ppermute | solution.py:675
  5.7 24.1 %copy-start.22 = (f32[1,512]{1,0:T(1,128)}, f32[1,512]{1,0:T(1,128)S(1)}, u32[]{:S(2)}) copy-start(f32[1,512]{1,0:T(1,128)S(1)} %collective-permute-done.8.b1) | copy-start | bytes 6148
  5.7 39.9 %collective-permute-start.7 = (bf16[512,512]{1,0:T(8,128)(2,1)}, bf16[512,512]{1,0:T(8,128)(2,1)S(1)}, u32[]{:S(2)}, u32[]{:S(2)}) collective-permute-start(bf16[512,512]{1,0:T(8,128)(2,1)} %u0.1), channel_id=1, source_target_pairs={{0,1},{1,0},{2,3},{3,2},{4,5},{5,4},{6,7},{7,6},{8,9},{9,8},{10,11... | collective-permute-start | bytes 1572872 | tf_op jit(solution)/shard_map/ppermute | solution.py:675
  30.8 14.7 %copy-start.16 = (bf16[128,512]{1,0:T(8,128)(2,1)}, bf16[128,512]{1,0:T(8,128)(2,1)S(1)}, u32[]{:S(2)}) copy-start(bf16[128,512]{1,0:T(8,128)(2,1)S(1)} %collective-permute-done.3.w1) | copy-start | bytes 393220
  30.9 2.3 %collective-permute-start = (bf16[1024,128]{1,0:T(8,128)(2,1)S(1)}, bf16[1024,128]{1,0:T(8,128)(2,1)S(1)}, u32[]{:S(2)}, u32[]{:S(2)}) collective-permute-start(bf16[1024,128]{1,0:T(8,128)(2,1)S(1)} %bitcast.52), channel_id=1, source_target_pairs={{0,1},{1,0},{2,3},{3,2},{4,5},{5,4},{6,7},{7,6},{8,9},{9,8},{10,11... | collective-permute-start | bytes 786440 | tf_op jit(solution)/shard_map/ppermute | solution.py:675
  31.3 14.3 %copy-start.17 = (bf16[128,512]{1,0:T(8,128)(2,1)}, bf16[128,512]{1,0:T(8,128)(2,1)S(1)}, u32[]{:S(2)}) copy-start(bf16[128,512]{1,0:T(8,128)(2,1)S(1)} %collective-permute-done.4.w2) | copy-start | bytes 393220
  31.3 8.3 %collective-permute-start.2 = (bf16[1024,128]{1,0:T(8,128)(2,1)S(1)}, bf16[1024,128]{1,0:T(8,128)(2,1)S(1)}, u32[]{:S(2)}, u32[]{:S(2)}) collective-permute-start(bf16[1024,128]{1,0:T(8,128)(2,1)S(1)} %bitcast.53), channel_id=1, source_target_pairs={{0,3},{1,2},{2,1},{3,0},{4,7},{5,6},{6,5},{7,4},{8,11},{9,10},{10,... | collective-permute-start | bytes 786440 | tf_op jit(solution)/shard_map/ppermute | solution.py:675
  33.0 12.6 %copy-start.18 = (bf16[128,512]{1,0:T(8,128)(2,1)}, bf16[128,512]{1,0:T(8,128)(2,1)S(1)}, u32[]{:S(2)}) copy-start(bf16[128,512]{1,0:T(8,128)(2,1)S(1)} %collective-permute-done.5.w3) | copy-start | bytes 393220
  33.0 12.5 %collective-permute-start.1 = (bf16[1024,128]{1,0:T(8,128)(2,1)S(1)}, bf16[1024,128]{1,0:T(8,128)(2,1)S(1)}, u32[]{:S(2)}, u32[]{:S(2)}) collective-permute-start(bf16[1024,128]{1,0:T(8,128)(2,1)S(1)} %bitcast.51), channel_id=1, source_target_pairs={{0,2},{1,3},{2,0},{3,1},{4,6},{5,7},{6,4},{7,5},{8,10},{9,11},{10,... | collective-permute-start | bytes 786440 | tf_op jit(solution)/shard_map/ppermute | solution.py:675
  33.1 12.5 %copy-start.13 = (bf16[1024,128]{1,0:T(8,128)(2,1)}, bf16[1024,128]{1,0:T(8,128)(2,1)S(1)}, u32[]{:S(2)}) copy-start(bf16[1024,128]{1,0:T(8,128)(2,1)S(1)} %collective-permute-done.a1) | copy-start | bytes 786436
  39.6 6.0 %copy-start.14 = (bf16[1024,128]{1,0:T(8,128)(2,1)}, bf16[1024,128]{1,0:T(8,128)(2,1)S(1)}, u32[]{:S(2)}) copy-start(bf16[1024,128]{1,0:T(8,128)(2,1)S(1)} %collective-permute-done.2.a3) | copy-start | bytes 786436
  45.5 0.9 copy-start.8
  45.5 1.0 copy-start.9
  64.5 3.1 %collective-permute-start.13 = (bf16[8,144,512]{2,1,0:T(8,128)(2,1)}, bf16[8,144,512]{2,1,0:T(8,128)(2,1)S(1)}, u32[]{:S(2)}, u32[]{:S(2)}) collective-permute-start(bf16[8,144,512]{2,1,0:T(8,128)(2,1)} %get-tuple-element.89), channel_id=1, source_target_pairs={{0,1},{1,0},{2,3},{3,2},{4,5},{5,4},{6,7},{7,6},{8,9},{9,8},{10,11... | collective-permute-start | bytes 3538952 | tf_op jit(solution)/shard_map/ppermute | solution.py:675
  64.5 14.6 %collective-permute-start.9 = (bf16[512,512]{1,0:T(8,128)(2,1)}, bf16[512,512]{1,0:T(8,128)(2,1)S(1)}, u32[]{:S(2)}, u32[]{:S(2)}) collective-permute-start(bf16[512,512]{1,0:T(8,128)(2,1)} %get-tuple-element.77), channel_id=1, source_target_pairs={{0,2},{1,3},{2,0},{3,1},{4,6},{5,7},{6,4},{7,5},{8,10},{9,11},{10,... | collective-permute-start | bytes 1572872 | tf_op jit(solution)/shard_map/ppermute | solution.py:675
  70.2 32.9 %all-to-all-start = ((bf16[8,144,512]{2,1,0:T(8,128)(2,1)}), bf16[8,144,512]{2,1,0:T(8,128)(2,1)S(1)}, u32[]{:S(2)}, u32[]{:S(2)}) async-start(bf16[8,144,512]{2,1,0:T(8,128)(2,1)} %add_convert_fusion), calls=%async_computation | async-start | bytes 2359296 | tf_op jit(solution)/shard_map/all_to_all | solution.py:709
  79.1 0.8 copy-start.12
  85.7 17.6 %collective-permute-start.10 = (bf16[512,128]{1,0:T(8,128)(2,1)}, bf16[512,128]{1,0:T(8,128)(2,1)S(1)}, u32[]{:S(2)}, u32[]{:S(2)}) collective-permute-start(bf16[512,128]{1,0:T(8,128)(2,1)} %get-tuple-element.80), channel_id=1, source_target_pairs={{0,1},{1,0},{2,3},{3,2},{4,5},{5,4},{6,7},{7,6},{8,9},{9,8},{10,11... | collective-permute-start | bytes 393224 | tf_op jit(solution)/shard_map/ppermute | solution.py:675
  85.7 17.6 %collective-permute-start.11 = (bf16[512,128]{1,0:T(8,128)(2,1)}, bf16[512,128]{1,0:T(8,128)(2,1)S(1)}, u32[]{:S(2)}, u32[]{:S(2)}) collective-permute-start(bf16[512,128]{1,0:T(8,128)(2,1)} %get-tuple-element.81), channel_id=1, source_target_pairs={{0,2},{1,3},{2,0},{3,1},{4,6},{5,7},{6,4},{7,5},{8,10},{9,11},{10,... | collective-permute-start | bytes 393224 | tf_op jit(solution)/shard_map/ppermute | solution.py:675
  87.5 15.8 %collective-permute-start.12 = (bf16[512,128]{1,0:T(8,128)(2,1)}, bf16[512,128]{1,0:T(8,128)(2,1)S(1)}, u32[]{:S(2)}, u32[]{:S(2)}) collective-permute-start(bf16[512,128]{1,0:T(8,128)(2,1)} %get-tuple-element.82), channel_id=1, source_target_pairs={{0,3},{1,2},{2,1},{3,0},{4,7},{5,6},{6,5},{7,4},{8,11},{9,10},{10,... | collective-permute-start | bytes 393224 | tf_op jit(solution)/shard_map/ppermute | solution.py:675
  103.3 8.4 %copy-start.19 = (bf16[512,128]{1,0:T(8,128)(2,1)}, bf16[512,128]{1,0:T(8,128)(2,1)S(1)}, u32[]{:S(2)}) copy-start(bf16[512,128]{1,0:T(8,128)(2,1)S(1)} %collective-permute-done.10.d1) | copy-start | bytes 393220
  103.3 8.3 %copy-start.20 = (bf16[512,128]{1,0:T(8,128)(2,1)}, bf16[512,128]{1,0:T(8,128)(2,1)S(1)}, u32[]{:S(2)}) copy-start(bf16[512,128]{1,0:T(8,128)(2,1)S(1)} %collective-permute-done.11.d2) | copy-start | bytes 393220
  103.3 8.3 %copy-start.21 = (bf16[512,128]{1,0:T(8,128)(2,1)}, bf16[512,128]{1,0:T(8,128)(2,1)S(1)}, u32[]{:S(2)}) copy-start(bf16[512,128]{1,0:T(8,128)(2,1)S(1)} %collective-permute-done.12.d3) | copy-start | bytes 393220
  104.5 37.2 %all-to-all-start.1 = ((bf16[8,128,512]{2,1,0:T(8,128)(2,1)}), bf16[8,128,512]{2,1,0:T(8,128)(2,1)S(1)}, u32[]{:S(2)}, u32[]{:S(2)}) async-start(bf16[8,128,512]{2,1,0:T(8,128)(2,1)} %broadcast_in_dim.45), calls=%async_computation.1 | async-start | bytes 2097152 | tf_op jit(solution)/shard_map/all_to_all | solution.py:709
  108.2 33.5 %collective-permute-start.17 = (bf16[1024,512]{1,0:T(8,128)(2,1)}, bf16[1024,512]{1,0:T(8,128)(2,1)}, u32[]{:S(2)}, u32[]{:S(2)}) collective-permute-start(bf16[1024,512]{1,0:T(8,128)(2,1)} %get-tuple-element.109), channel_id=1, source_target_pairs={{0,2},{1,3},{2,0},{3,1},{4,6},{5,7},{6,4},{7,5},{8,10},{9,11},{10,... | collective-permute-start | bytes 3145736 | tf_op jit(solution)/shard_map/ppermute | solution.py:675
  109.8 30.5 %collective-permute-start.14 = (bf16[128,512]{1,0:T(8,128)(2,1)}, bf16[128,512]{1,0:T(8,128)(2,1)S(1)}, u32[]{:S(2)}, u32[]{:S(2)}) collective-permute-start(bf16[128,512]{1,0:T(8,128)(2,1)} %get-tuple-element.106), channel_id=1, source_target_pairs={{0,1},{1,0},{2,3},{3,2},{4,5},{5,4},{6,7},{7,6},{8,9},{9,8},{10,11... | collective-permute-start | bytes 393224 | tf_op jit(solution)/shard_map/ppermute | solution.py:675
  109.8 30.5 %collective-permute-start.15 = (bf16[128,512]{1,0:T(8,128)(2,1)}, bf16[128,512]{1,0:T(8,128)(2,1)S(1)}, u32[]{:S(2)}, u32[]{:S(2)}) collective-permute-start(bf16[128,512]{1,0:T(8,128)(2,1)} %get-tuple-element.107), channel_id=1, source_target_pairs={{0,2},{1,3},{2,0},{3,1},{4,6},{5,7},{6,4},{7,5},{8,10},{9,11},{10,... | collective-permute-start | bytes 393224 | tf_op jit(solution)/shard_map/ppermute | solution.py:675
  110.3 30.1 %collective-permute-start.16 = (bf16[128,512]{1,0:T(8,128)(2,1)}, bf16[128,512]{1,0:T(8,128)(2,1)S(1)}, u32[]{:S(2)}, u32[]{:S(2)}) collective-permute-start(bf16[128,512]{1,0:T(8,128)(2,1)} %get-tuple-element.108), channel_id=1, source_target_pairs={{0,3},{1,2},{2,1},{3,0},{4,7},{5,6},{6,5},{7,4},{8,11},{9,10},{10,... | collective-permute-start | bytes 393224 | tf_op jit(solution)/shard_map/ppermute | solution.py:675
  140.3 7.8 %copy-start = (f32[1024,512]{1,0:T(8,128)S(1)}, f32[1024,512]{1,0:T(8,128)}, u32[]{:S(2)}) copy-start(f32[1024,512]{1,0:T(8,128)} %get-tuple-element.117.keep0.keep1) | copy-start | bytes 6291460
  141.7 6.4 %collective-permute-start.19 = (bf16[1024,512]{1,0:T(8,128)(2,1)}, bf16[1024,512]{1,0:T(8,128)(2,1)}, u32[]{:S(2)}, u32[]{:S(2)}) collective-permute-start(bf16[1024,512]{1,0:T(8,128)(2,1)} %get-tuple-element.118), channel_id=1, source_target_pairs={{0,1},{1,0},{2,3},{3,2},{4,5},{5,4},{6,7},{7,6},{8,9},{9,8},{10,11... | collective-permute-start | bytes 3145736 | tf_op jit(solution)/shard_map/ppermute | solution.py:675
  143.8 25.0 %all-to-all-start.2 = ((bf16[8,96,512]{2,1,0:T(8,128)(2,1)}), bf16[8,96,512]{2,1,0:T(8,128)(2,1)}, u32[]{:S(2)}, u32[]{:S(2)}) async-start(bf16[8,96,512]{2,1,0:T(8,128)(2,1)} %constant_dynamic-update-slice_fusion), calls=%async_computation.2 | async-start | bytes 1572864 | tf_op jit(solution)/shard_map/all_to_all | solution.py:709
  149.3 14.1 %collective-permute-start.20 = (bf16[512,512]{1,0:T(8,128)(2,1)S(1)}, bf16[512,512]{1,0:T(8,128)(2,1)S(1)}, u32[]{:S(2)}, u32[]{:S(2)}) collective-permute-start(bf16[512,512]{1,0:T(8,128)(2,1)S(1)} %bitcast.47), channel_id=1, source_target_pairs={{0,2},{1,3},{2,0},{3,1},{4,6},{5,7},{6,4},{7,5},{8,10},{9,11},{10,... | collective-permute-start | bytes 1572872 | tf_op jit(solution)/shard_map/ppermute | solution.py:675
  164.2 5.2 %copy-start.1 = (f32[1024,512]{1,0:T(8,128)S(1)}, f32[1024,512]{1,0:T(8,128)}, u32[]{:S(2)}) copy-start(f32[1024,512]{1,0:T(8,128)} %get-tuple-element.74) | copy-start | bytes 6291460
  168.8 13.5 %collective-permute-start.22 = (bf16[512,512]{1,0:T(8,128)(2,1)}, bf16[512,512]{1,0:T(8,128)(2,1)}, u32[]{:S(2)}, u32[]{:S(2)}) collective-permute-start(bf16[512,512]{1,0:T(8,128)(2,1)} %close.1.g0), channel_id=1, source_target_pairs={{0,2},{1,3},{2,0},{3,1},{4,6},{5,7},{6,4},{7,5},{8,10},{9,11},{10,... | collective-permute-start | bytes 1572872 | tf_op jit(solution)/shard_map/ppermute | solution.py:675
  171.9 14.9 %collective-permute-start.18 = (bf16[1024,512]{1,0:T(8,128)(2,1)}, bf16[1024,512]{1,0:T(8,128)(2,1)S(1)}, u32[]{:S(2)}, u32[]{:S(2)}) collective-permute-start(bf16[1024,512]{1,0:T(8,128)(2,1)} %add_convert_fusion.1.m0), channel_id=1, source_target_pairs={{0,1},{1,0},{2,3},{3,2},{4,5},{5,4},{6,7},{7,6},{8,9},{9,8},{10,11... | collective-permute-start | bytes 3145736 | tf_op jit(solution)/shard_map/ppermute | solution.py:675
  173.2 9.2 %collective-permute-start.24 = (f32[5,512]{1,0:T(8,128)S(1)}, f32[5,512]{1,0:T(8,128)S(1)}, u32[]{:S(2)}, u32[]{:S(2)}) collective-permute-start(f32[5,512]{1,0:T(8,128)S(1)} %slice.85), channel_id=1, source_target_pairs={{0,1},{1,0},{2,3},{3,2},{4,5},{5,4},{6,7},{7,6},{8,9},{9,8},{10,11... | collective-permute-start | bytes 30728 | tf_op jit(solution)/shard_map/ppermute | solution.py:675
  174.7 22.8 %all-to-all-start.3 = ((bf16[8,80,512]{2,1,0:T(8,128)(2,1)}), bf16[8,80,512]{2,1,0:T(8,128)(2,1)S(1)}, u32[]{:S(2)}, u32[]{:S(2)}) async-start(bf16[8,80,512]{2,1,0:T(8,128)(2,1)} %broadcast_in_dim.46), calls=%async_computation.3 | async-start | bytes 1310720 | tf_op jit(solution)/shard_map/all_to_all | solution.py:709
  180.0 1.6 copy-start.2
  181.6 5.2 %collective-permute-start.21 = (bf16[512,512]{1,0:T(8,128)(2,1)S(1)}, bf16[512,512]{1,0:T(8,128)(2,1)S(1)}, u32[]{:S(2)}, u32[]{:S(2)}) collective-permute-start(bf16[512,512]{1,0:T(8,128)(2,1)S(1)} %copy-done.2), channel_id=1, source_target_pairs={{0,1},{1,0},{2,3},{3,2},{4,5},{5,4},{6,7},{7,6},{8,9},{9,8},{10,11... | collective-permute-start | bytes 1572872 | tf_op jit(solution)/shard_map/ppermute | solution.py:675
  182.4 4.5 %collective-permute-start.23 = (bf16[512,512]{1,0:T(8,128)(2,1)}, bf16[512,512]{1,0:T(8,128)(2,1)S(1)}, u32[]{:S(2)}, u32[]{:S(2)}) collective-permute-start(bf16[512,512]{1,0:T(8,128)(2,1)} %collective-permute-done.22.g2), channel_id=1, source_target_pairs={{0,1},{1,0},{2,3},{3,2},{4,5},{5,4},{6,7},{7,6},{8,9},{9,8},{10,11... | collective-permute-start | bytes 1572872 | tf_op jit(solution)/shard_map/ppermute | solution.py:675
  182.4 3.8 %collective-permute-start.25 = (f32[5,512]{1,0:T(8,128)S(1)}, f32[5,512]{1,0:T(8,128)S(1)}, u32[]{:S(2)}, u32[]{:S(2)}) collective-permute-start(f32[5,512]{1,0:T(8,128)S(1)} %slice_add_fusion), channel_id=1, source_target_pairs={{0,2},{1,3},{2,0},{3,1},{4,6},{5,7},{6,4},{7,5},{8,10},{9,11},{10,... | collective-permute-start | bytes 30728 | tf_op jit(solution)/shard_map/ppermute | solution.py:675
  186.8 1.0 copy-start.7
  186.8 1.1 copy-start.10
  187.9 0.8 copy-start.11
  (5 other events, 3.5 us)

commit v2 on v1

--- a/solution.py
+++ b/solution.py
@@ -234,7 +234,7 @@
     count, block, half_rows,
     kind, place, p, d0, d1, d2, d3, ot, linv, qc, qp, v, ktt, wp, st, ct,
     wq, wk, wv, normed, gain, shift, sums,
-    last, near, mine,
+    last, small, near, mine,
     wcat, acc, dk, dv, low, low_t, d_scr, dcat, dstack, qstack, delta, mom, colsum, dwp, cb, pb,
 ):
     step = pl.program_id(0)
@@ -343,9 +343,6 @@
         as_row = lambda values: jnp.broadcast_to(
             jnp.sum(values, axis=1, keepdims=True), (values.shape[0], 128)
         ).T[:1]
-        parts = last.shape[0]
-        share = width // parts
-        extra = cols // parts
         column = jnp.broadcast_to(colsum[...], (8, 3 * cols)).T[:, :1]
         weights = wcat[...].astype(f32).T
         by_gain = jnp.sum(mom[...] * weights, axis=0, keepdims=True)
@@ -354,16 +351,12 @@
         biases = jnp.concatenate(
             [as_row(cb[...]), as_row(pb[...]), jnp.zeros((1, width - 2 * cols), f32)], axis=1
         )
-        tail = jnp.concatenate(
-            [by_gain, by_shift, sums[...], biases, jnp.zeros((10, width), f32)], axis=0
+        small[...] = jnp.concatenate(
+            [by_gain, by_shift, sums[...], biases, jnp.zeros((9, width), f32)], axis=0
         ).astype(bf16)
-        by_table = dwp[...].astype(bf16)
-        for r in range(parts):
-            at = slice(r * share, (r + 1) * share)
-            last[r, :extra] = jnp.zeros((extra, width), bf16)
-            last[r, extra : extra + share, : 3 * cols] = full[at]
-            last[r, extra : extra + share, 3 * cols :] = by_table[at]
-            last[r, extra + share :] = tail
+        last[:cols] = jnp.zeros((cols, width), bf16)
+        last[cols:, : 3 * cols] = full
+        last[cols:, 3 * cols :] = dwp[...].astype(bf16)
 
 
 def attention_backward(
@@ -377,8 +370,7 @@
     col = lambda n, w: pl.BlockSpec((n, w), lambda i: (0, count - 1 - i))
     row = lambda n, w: pl.BlockSpec((n, w), lambda i: (count - 1 - i, 0))
     smem = pl.BlockSpec(memory_space=pltpu.SMEM)
-    parts = first_parts()
-    message = (parts, (width + cols) // parts + 16, width)
+    message = (cols + width, width)
     return pl.pallas_call(
         functools.partial(backward_body, count, block, length // 2),
         grid=(count,),
@@ -391,11 +383,14 @@
             *[whole((width, cols))] * 3, row(block, width),
             whole(gain.shape), whole(shift.shape), whole(sums.shape),
         ],
-        out_specs=[whole(message), row(block // 2, width), row(block // 2, width)],
+        out_specs=[
+            whole(message), whole((16, width)), row(block // 2, width), row(block // 2, width)
+        ],
         out_shape=[
             jax.ShapeDtypeStruct(message, bf16),
+            jax.ShapeDtypeStruct((16, width), bf16),
             jax.ShapeDtypeStruct((length // 2, width), bf16),
-            jax.ShapeDtypeStruct((length // 2, width), f32),
+            jax.ShapeDtypeStruct((length // 2, width), bf16),
         ],
         scratch_shapes=[
             pltpu.VMEM((width, 3 * cols), bf16),
@@ -416,7 +411,7 @@
             pltpu.VMEM((cols, block), f32),
         ],
         compiler_params=params(),
-        cost_estimate=cost(100),
+        cost_estimate=cost(8),
         name="attention_backward",
     )(
         kind, place, p, *grads, ot, linv, qc, qp, v, ktt, wp, st, ct, wq, wk, wv, normed,
@@ -427,75 +422,74 @@
 def feed_body(
     place, tokens, cot, own_att, a1, a2, a3, w0, w1, w2, w3, i0, i1, u0, u1, b0, b1,
     bu, gain, shift,
-    back_keep, back_send, out_keep, out_send, res_own, grad0, grad1,
-    back_scr, res_scr, sum0, sum1,
+    back_keep, back_send, out, res_own, bias, near, keep,
+    hidden_t, act_t, pres, cots,
 ):
     step = pl.program_id(0)
     own, width = res_own.shape
-    cols = a1.shape[1]
-    share = i0.shape[1]
-    c = cot[...]
-    residual = tokens[...].astype(f32)
-    residual = residual + dot(own_att[...].reshape(2 * own, cols), w0[...])
-    for att, wo in ((a1, w1), (a2, w2), (a3, w3)):
-        residual = residual + dot(att[...], wo[...])
-    res_scr[...] = residual
-    normed, _ = norm_parts(residual)
-    hidden = (normed * gain[...] + shift[...]).astype(bf16)
-    hidden_t = hidden.T
-    mixed = None
-    back = None
-    for n, wi, wu, bi, total in ((0, i0, u0, b0, sum0), (1, i1, u1, b1, sum1)):
-        x = dot(hidden, wi[...]) + bi[...]
-        square = x * x
-        t = jnp.tanh(GELU_A * x * (1.0 + GELU_B * square))
-        act = (0.5 * x * (1.0 + t)).astype(bf16)
-        slope = 0.5 * (1.0 + t) + (0.5 * GELU_A) * x * (1.0 - t * t) * (
-            1.0 + (3.0 * GELU_B) * square
-        )
-        out_n = dot(act, wu[...])
-        pre = (dot_nt(c, wu[...]) * slope).astype(bf16)
-        back_n = dot_nt(pre, wi[...])
-        mixed = out_n if mixed is None else mixed + out_n
-        back = back_n if back is None else back + back_n
-        inner = dot(hidden_t, pre)
-        outer = dot(act.T, c)
-        bias = jnp.sum(pre.astype(f32), axis=0, keepdims=True)
-        bias = jnp.broadcast_to(bias, (16, share))
+    steps = cots.shape[0] // own
+
+    @pl.when(step < steps)
+    def rows():
+        c = cot[...]
+        residual = tokens[...].astype(f32)
+        residual = residual + dot(own_att[...].reshape(own_att.shape[-2:]), w0[...])
+        for att, wo in ((a1, w1), (a2, w2), (a3, w3)):
+            residual = residual + dot(att[...], wo[...])
+        normed, _ = norm_parts(residual)
+        hidden = (normed * gain[...] + shift[...]).astype(bf16)
+        here = pl.ds(pl.multiple_of(step * own, own), own)
+        cots[here, :] = c
+        hidden_t[:, here] = hidden.T
+        mixed = 0.5 * (residual + bu[...])
+        back = None
+        sums = []
+        for n, wi, wu, bi in ((0, i0, u0, b0), (1, i1, u1, b1)):
+            x = dot(hidden, wi[...]) + bi[...]
+            square = x * x
+            t = jnp.tanh(GELU_A * x * (1.0 + GELU_B * square))
+            act = (0.5 * x * (1.0 + t)).astype(bf16)
+            slope = 0.5 * (1.0 + t) + (0.5 * GELU_A) * x * (1.0 - t * t) * (
+                1.0 + (3.0 * GELU_B) * square
+            )
+            act_t[n, :, here] = act.T
+            mixed = mixed + dot(act, wu[...])
+            pre = (dot_nt(c, wu[...]) * slope).astype(bf16)
+            pres[n, here, :] = pre
+            sums.append(jnp.sum(pre.astype(f32), axis=0, keepdims=True))
+            back_n = dot_nt(pre, wi[...])
+            back = back_n if back is None else back + back_n
+        out[...] = mixed.astype(bf16)
+        sums = jnp.concatenate(sums, axis=0)
 
         @pl.when(step == 0)
-        def first(total=total, inner=inner, outer=outer, bias=bias):
-            total[:width] = inner
-            total[width : width + share] = outer
-            total[width + share :] = bias
+        def first():
+            bias[...] = sums
 
         @pl.when(step > 0)
-        def later(total=total, inner=inner, outer=outer, bias=bias):
-            total[:width] += inner
-            total[width : width + share] += outer
-            total[width + share :] += bias
-
-    back_scr[...] = back
-    mine = pl.multiple_of(place[2] * own, own)
-    other = pl.multiple_of((1 - place[2]) * own, own)
-    res_own[...] = res_scr[pl.ds(mine, own), :]
-    back_keep[...] = back_scr[pl.ds(mine, own), :]
-    back_send[...] = back_scr[pl.ds(other, own), :].astype(bf16)
-    out_keep[...] = mixed + residual + bu[...]
-    out_send[...] = mixed.astype(bf16)
-
-    @pl.when(step == pl.num_programs(0) - 1)
-    def finish():
-        parts = grad0.shape[0]
-        mid = width // parts
-        end = mid + share // parts
-        for total, grad in ((sum0, grad0), (sum1, grad1)):
-            bias = total[width + share :].astype(bf16)
+        def later():
+            bias[...] += sums
+
+        @pl.when(step % 2 == place[2])
+        def mine():
+            res_own[...] = residual
+            back_keep[...] = back.astype(bf16)
+
+        @pl.when(step % 2 != place[2])
+        def other():
+            back_send[...] = back.astype(bf16)
+
+    for n, ref in ((1, near), (0, keep)):
+
+        @pl.when(step == steps + 1 - n)
+        def grads(n=n, ref=ref):
+            parts, length, _ = ref.shape
+            share = length // 2
+            inner = dot(hidden_t[...], pres[n]).astype(bf16)
+            outer = dot(act_t[n], cots[...]).astype(bf16)
             for r in range(parts):
-                grad[r, :mid] = total[r * mid : (r + 1) * mid].astype(bf16)
-                at = width + r * (end - mid)
-                grad[r, mid:end] = total[at : at + end - mid].astype(bf16)
-                grad[r, end:] = bias
+                ref[r, :share] = inner[r * share : (r + 1) * share]
+                ref[r, share:] = outer[r * share : (r + 1) * share]
 
 
 def feed(place, tokens, cot, own_att, atts, wos, wis, wus, bis, bu, gain, shift):
@@ -504,36 +498,42 @@
     share = wis[0].shape[1]
     own = rows // 4
     spec = lambda s: pl.BlockSpec(s, lambda i, place: (0,) * len(s))
-    step = lambda n, w: pl.BlockSpec((n, w), lambda i, place: (i, 0))
+    at = lambda i: jnp.minimum(i, 3)
+    step = lambda w: pl.BlockSpec((own, w), lambda i, place: (at(i), 0))
+    half = pl.BlockSpec((own, width), lambda i, place: (at(i) // 2, 0))
     parts = first_parts()
-    grad_shape = (parts, (width + share) // parts + 16, width)
-    att = pl.BlockSpec((1, 2, 1, own, cols), lambda i, place: (i, 0, place[1], 0, 0))
+    grad_shape = (parts, (width + share) // parts, width)
+    att = pl.BlockSpec((1, 1, own, cols), lambda i, place: (at(i), place[1], 0, 0))
     others = (*wos, *wis, *wus, *bis, bu, gain, shift)
     shape = jax.ShapeDtypeStruct
     return pl.pallas_call(
         feed_body,
         grid_spec=pltpu.PrefetchScalarGridSpec(
             num_scalar_prefetch=1,
-            grid=(2,),
-            in_specs=[step(2 * own, width), step(2 * own, width), att]
-            + [step(2 * own, cols)] * 3
+            grid=(6,),
+            in_specs=[step(width), step(width), att]
+            + [step(cols)] * 3
             + [spec(o.shape) for o in others],
             out_specs=[
-                step(own, width), step(own, width), step(2 * own, width), step(2 * own, width),
-                step(own, width), spec(grad_shape), spec(grad_shape),
+                half, half, step(width), half, spec((2, share)), spec(grad_shape),
+                spec(grad_shape),
             ],
-            scratch_shapes=[pltpu.VMEM((2 * own, width), f32)] * 2
-            + [pltpu.VMEM((width + share + 16, width), f32)] * 2,
+            scratch_shapes=[
+                pltpu.VMEM((width, rows), bf16),
+                pltpu.VMEM((2, share, rows), bf16),
+                pltpu.VMEM((2, rows, share), bf16),
+                pltpu.VMEM((rows, width), bf16),
+            ],
         ),
         out_shape=[
-            shape((2 * own, width), f32), shape((2 * own, width), bf16),
-            shape((rows, width), f32), shape((rows, width), bf16),
-            shape((2 * own, width), f32), shape(grad_shape, bf16), shape(grad_shape, bf16),
+            shape((2 * own, width), bf16), shape((2 * own, width), bf16),
+            shape((rows, width), bf16), shape((2 * own, width), f32), shape((2, share), f32),
+            shape(grad_shape, bf16), shape(grad_shape, bf16),
         ],
         compiler_params=params(),
         cost_estimate=cost(13),
         name="feed",
-    )(place, tokens, cot, own_att.reshape(2, 2, 2, own, cols), *atts, *others)
+    )(place, tokens, cot, own_att.reshape(4, 2, own, cols), *atts, *others)
 
 
 def turn_body(
@@ -541,7 +541,7 @@
     res_out, sums_out, g0, g1, g2, g3, o0, o1, o2, o3, total,
 ):
     step = pl.program_id(0)
-    back = keep[...] + got[...].astype(f32)
+    back = keep[...].astype(f32) + got[...].astype(f32)
     c = cot[...].astype(f32)
     normed, scale = norm_parts(residual[...])
     fold = lambda values: jnp.sum(values, axis=0, keepdims=True)
@@ -553,8 +553,8 @@
         - normed * jnp.mean(e * normed, axis=-1, keepdims=True)
     )
     res = c + scale * inner
-    res_out[...] = res
     branch = res.astype(bf16)
+    res_out[...] = branch
     for wo, out in ((w0, g0), (w1, g1), (w2, g2), (w3, g3)):
         out[...] = dot_nt(branch, wo[...]).astype(bf16)
     products = [dot(att[...].T, branch) for att in (a0, a1, a2, a3)]
@@ -579,7 +579,7 @@
     spec = lambda s: pl.BlockSpec(s, lambda i, place: (0,) * len(s))
     step = lambda w: pl.BlockSpec((own, w), lambda i, place: (i, 0))
     half = lambda w: pl.BlockSpec((own, w), lambda i, place: (2 * i + place[2], 0))
-    shapes = [((rows, width), f32), ((3, width), f32)]
+    shapes = [((rows, width), bf16), ((3, width), f32)]
     shapes = shapes + [((rows, cols), bf16)] * 4
     shapes = shapes + [((cols, width), t) for t in (f32, bf16, bf16, bf16)]
     return pl.pallas_call(
@@ -608,7 +608,7 @@
     own = t0.shape[0]
     for part, keep, near, tokens in ((0, keep0, near0, t0), (1, keep1, near1, t1)):
         rows = slice(part * own, (part + 1) * own)
-        total = keep[...] + near[...].astype(f32) + got[rows].astype(f32)
+        total = keep[...].astype(f32) + near[...].astype(f32) + got[rows].astype(f32)
         normed, scale = norm_parts(tokens[...].astype(f32))
         e = total * gain[...]
         inner = (
@@ -616,7 +616,7 @@
             - jnp.mean(e, axis=-1, keepdims=True)
             - normed * jnp.mean(e * normed, axis=-1, keepdims=True)
         )
-        out[rows] = (res[rows] + scale * inner).astype(bf16)
+        out[rows] = (res[rows].astype(f32) + scale * inner).astype(bf16)
 
 
 def close(place, keep, near, got, tokens, res, gain):
@@ -642,29 +642,40 @@
     )(place, keep, keep, near, near, got, tokens, tokens, res, gain)
 
 
-def collect_body(place, m0, m1, g0, g1, g2, g3, mixed, grad):
+def collect_body(place, m0, m1, g0, g1, g2, g3, mixed, grad, sems):
     own = g0.shape[0] // 2
-    core, high = place[1], place[2]
+    core = place[1]
+    copies = []
     for part in range(2):
         for flip, ref in ((0, m0), (1, m1)):
             for at_high in range(2):
                 put = pl.multiple_of((4 * part + 2 * at_high + (core ^ flip)) * own, own)
-                mixed[pl.ds(put, own), :] = ref[(2 * part + at_high) * own :][:own]
+                copies.append((ref.at[pl.ds((2 * part + at_high) * own, own)], mixed, put))
         for n, ref in enumerate((g0, g1, g2, g3)):
             put = pl.multiple_of((4 * part + (place[0] ^ n)) * own, own)
-            grad[pl.ds(put, own), :] = ref[part * own : (part + 1) * own]
+            copies.append((ref.at[pl.ds(part * own, own)], grad, put))
+    copies = [
+        pltpu.make_async_copy(source, target.at[pl.ds(put, own)], sems.at[at])
+        for at, (source, target, put) in enumerate(copies)
+    ]
+    for copy in copies:
+        copy.start()
+    for copy in copies:
+        copy.wait()
 
 
 def collect(place, mixed, grads):
     rows, width = grads[0].shape
-    vmem = pl.BlockSpec(memory_space=pltpu.VMEM)
+    hbm = pl.BlockSpec(memory_space=pl.ANY)
     shape = jax.ShapeDtypeStruct((4 * rows, width), bf16)
     return pl.pallas_call(
         collect_body,
-        in_specs=[pl.BlockSpec(memory_space=pltpu.SMEM)] + [vmem] * 6,
-        out_specs=[vmem] * 2,
+        in_specs=[pl.BlockSpec(memory_space=pltpu.SMEM)]
+        + [pl.BlockSpec(memory_space=pltpu.VMEM)] * 6,
+        out_specs=[hbm] * 2,
         out_shape=[shape] * 2,
-        compiler_params=pltpu.CompilerParams(vmem_limit_bytes=60 * 2**20),
+        scratch_shapes=[pltpu.SemaphoreType.DMA((16,))],
+        compiler_params=pltpu.CompilerParams(vmem_limit_bytes=16 * 2**20),
         cost_estimate=cost(3),
         name="collect",
     )(place, *mixed, *grads)
@@ -677,11 +688,6 @@
 
 def block_of(value, index, count):
     return lax.dynamic_slice_in_dim(value, index * count, count, 0)
-
-
-def gather_mp(value):
-    beyond = swap(value, "mp", 2)
-    return [value, swap(value, "mp", 1), beyond, swap(beyond, "mp", 1)]
 
 
 def levels(size):
@@ -727,26 +733,62 @@
     return 1 << levels(lax.axis_size("dp"))[0][1]
 
 
-def reduce_dp(parts, before=None):
-    for at, (shift, wide) in enumerate(levels(lax.axis_size("dp"))):
-        if at:
-            count = 1 << wide
-            small = jnp.broadcast_to(total[None, -16:], (count, 16, total.shape[1]))
-            rows = total[:-16].reshape(count, -1, total.shape[1])
-            parts = jnp.concatenate([rows, small], axis=1).astype(bf16)
-        got = exchange(parts, shift, wide)
-        if before is not None:
-            got, before = lax.optimization_barrier((got, before))
-        total = jnp.sum(got.astype(f32), axis=0)
-    return total[:-16].astype(bf16), total[-16:], before
-
-
-def spread_dp(value):
-    for shift, wide in reversed(levels(lax.axis_size("dp"))):
-        count = 1 << wide
-        parts = jnp.broadcast_to(value[None], (count,) + value.shape)
-        value = exchange(parts, shift, wide).reshape((count * value.shape[0],) + value.shape[1:])
-    return value.reshape(first_parts(), -1, value.shape[1])
+def start_dp(parts):
+    return exchange(parts, *levels(lax.axis_size("dp"))[0])
+
+
+def fold_dp(got):
+    total = jnp.sum(got.astype(f32), axis=0)
+    for shift, wide in levels(lax.axis_size("dp"))[1:]:
+        parts = total.astype(bf16).reshape(1 << wide, -1, total.shape[1])
+        total = jnp.sum(exchange(parts, shift, wide).astype(f32), axis=0)
+    return total.astype(bf16)
+
+
+def masks():
+    return [1 << bit for bit in range(lax.axis_size("dp").bit_length() - 1)]
+
+
+def halves(value, mask):
+    bit = (lax.axis_index("dp") & mask) != 0
+    rows = value.shape[0] // 2
+    low, high = value[:rows], value[rows:]
+    return jnp.where(bit, low, high), jnp.where(bit, high, low)
+
+
+def give(value, small, mask):
+    return jnp.concatenate([halves(value, mask)[0], small], axis=0)
+
+
+def halve_dp(value, small, mask, other=None):
+    got, other = lax.optimization_barrier((swap(give(value, small, mask), "dp", mask), other))
+    got = got.astype(f32)
+    kept = halves(value, mask)[1]
+    rows = kept.shape[0]
+    value = (kept.astype(f32) + got[:rows]).astype(bf16)
+    return value, (small.astype(f32) + got[rows:]).astype(bf16), other
+
+
+def after(value, *others):
+    return lax.optimization_barrier((value, others))[0]
+
+
+def double_dp(value, mask, other=None):
+    bit = (lax.axis_index("dp") & mask) != 0
+    got, other = lax.optimization_barrier((swap(value, "dp", mask), other))
+    value = jnp.concatenate([jnp.where(bit, got, value), jnp.where(bit, value, got)], axis=0)
+    return value, other
+
+
+def by_index(value):
+    bits = len(masks())
+    width = value.shape[-1]
+    value = value.reshape((2,) * bits + (-1, width)).transpose(*reversed(range(bits)), bits, bits + 1)
+    wides = [wide for _, wide in levels(lax.axis_size("dp"))]
+    value = value.reshape(*[1 << wide for wide in reversed(wides)], -1, width)
+    count = len(wides)
+    value = value.transpose(*reversed(range(count)), count, count + 1)
+    return value.reshape(1 << wides[0], -1, width)
 
 
 def shards(
@@ -775,10 +817,7 @@
 
     tie = lax.optimization_barrier
     wos = [output_weight] + [swap(output_weight, "mp", n) for n in (1, 2, 3)]
-    wis = [inner_weight, swap(inner_weight, "mp", 1)]
-    wus = [outer_weight, swap(outer_weight, "mp", 1)]
     bis = [inner_bias[None], swap(inner_bias[None], "mp", 1)]
-
     projections = (query_weight, key_weight, value_weight)
     tokens_own, cot_own, normed, qc, qp, v, ktt, p, ot, attended, linv = attention_forward(
         item_kind, place, tokens, cotangent, gain1, shift1, *projections, content_bias[None],
@@ -787,60 +826,71 @@
     blocks = attended.reshape(4, 2, own, cols)
     pick = lambda c: lax.dynamic_index_in_dim(blocks, c, 1, False).reshape(4 * own, cols)
     near, far = pick(1 - core), pick(core)
+    near, far, wi, wu, wos, bis = tie((near, far, inner_weight, outer_weight, wos, bis))
+    wis = [inner_weight, swap(wi, "mp", 1)]
+    wus = [outer_weight, swap(wu, "mp", 1)]
     atts = [swap(near, "mp", 1), swap(far, "mp", 2), swap(near, "mp", 3)]
-    back_keep, back_send, out_keep, out_send, residual, keep, near = feed(
+    back_keep, back_send, out, residual, bias, near, keep = feed(
         place, tokens_own, cot_own, attended, atts, wos, wis, wus, bis, bu, gain2, shift2
     )
     back_got = swap(back_send, "mp", 2)
     near_got = swap(near, "mp", 1)
     feed_sum = (keep.astype(f32) + near_got.astype(f32)).astype(bf16)
-    feed_part, feed_small, _ = reduce_dp(feed_sum)
+    feed_got = start_dp(feed_sum)
 
     res, sums, *turned = turn(
         place, back_keep, back_got, residual, cot_own, attended, atts, wos, gain2
     )
     grads, weight_parts = turned[:4], turned[4:]
     grads = [grads[0]] + [swap(grads[n], "mp", n) for n in (1, 2, 3)]
-    grads, weight_parts, out_send, feed_part = tie(
-        (grads, weight_parts, out_send, feed_part)
-    )
-    feed_total = spread_dp(feed_part)
+    sums = jnp.concatenate([sums, bias[:1] + swap(bias[1:], "mp", 1)], axis=0)
+    grads, weight_parts, out_send, sums = tie((grads, weight_parts, out, sums))
     weight_parts = [weight_parts[0]] + [swap(weight_parts[n], "mp", n) for n in (1, 2, 3)]
     out_got = swap(out_send, "mp", 2)
 
-    last, near, keep = attention_backward(
+    last, small, near, keep = attention_backward(
         item_kind, place, p, grads, ot, linv, qc, qp, v, ktt, position_weight,
         st, ct, *projections, normed, gain1, shift1, sums, block,
     )
-    last, near, keep, weight_parts, out_got, feed_total = tie(
-        (last, near, keep, weight_parts, out_got, feed_total)
+    last, small, near, keep, weight_parts, out_got, feed_got = tie(
+        (last, small, near, keep, weight_parts, out_got, feed_got)
     )
     near = swap(near, "mp", 1)
-    parts = first_parts()
     out_sum = sum(x.astype(f32) for x in weight_parts).astype(bf16)
-    last = lax.dynamic_update_slice(
-        last, out_sum.reshape(parts, cols // parts, width), (0, 0, 0)
-    )
+    last = lax.dynamic_update_slice(last, out_sum, (0, 0))
     pick = lambda x: lax.dynamic_index_in_dim(x.reshape(2, 2, own, width), 1 - high, 1, False)
-    far = (pick(keep) + pick(near).astype(f32)).astype(bf16).reshape(2 * own, width)
+    far = (pick(keep).astype(f32) + pick(near).astype(f32)).astype(bf16).reshape(2 * own, width)
+    first, *middle = masks()
+    feed_total = fold_dp(after(feed_got, give(last, small, first), far))
     far = swap(far, "mp", 2)
-    mixed = (out_keep + out_got.astype(f32)).astype(bf16)
+
+    last, small, far = halve_dp(last, small, first, far)
+    mixed = (out.astype(f32) + out_got.astype(f32)).astype(bf16)
     mixed = [mixed, swap(mixed, "mp", 1)]
     grad = close(place, keep, near, far, tokens_own, res, gain1)
-    last_part, last_small, grad = reduce_dp(last, grad)
-    tokens_grad = gather_mp(grad)
-    last_total = spread_dp(last_part).astype(f32)
+    beyond = swap(grad, "mp", 2)
+    for mask in reversed(masks()):
+        feed_total, _ = double_dp(feed_total, mask)
+    for mask in middle:
+        last, small, _ = halve_dp(last, small, mask)
+    for mask in reversed(middle):
+        last, _ = double_dp(last, mask)
+    tokens_grad = [grad, swap(grad, "mp", 1), beyond, swap(beyond, "mp", 1)]
+    small = after(small, last)
     mixed, tokens_grad = collect(place, mixed, tokens_grad)
+    last_total, (mixed, tokens_grad) = double_dp(last, first, (mixed, tokens_grad))
+    last_total = last_total.astype(f32)
+    last_small = small.astype(f32)
+    feed_total = by_index(feed_total)
 
     summed = last_small[:5]
     summed = summed + swap(summed, "mp", 1)
     summed = summed + swap(summed, "mp", 2)
     feed_total = feed_total.astype(f32)
-    split = width // parts
-    begin = cols // parts
+    split = width // first_parts()
     inner_grad = feed_total[:, :split].reshape(width, share)
     outer_grad = feed_total[:, split:].reshape(share, width)
-    whole_grad = last_total[:, begin:].reshape(width, width)
+    whole_grad = last_total[cols:]
 
     return (
         mixed,
@@ -851,13 +901,13 @@
         whole_grad[:, cols : 2 * cols],
         whole_grad[:, 2 * cols : 3 * cols],
         whole_grad[:, 3 * cols :],
-        last_small[5, :cols],
-        last_small[5, cols : 2 * cols],
-        last_total[:, :begin].reshape(cols, width),
+        last_small[6, :cols],
+        last_small[6, cols : 2 * cols],
+        last_total[:cols],
         summed[2],
         summed[3],
         inner_grad,
-        feed_small[0],
+        last_small[5],
         outer_grad,
         summed[4],
     )

time: 201 us -> 191 us (0.950)
  Pallas kernels: 84.9 us -> 71.9 us
  starting transfers between devices: 33.9 us -> 40.3 us
  local copies, waits for them, and re-layouts: 14.8 us -> 9.75 us
  other arithmetic: 9.7 us -> 12.8 us
    all_to_all x4 -> x1, waiting for transfers between devices: 20.1 us -> 0.01 us  [exchange(): lax.all_to_all(value, 'dp', split_axis=0, concat_axis=0, tiled=True, axis...]
    ppermute x26 -> x36, waiting for transfers between devices: 34.3 us -> 54.2 us  [swap(): return lax.ppermute(value, axis, [(i, i ^ mask) for i in range(size)])]
    ppermute x26 -> x36, starting transfers between devices: 16.6 us -> 31.1 us  [swap(): return lax.ppermute(value, axis, [(i, i ^ mask) for i in range(size)])]
    all_to_all x4 -> x1, starting transfers between devices: 17.2 us -> 9.15 us  [exchange(): lax.all_to_all(value, 'dp', split_axis=0, concat_axis=0, tiled=True, axis...]
    pallas_call x1, Pallas kernels: 28.6 us -> 22 us  [attention_backward(): pl.pallas_call(functools.partial(backward_body, count, block, length // 2...]
    pallas_call x1, Pallas kernels: 23.9 us -> 19.8 us  [attention_forward(): pl.pallas_call(functools.partial(forward_body, block, length // 2), grid=...]
    unnamed x46 -> x52, local copies, waits for them, and re-layouts: 5.87 us -> 2.8 us
    concatenate x0 -> x9, other arithmetic: none -> 2.95 us  [the longest x3 1.5 us: give(): return jnp.concatenate([halves(value, mask)[0], small], axis=0)]
  transfers between devices with their start and end apart: 30 -> 37, of which waited for: 10 -> 16; matrix products, arithmetic and copies ran while one was open for 8% -> 8% of each run, Pallas kernels for 34% -> 28%
where the time goes in v2:
time: 191 us
  Pallas kernels  71.9 us (38%)
  waiting for transfers between devices  54.2 us (28%)
  starting transfers between devices  40.3 us (21%)
  other arithmetic  12.8 us (7%)
  local copies, waits for them, and re-layouts  9.75 us (5%)
    ppermute x36, waiting for transfers between devices, swap(): return lax.ppermute(value, axis, [(i, i ^ mask) for i in range(size)])  54.2 us
    ppermute x36, starting transfers between devices, swap(): return lax.ppermute(value, axis, [(i, i ^ mask) for i in range(size)])  31.1 us
    pallas_call x1, Pallas kernels, attention_backward(): pl.pallas_call(functools.partial(backward_body, count, block, length // 2...  22 us
    pallas_call x1, Pallas kernels, attention_forward(): pl.pallas_call(functools.partial(forward_body, block, length // 2), grid=...  19.8 us
    pallas_call x1, Pallas kernels, feed(): pl.pallas_call(feed_body, grid_spec=pltpu.PrefetchScalarGridSpec(num_scal...  17.7 us
    all_to_all x1, starting transfers between devices, exchange(): lax.all_to_all(value, 'dp', split_axis=0, concat_axis=0, tiled=True, axis...  9.15 us
    pallas_call x1, Pallas kernels, turn(): pl.pallas_call(turn_body, grid_spec=pltpu.PrefetchScalarGridSpec(num_scal...  5.77 us
    pallas_call x1, Pallas kernels, close(): pl.pallas_call(close_body, grid_spec=pltpu.PrefetchScalarGridSpec(num_sca...  3.95 us
  transfers between devices with their start and end apart: 37, of which 16 were waited for; matrix products, arithmetic and copies ran while one was open for 8% of the time, Pallas kernels for 28%

profile of v2, /device:TPU:0, one launch (start us, length us, event | category | flops | bytes accessed | tf_op | source)
XLA Modules:
  0.0 190.7 jit_solution(5616202948639137564)
XLA Ops:
  1.2 2.6 %collective-permute-start.1 = (bf16[128,512]{1,0:T(8,128)(2,1)}, bf16[128,512]{1,0:T(8,128)(2,1)S(1)}, u32[]{:S(2)}, u32[]{:S(2)}) collective-permute-start(bf16[128,512]{1,0:T(8,128)(2,1)} %w0.1), channel_id=1, source_target_pairs={{0,2},{1,3},{2,0},{3,1},{4,6},{5,7},{6,4},{7,5},{8,10},{9,11},{10,... | collective-permute-start | bytes 393224 | tf_op jit(solution)/shard_map/ppermute | solution.py:686
  5.3 19.8 %attention_forward.1 = (bf16[1024,512]{1,0:T(8,128)(2,1)}, bf16[1024,512]{1,0:T(8,128)(2,1)}, bf16[2048,512]{1,0:T(8,128)(2,1)}, bf16[2048,128]{1,0:T(8,128)(2,1...) custom-call(s32[1]{0:T(128)S(6)} %copy.49.kind, ...), custom_call_target="tpu_custom_call" | custom-call | flops 27499999232 | bytes 1024 | tf_op jit(solution)/shard_map/attention_forward/pallas_call | solution.py:193
  25.1 1.1 constant_dynamic-slice_fusion
  27.2 1.7 collective-permute-start.6
  29.4 6.2 %collective-permute-done.6.a3 = bf16[1024,128]{1,0:T(8,128)(2,1)S(1)} collective-permute-done((bf16[1024,128]{1,0:T(8,128)(2,1)S(1)}, bf16[1024,128]{1,0:T(8,128)(2,1)S(1)}, u32[]{:S(2)}, u32[]{:S(2)}) %collective-permute-start.6) | collective-permute-done | bytes 262176 | tf_op jit(solution)/shard_map/ppermute | solution.py:686
  35.5 5.9 %collective-permute-done.5.a2 = bf16[1024,128]{1,0:T(8,128)(2,1)S(1)} collective-permute-done((bf16[1024,128]{1,0:T(8,128)(2,1)S(1)}, bf16[1024,128]{1,0:T(8,128)(2,1)S(1)}, u32[]{:S(2)}, u32[]{:S(2)}) %collective-permute-start.5) | collective-permute-done | bytes 262176 | tf_op jit(solution)/shard_map/ppermute | solution.py:686
  42.5 17.7 %feed.1 = (bf16[512,512]{1,0:T(8,128)(2,1)}, bf16[512,512]{1,0:T(8,128)(2,1)}, bf16[1024,512]{1,0:T(8,128)(2,1)}, f32[512,512]{1,0:T(8,128)}, f32[2,512]{1,0:T(2...) custom-call(s32[3]{0:T(128)} %pad_add_fusion.place, bf16[1024,512]{1,0:T(8,128)(2,1)} %get-tuple-element.89.tokens.t0.t1, ...), custom_call_target="tpu_custom_call" | custom-call | flops 14300000256 | bytes 1024 | tf_op jit(solution)/shard_map/feed/pallas_call | solution.py:509
  60.3 1.8 collective-permute-start.9
  62.1 0.7 slice.104
  63.1 2.5 %add_convert_fusion.1 = bf16[8,128,512]{2,1,0:T(8,128)(2,1)} fusion(bf16[8,128,512]{2,1,0:T(8,128)(2,1)S(1)} %collective-permute-done.18, bf16[8,128,512]{2,1,0:T(8,128)(2,1)} %get-tuple-element.137), kind=kLoop, calls=%fused_computation.2 | loop fusion | flops 2097152 | bytes 3145728 | tf_op jit(solution)/shard_map/convert_element_type | solution.py:838
  65.7 9.1 %all-to-all-start = ((bf16[8,128,512]{2,1,0:T(8,128)(2,1)}), bf16[8,128,512]{2,1,0:T(8,128)(2,1)S(1)}, u32[]{:S(2)}, u32[]{:S(2)}) async-start(bf16[8,128,512]{2,1,0:T(8,128)(2,1)} %add_convert_fusion.1), calls=%async_computation | async-start | bytes 2097152 | tf_op jit(solution)/shard_map/all_to_all | solution.py:715
  74.8 0.8 copy-done.14
  75.6 5.8 %turn.1 = (bf16[512,512]{1,0:T(8,128)(2,1)}, f32[3,512]{1,0:T(4,128)}, bf16[512,128]{1,0:T(8,128)(2,1)}, bf16[512,128]{1,0:T(8,128)(2,1)}, bf16[512,128]{1,0:T(8...) custom-call(s32[3]{0:T(128)} %pad_add_fusion.place, ...), custom_call_target="tpu_custom_call" | custom-call | flops 65999998976 | bytes 1024 | tf_op jit(solution)/shard_map/turn/pallas_call | solution.py:585
  81.5 1.8 collective-permute-start.11
  83.4 1.3 pad_maximum_fusion.8.sums
  84.7 3.4 %collective-permute-done.11.d2 = bf16[512,128]{1,0:T(8,128)(2,1)S(1)} collective-permute-done((bf16[512,128]{1,0:T(8,128)(2,1)}, bf16[512,128]{1,0:T(8,128)(2,1)S(1)}, u32[]{:S(2)}, u32[]{:S(2)}) %collective-permute-start.11) | collective-permute-done | bytes 131104 | tf_op jit(solution)/shard_map/ppermute | solution.py:686
  88.1 1.9 collective-permute-done.12.d3
  90.0 1.7 collective-permute-start.17
  92.0 0.9 collective-permute-start.15
  93.6 22.0 %attention_backward.1 = (bf16[640,512]{1,0:T(8,128)(2,1)}, bf16[16,512]{1,0:T(8,128)(2,1)}, bf16[1024,512]{1,0:T(8,128)(2,1)}, bf16[1024,512]{1,0:T(8,128)(2,1)}) custom-call(s32[1]{0:T(128)S(6)} %copy.49.kind, s32[3]{0:T(128)} %pad_add_fusion.place, bf16[2048,4096]{1,0:T(8,128)(2,1)} %get-tuple-element.88.p, bf16[512,128]{1,0:T(8,128)(2,1)} %get-tuple-element.116.d0, ...), custom_call_target="tpu_custom_call" | custom-call | flops 8800000000 | bytes 1024 | tf_op jit(solution)/shard_map/attention_backward/pallas_call | solution.py:374
  115.6 3.1 %collective-permute-done.15 = bf16[128,512]{1,0:T(8,128)(2,1)S(1)} collective-permute-done((bf16[128,512]{1,0:T(8,128)(2,1)}, bf16[128,512]{1,0:T(8,128)(2,1)S(1)}, u32[]{:S(2)}, u32[]{:S(2)}) %collective-permute-start.15) | collective-permute-done | bytes 131104 | tf_op jit(solution)/shard_map/ppermute | solution.py:686
  118.7 2.2 %collective-permute-done.16 = bf16[128,512]{1,0:T(8,128)(2,1)S(1)} collective-permute-done((bf16[128,512]{1,0:T(8,128)(2,1)}, bf16[128,512]{1,0:T(8,128)(2,1)S(1)}, u32[]{:S(2)}, u32[]{:S(2)}) %collective-permute-start.16) | collective-permute-done | bytes 131104 | tf_op jit(solution)/shard_map/ppermute | solution.py:686
  120.9 0.7 copy-done.7
  121.7 1.8 fusion.3
  123.5 1.1 broadcast_select_fusion.4
  124.6 1.5 pad_maximum_fusion.2
  126.1 2.0 %add_convert_fusion.2 = bf16[2,1,256,512]{3,2,0,1:T(8,128)(2,1)} fusion(bf16[2,2,256,512]{3,2,1,0:T(8,128)(2,1)} %bitcast.15, s32[]{:T(128)S(6)} %select_n.117, bf16[2,2,256,512]{3,2,1,0:T(8,128)(2,1)S(1)} %bitcast.48), kind=kLoop, calls=%fused_computation.4 | loop fusion | flops 1048576 | bytes 1572868 | tf_op jit(solution)/shard_map/convert_element_type | solution.py:862
  128.2 2.7 %collective-permute-start.33 = (bf16[128,512]{1,0:T(8,128)(2,1)S(1)}, bf16[128,512]{1,0:T(8,128)(2,1)S(1)}, u32[]{:S(2)}, u32[]{:S(2)}) collective-permute-start(bf16[128,512]{1,0:T(8,128)(2,1)S(1)} %reduce_sum.12), channel_id=1, source_target_pairs={{0,16},{4,20},{8,24},{12,28},{16,0},{20,4},{24,8},{28,12},{1,17},{... | collective-permute-start | bytes 393224 | tf_op jit(solution)/shard_map/ppermute | solution.py:686
  130.9 7.6 %collective-permute-start.19 = (bf16[336,512]{1,0:T(8,128)(2,1)}, bf16[336,512]{1,0:T(8,128)(2,1)S(1)}, u32[]{:S(2)}, u32[]{:S(2)}) collective-permute-start(bf16[336,512]{1,0:T(8,128)(2,1)} %pad_maximum_fusion.2), channel_id=1, source_target_pairs={{0,4},{4,0},{8,12},{12,8},{16,20},{20,16},{24,28},{28,24},{1,5},{5... | collective-permute-start | bytes 1032200 | tf_op jit(solution)/shard_map/ppermute | solution.py:686
  138.5 0.9 collective-permute-start.21
  139.9 7.0 %collective-permute-done.34 = bf16[256,512]{1,0:T(8,128)(2,1)S(1)} collective-permute-done((bf16[256,512]{1,0:T(8,128)(2,1)S(1)}, bf16[256,512]{1,0:T(8,128)(2,1)S(1)}, u32[]{:S(2)}, u32[]{:S(2)}) %collective-permute-start.34) | collective-permute-done | bytes 262176 | tf_op jit(solution)/shard_map/ppermute | solution.py:686
  147.0 5.2 %collective-permute-done.21.got = bf16[512,512]{1,0:T(8,128)(2,1)S(1)} collective-permute-done((bf16[512,512]{1,0:T(8,128)(2,1)}, bf16[512,512]{1,0:T(8,128)(2,1)S(1)}, u32[]{:S(2)}, u32[]{:S(2)}) %collective-permute-start.21) | collective-permute-done | bytes 524320 | tf_op jit(solution)/shard_map/ppermute | solution.py:686
  153.0 0.9 collective-permute-start.35
  153.9 4.2 %collective-permute-done.22 = bf16[176,512]{1,0:T(8,128)(2,1)S(1)} collective-permute-done((bf16[176,512]{1,0:T(8,128)(2,1)S(1)}, bf16[176,512]{1,0:T(8,128)(2,1)S(1)}, u32[]{:S(2)}, u32[]{:S(2)}) %collective-permute-start.22) | collective-permute-done | bytes 180256 | tf_op jit(solution)/shard_map/ppermute | solution.py:686
  158.7 3.9 %close.1.g0 = bf16[512,512]{1,0:T(8,128)(2,1)} custom-call(s32[3]{0:T(128)} %pad_add_fusion.place, bf16[1024,512]{1,0:T(8,128)(2,1)} %get-tuple-element.145.keep0.keep1, bf16[1024,512]{1,0:T(8,128)(2,1)} %get-tuple-element.145.keep0.keep1, bf16[1024,512]{1,0:T(8,128)(2,1)} %collective-permute-done.20.near0.near1, ...), custom_call_target="tpu_custom_call" | custom-call | flops 2200000000 | bytes 1024 | tf_op jit(solution)/shard_map/close/pallas_call | solution.py:627
  162.6 0.7 collective-permute-start.29
  163.4 1.0 collective-permute-done.23
  164.4 1.7 collective-permute-start.24
  166.1 5.3 %collective-permute-done.24 = bf16[80,512]{1,0:T(8,128)(2,1)S(1)} collective-permute-done((bf16[80,512]{1,0:T(8,128)(2,1)S(1)}, bf16[80,512]{1,0:T(8,128)(2,1)S(1)}, u32[]{:S(2)}, u32[]{:S(2)}) %collective-permute-start.24) | collective-permute-done | bytes 81952 | tf_op jit(solution)/shard_map/ppermute | solution.py:686
  172.3 4.6 %collective-permute-done.25 = bf16[160,512]{1,0:T(8,128)(2,1)S(1)} collective-permute-done((bf16[160,512]{1,0:T(8,128)(2,1)S(1)}, bf16[160,512]{1,0:T(8,128)(2,1)S(1)}, u32[]{:S(2)}, u32[]{:S(2)}) %collective-permute-start.25) | collective-permute-done | bytes 163872 | tf_op jit(solution)/shard_map/ppermute | solution.py:686
  177.0 1.6 fusion.7
  178.6 0.8 collective-permute-start.26
  179.7 1.0 collective-permute-start.32
  181.8 1.7 collective-permute-done.32
  184.2 2.7 %collect.1 = (bf16[2048,512]{1,0:T(8,128)(2,1)}, bf16[2048,512]{1,0:T(8,128)(2,1)}) custom-call(s32[3]{0:T(128)S(1)} %copy-done, bf16[1024,512]{1,0:T(8,128)(2,1)S(1)} %add_convert_fusion.m0, bf16[1024,512]{1,0:T(8,128)(2,1)S(1)} %collective-permute-done.27.m1, bf16[512,512]{1,0:T(8,128)(2,1)S(1)} %copy-done.1, ...), custom_call_target="tpu_custom_call" | custom-call | flops 3300000000 | bytes 1024 | tf_op jit(solution)/shard_map/collect/pallas_call | solution.py:671
  186.9 1.8 collective-permute-done.26
  189.0 1.0 fusion.8
  190.0 0.7 slice.154
  (133 shorter events, 10.8 us)
Async XLA Ops:
  0.7 25.5 %collective-permute-start = (bf16[128,512]{1,0:T(8,128)(2,1)}, bf16[128,512]{1,0:T(8,128)(2,1)S(1)}, u32[]{:S(2)}, u32[]{:S(2)}) collective-permute-start(bf16[128,512]{1,0:T(8,128)(2,1)} %w0.1), channel_id=1, source_target_pairs={{0,1},{1,0},{2,3},{3,2},{4,5},{5,4},{6,7},{7,6},{8,9},{9,8},{10,11... | collective-permute-start | bytes 393224 | tf_op jit(solution)/shard_map/ppermute | solution.py:686
  1.2 25.0 %collective-permute-start.1 = (bf16[128,512]{1,0:T(8,128)(2,1)}, bf16[128,512]{1,0:T(8,128)(2,1)S(1)}, u32[]{:S(2)}, u32[]{:S(2)}) collective-permute-start(bf16[128,512]{1,0:T(8,128)(2,1)} %w0.1), channel_id=1, source_target_pairs={{0,2},{1,3},{2,0},{3,1},{4,6},{5,7},{6,4},{7,5},{8,10},{9,11},{10,... | collective-permute-start | bytes 393224 | tf_op jit(solution)/shard_map/ppermute | solution.py:686
  3.8 22.5 %collective-permute-start.2 = (bf16[128,512]{1,0:T(8,128)(2,1)}, bf16[128,512]{1,0:T(8,128)(2,1)S(1)}, u32[]{:S(2)}, u32[]{:S(2)}) collective-permute-start(bf16[128,512]{1,0:T(8,128)(2,1)} %w0.1), channel_id=1, source_target_pairs={{0,3},{1,2},{2,1},{3,0},{4,7},{5,6},{6,5},{7,4},{8,11},{9,10},{10,... | collective-permute-start | bytes 393224 | tf_op jit(solution)/shard_map/ppermute | solution.py:686
  3.8 22.3 %collective-permute-start.3 = (f32[1,512]{1,0:T(1,128)}, f32[1,512]{1,0:T(1,128)S(1)}, u32[]{:S(2)}, u32[]{:S(2)}) collective-permute-start(f32[1,512]{1,0:T(1,128)} %bitcast.55), channel_id=1, source_target_pairs={{0,1},{1,0},{2,3},{3,2},{4,5},{5,4},{6,7},{7,6},{8,9},{9,8},{10,11... | collective-permute-start | bytes 6152 | tf_op jit(solution)/shard_map/ppermute | solution.py:686
  5.3 21.0 %copy-start.10 = (bf16[512,512]{1,0:T(8,128)(2,1)S(1)}, bf16[512,512]{1,0:T(8,128)(2,1)}, u32[]{:S(2)}) copy-start(bf16[512,512]{1,0:T(8,128)(2,1)} %i0.1) | copy-start | bytes 1572868
  5.3 21.4 %copy-start.11 = (bf16[512,512]{1,0:T(8,128)(2,1)S(1)}, bf16[512,512]{1,0:T(8,128)(2,1)}, u32[]{:S(2)}) copy-start(bf16[512,512]{1,0:T(8,128)(2,1)} %u0.1) | copy-start | bytes 1572868
  26.2 15.3 %copy-start.25 = (f32[1,512]{1,0:T(1,128)}, f32[1,512]{1,0:T(1,128)S(1)}, u32[]{:S(2)}) copy-start(f32[1,512]{1,0:T(1,128)S(1)} %collective-permute-done.3.b1) | copy-start | bytes 6148
  26.2 15.3 %copy-start.19 = (bf16[128,512]{1,0:T(8,128)(2,1)}, bf16[128,512]{1,0:T(8,128)(2,1)S(1)}, u32[]{:S(2)}) copy-start(bf16[128,512]{1,0:T(8,128)(2,1)S(1)} %collective-permute-done.w1) | copy-start | bytes 393220
  26.2 15.3 %copy-start.20 = (bf16[128,512]{1,0:T(8,128)(2,1)}, bf16[128,512]{1,0:T(8,128)(2,1)S(1)}, u32[]{:S(2)}) copy-start(bf16[128,512]{1,0:T(8,128)(2,1)S(1)} %collective-permute-done.1.w2) | copy-start | bytes 393220
  26.2 15.2 %copy-start.21 = (bf16[128,512]{1,0:T(8,128)(2,1)}, bf16[128,512]{1,0:T(8,128)(2,1)S(1)}, u32[]{:S(2)}) copy-start(bf16[128,512]{1,0:T(8,128)(2,1)S(1)} %collective-permute-done.2.w3) | copy-start | bytes 393220
  26.2 15.2 %collective-permute-start.7 = (bf16[512,512]{1,0:T(8,128)(2,1)S(1)}, bf16[512,512]{1,0:T(8,128)(2,1)S(1)}, u32[]{:S(2)}, u32[]{:S(2)}) collective-permute-start(bf16[512,512]{1,0:T(8,128)(2,1)S(1)} %copy-done.10), channel_id=1, source_target_pairs={{0,1},{1,0},{2,3},{3,2},{4,5},{5,4},{6,7},{7,6},{8,9},{9,8},{10,11... | collective-permute-start | bytes 1572872 | tf_op jit(solution)/shard_map/ppermute | solution.py:686
  26.7 14.7 %collective-permute-start.8 = (bf16[512,512]{1,0:T(8,128)(2,1)S(1)}, bf16[512,512]{1,0:T(8,128)(2,1)S(1)}, u32[]{:S(2)}, u32[]{:S(2)}) collective-permute-start(bf16[512,512]{1,0:T(8,128)(2,1)S(1)} %copy-done.11), channel_id=1, source_target_pairs={{0,1},{1,0},{2,3},{3,2},{4,5},{5,4},{6,7},{7,6},{8,9},{9,8},{10,11... | collective-permute-start | bytes 1572872 | tf_op jit(solution)/shard_map/ppermute | solution.py:686
  26.8 2.5 %collective-permute-start.4 = (bf16[1024,128]{1,0:T(8,128)(2,1)S(1)}, bf16[1024,128]{1,0:T(8,128)(2,1)S(1)}, u32[]{:S(2)}, u32[]{:S(2)}) collective-permute-start(bf16[1024,128]{1,0:T(8,128)(2,1)S(1)} %bitcast.46), channel_id=1, source_target_pairs={{0,1},{1,0},{2,3},{3,2},{4,5},{5,4},{6,7},{7,6},{8,9},{9,8},{10,11... | collective-permute-start | bytes 786440 | tf_op jit(solution)/shard_map/ppermute | solution.py:686
  27.2 8.3 %collective-permute-start.6 = (bf16[1024,128]{1,0:T(8,128)(2,1)S(1)}, bf16[1024,128]{1,0:T(8,128)(2,1)S(1)}, u32[]{:S(2)}, u32[]{:S(2)}) collective-permute-start(bf16[1024,128]{1,0:T(8,128)(2,1)S(1)} %bitcast.47), channel_id=1, source_target_pairs={{0,3},{1,2},{2,1},{3,0},{4,7},{5,6},{6,5},{7,4},{8,11},{9,10},{10,... | collective-permute-start | bytes 786440 | tf_op jit(solution)/shard_map/ppermute | solution.py:686
  28.9 12.5 %collective-permute-start.5 = (bf16[1024,128]{1,0:T(8,128)(2,1)S(1)}, bf16[1024,128]{1,0:T(8,128)(2,1)S(1)}, u32[]{:S(2)}, u32[]{:S(2)}) collective-permute-start(bf16[1024,128]{1,0:T(8,128)(2,1)S(1)} %bitcast.45), channel_id=1, source_target_pairs={{0,2},{1,3},{2,0},{3,1},{4,6},{5,7},{6,4},{7,5},{8,10},{9,11},{10,... | collective-permute-start | bytes 786440 | tf_op jit(solution)/shard_map/ppermute | solution.py:686
  29.4 12.1 %copy-start.16 = (bf16[1024,128]{1,0:T(8,128)(2,1)}, bf16[1024,128]{1,0:T(8,128)(2,1)S(1)}, u32[]{:S(2)}) copy-start(bf16[1024,128]{1,0:T(8,128)(2,1)S(1)} %collective-permute-done.4.a1) | copy-start | bytes 786436
  60.2 2.9 %collective-permute-start.18 = (bf16[8,128,512]{2,1,0:T(8,128)(2,1)}, bf16[8,128,512]{2,1,0:T(8,128)(2,1)S(1)}, u32[]{:S(2)}, u32[]{:S(2)}) collective-permute-start(bf16[8,128,512]{2,1,0:T(8,128)(2,1)} %get-tuple-element.138), channel_id=1, source_target_pairs={{0,1},{1,0},{2,3},{3,2},{4,5},{5,4},{6,7},{7,6},{8,9},{9,8},{10,11... | collective-permute-start | bytes 3145736 | tf_op jit(solution)/shard_map/ppermute | solution.py:686
  60.3 14.6 %collective-permute-start.9 = (bf16[512,512]{1,0:T(8,128)(2,1)}, bf16[512,512]{1,0:T(8,128)(2,1)S(1)}, u32[]{:S(2)}, u32[]{:S(2)}) collective-permute-start(bf16[512,512]{1,0:T(8,128)(2,1)} %get-tuple-element.103), channel_id=1, source_target_pairs={{0,2},{1,3},{2,0},{3,1},{4,6},{5,7},{6,4},{7,5},{8,10},{9,11},{10,... | collective-permute-start | bytes 1572872 | tf_op jit(solution)/shard_map/ppermute | solution.py:686
  62.8 20.6 %collective-permute-start.13 = (f32[1,512]{1,0:T(1,128)S(1)}, f32[1,512]{1,0:T(1,128)S(1)}, u32[]{:S(2)}, u32[]{:S(2)}) collective-permute-start(f32[1,512]{1,0:T(1,128)S(1)} %slice.104), channel_id=1, source_target_pairs={{0,1},{1,0},{2,3},{3,2},{4,5},{5,4},{6,7},{7,6},{8,9},{9,8},{10,11... | collective-permute-start | bytes 6152 | tf_op jit(solution)/shard_map/ppermute | solution.py:686
  65.7 55.9 %all-to-all-start = ((bf16[8,128,512]{2,1,0:T(8,128)(2,1)}), bf16[8,128,512]{2,1,0:T(8,128)(2,1)S(1)}, u32[]{:S(2)}, u32[]{:S(2)}) async-start(bf16[8,128,512]{2,1,0:T(8,128)(2,1)} %add_convert_fusion.1), calls=%async_computation | async-start | bytes 2097152 | tf_op jit(solution)/shard_map/all_to_all | solution.py:715
  75.6 14.3 %copy-start.3 = (bf16[1024,512]{1,0:T(8,128)(2,1)S(1)}, bf16[1024,512]{1,0:T(8,128)(2,1)}, u32[]{:S(2)}) copy-start(bf16[1024,512]{1,0:T(8,128)(2,1)} %get-tuple-element.136) | copy-start | bytes 3145732
  81.4 3.3 %collective-permute-start.10 = (bf16[512,128]{1,0:T(8,128)(2,1)}, bf16[512,128]{1,0:T(8,128)(2,1)S(1)}, u32[]{:S(2)}, u32[]{:S(2)}) collective-permute-start(bf16[512,128]{1,0:T(8,128)(2,1)} %get-tuple-element.106), channel_id=1, source_target_pairs={{0,1},{1,0},{2,3},{3,2},{4,5},{5,4},{6,7},{7,6},{8,9},{9,8},{10,11... | collective-permute-start | bytes 393224 | tf_op jit(solution)/shard_map/ppermute | solution.py:686
  81.5 6.6 %collective-permute-start.11 = (bf16[512,128]{1,0:T(8,128)(2,1)}, bf16[512,128]{1,0:T(8,128)(2,1)S(1)}, u32[]{:S(2)}, u32[]{:S(2)}) collective-permute-start(bf16[512,128]{1,0:T(8,128)(2,1)} %get-tuple-element.107), channel_id=1, source_target_pairs={{0,2},{1,3},{2,0},{3,1},{4,6},{5,7},{6,4},{7,5},{8,10},{9,11},{10,... | collective-permute-start | bytes 393224 | tf_op jit(solution)/shard_map/ppermute | solution.py:686
  83.3 6.7 %collective-permute-start.12 = (bf16[512,128]{1,0:T(8,128)(2,1)}, bf16[512,128]{1,0:T(8,128)(2,1)S(1)}, u32[]{:S(2)}, u32[]{:S(2)}) collective-permute-start(bf16[512,128]{1,0:T(8,128)(2,1)} %get-tuple-element.108), channel_id=1, source_target_pairs={{0,3},{1,2},{2,1},{3,0},{4,7},{5,6},{6,5},{7,4},{8,11},{9,10},{10,... | collective-permute-start | bytes 393224 | tf_op jit(solution)/shard_map/ppermute | solution.py:686
  90.0 31.6 %collective-permute-start.17 = (bf16[1024,512]{1,0:T(8,128)(2,1)S(1)}, bf16[1024,512]{1,0:T(8,128)(2,1)S(1)}, u32[]{:S(2)}, u32[]{:S(2)}) collective-permute-start(bf16[1024,512]{1,0:T(8,128)(2,1)S(1)} %copy-done.3), channel_id=1, source_target_pairs={{0,2},{1,3},{2,0},{3,1},{4,6},{5,7},{6,4},{7,5},{8,10},{9,11},{10,... | collective-permute-start | bytes 3145736 | tf_op jit(solution)/shard_map/ppermute | solution.py:686
  91.7 23.9 %collective-permute-start.14 = (bf16[128,512]{1,0:T(8,128)(2,1)}, bf16[128,512]{1,0:T(8,128)(2,1)S(1)}, u32[]{:S(2)}, u32[]{:S(2)}) collective-permute-start(bf16[128,512]{1,0:T(8,128)(2,1)} %get-tuple-element.133), channel_id=1, source_target_pairs={{0,1},{1,0},{2,3},{3,2},{4,5},{5,4},{6,7},{7,6},{8,9},{9,8},{10,11... | collective-permute-start | bytes 393224 | tf_op jit(solution)/shard_map/ppermute | solution.py:686
  92.0 26.7 %collective-permute-start.15 = (bf16[128,512]{1,0:T(8,128)(2,1)}, bf16[128,512]{1,0:T(8,128)(2,1)S(1)}, u32[]{:S(2)}, u32[]{:S(2)}) collective-permute-start(bf16[128,512]{1,0:T(8,128)(2,1)} %get-tuple-element.134), channel_id=1, source_target_pairs={{0,2},{1,3},{2,0},{3,1},{4,6},{5,7},{6,4},{7,5},{8,10},{9,11},{10,... | collective-permute-start | bytes 393224 | tf_op jit(solution)/shard_map/ppermute | solution.py:686
  92.9 28.0 %collective-permute-start.16 = (bf16[128,512]{1,0:T(8,128)(2,1)}, bf16[128,512]{1,0:T(8,128)(2,1)S(1)}, u32[]{:S(2)}, u32[]{:S(2)}) collective-permute-start(bf16[128,512]{1,0:T(8,128)(2,1)} %get-tuple-element.135), channel_id=1, source_target_pairs={{0,3},{1,2},{2,1},{3,0},{4,7},{5,6},{6,5},{7,4},{8,11},{9,10},{10,... | collective-permute-start | bytes 393224 | tf_op jit(solution)/shard_map/ppermute | solution.py:686
  93.6 28.1 %copy-start.4 = (f32[128,512]{1,0:T(8,128)S(1)}, f32[128,512]{1,0:T(8,128)}, u32[]{:S(2)}) copy-start(f32[128,512]{1,0:T(8,128)} %get-tuple-element.140) | copy-start | bytes 786436
  121.6 4.5 %collective-permute-start.20 = (bf16[1024,512]{1,0:T(8,128)(2,1)}, bf16[1024,512]{1,0:T(8,128)(2,1)}, u32[]{:S(2)}, u32[]{:S(2)}) collective-permute-start(bf16[1024,512]{1,0:T(8,128)(2,1)} %get-tuple-element.146), channel_id=1, source_target_pairs={{0,1},{1,0},{2,3},{3,2},{4,5},{5,4},{6,7},{7,6},{8,9},{9,8},{10,11... | collective-permute-start | bytes 3145736 | tf_op jit(solution)/shard_map/ppermute | solution.py:686
  128.2 11.2 %collective-permute-start.33 = (bf16[128,512]{1,0:T(8,128)(2,1)S(1)}, bf16[128,512]{1,0:T(8,128)(2,1)S(1)}, u32[]{:S(2)}, u32[]{:S(2)}) collective-permute-start(bf16[128,512]{1,0:T(8,128)(2,1)S(1)} %reduce_sum.12), channel_id=1, source_target_pairs={{0,16},{4,20},{8,24},{12,28},{16,0},{20,4},{24,8},{28,12},{1,17},{... | collective-permute-start | bytes 393224 | tf_op jit(solution)/shard_map/ppermute | solution.py:686
  130.9 16.1 %collective-permute-start.19 = (bf16[336,512]{1,0:T(8,128)(2,1)}, bf16[336,512]{1,0:T(8,128)(2,1)S(1)}, u32[]{:S(2)}, u32[]{:S(2)}) collective-permute-start(bf16[336,512]{1,0:T(8,128)(2,1)} %pad_maximum_fusion.2), channel_id=1, source_target_pairs={{0,4},{4,0},{8,12},{12,8},{16,20},{20,16},{24,28},{28,24},{1,5},{5... | collective-permute-start | bytes 1032200 | tf_op jit(solution)/shard_map/ppermute | solution.py:686
  138.5 13.7 %collective-permute-start.21 = (bf16[512,512]{1,0:T(8,128)(2,1)}, bf16[512,512]{1,0:T(8,128)(2,1)S(1)}, u32[]{:S(2)}, u32[]{:S(2)}) collective-permute-start(bf16[512,512]{1,0:T(8,128)(2,1)} %bitcast.44), channel_id=1, source_target_pairs={{0,2},{1,3},{2,0},{3,1},{4,6},{5,7},{6,4},{7,5},{8,10},{9,11},{10,... | collective-permute-start | bytes 1572872 | tf_op jit(solution)/shard_map/ppermute | solution.py:686
  139.5 12.8 %copy-start.2 = (bf16[640,512]{1,0:T(8,128)(2,1)S(1)}, bf16[640,512]{1,0:T(8,128)(2,1)}, u32[]{:S(2)}) copy-start(bf16[640,512]{1,0:T(8,128)(2,1)} %fusion.3) | copy-start | bytes 1966084
  139.5 7.5 %collective-permute-start.34 = (bf16[256,512]{1,0:T(8,128)(2,1)S(1)}, bf16[256,512]{1,0:T(8,128)(2,1)S(1)}, u32[]{:S(2)}, u32[]{:S(2)}) collective-permute-start(bf16[256,512]{1,0:T(8,128)(2,1)S(1)} %pad_maximum_fusion.4), channel_id=1, source_target_pairs={{0,8},{4,12},{8,0},{12,4},{16,24},{20,28},{24,16},{28,20},{1,9},{5... | collective-permute-start | bytes 786440 | tf_op jit(solution)/shard_map/ppermute | solution.py:686
  139.9 12.6 %copy-start.8 = (bf16[16,512]{1,0:T(8,128)(2,1)S(1)}, bf16[16,512]{1,0:T(8,128)(2,1)}, u32[]{:S(2)}) copy-start(bf16[16,512]{1,0:T(8,128)(2,1)} %get-tuple-element.144) | copy-start | bytes 49156
  139.9 44.3 %collective-permute-start.27 = (bf16[1024,512]{1,0:T(8,128)(2,1)S(1)}, bf16[1024,512]{1,0:T(8,128)(2,1)S(1)}, u32[]{:S(2)}, u32[]{:S(2)}) collective-permute-start(bf16[1024,512]{1,0:T(8,128)(2,1)S(1)} %add_convert_fusion.m0), channel_id=1, source_target_pairs={{0,1},{1,0},{2,3},{3,2},{4,5},{5,4},{6,7},{7,6},{8,9},{9,8},{10,11... | collective-permute-start | bytes 3145736 | tf_op jit(solution)/shard_map/ppermute | solution.py:686
  152.5 5.6 %collective-permute-start.22 = (bf16[176,512]{1,0:T(8,128)(2,1)S(1)}, bf16[176,512]{1,0:T(8,128)(2,1)S(1)}, u32[]{:S(2)}, u32[]{:S(2)}) collective-permute-start(bf16[176,512]{1,0:T(8,128)(2,1)S(1)} %pad_maximum_fusion.5), channel_id=1, source_target_pairs={{0,8},{4,12},{8,0},{12,4},{16,24},{20,28},{24,16},{28,20},{1,9},{5... | collective-permute-start | bytes 540680 | tf_op jit(solution)/shard_map/ppermute | solution.py:686
  153.0 18.5 %collective-permute-start.35 = (bf16[512,512]{1,0:T(8,128)(2,1)S(1)}, bf16[512,512]{1,0:T(8,128)(2,1)S(1)}, u32[]{:S(2)}, u32[]{:S(2)}) collective-permute-start(bf16[512,512]{1,0:T(8,128)(2,1)S(1)} %pad_maximum_fusion.1), channel_id=1, source_target_pairs={{0,4},{4,0},{8,12},{12,8},{16,20},{20,16},{24,28},{28,24},{1,5},{5... | collective-permute-start | bytes 1572872 | tf_op jit(solution)/shard_map/ppermute | solution.py:686
  158.3 6.1 %collective-permute-start.23 = (bf16[96,512]{1,0:T(8,128)(2,1)S(1)}, bf16[96,512]{1,0:T(8,128)(2,1)S(1)}, u32[]{:S(2)}, u32[]{:S(2)}) collective-permute-start(bf16[96,512]{1,0:T(8,128)(2,1)S(1)} %pad_maximum_fusion.7), channel_id=1, source_target_pairs={{0,16},{4,20},{8,24},{12,28},{16,0},{20,4},{24,8},{28,12},{1,17},{... | collective-permute-start | bytes 294920 | tf_op jit(solution)/shard_map/ppermute | solution.py:686
  162.6 16.8 %collective-permute-start.29 = (bf16[512,512]{1,0:T(8,128)(2,1)}, bf16[512,512]{1,0:T(8,128)(2,1)S(1)}, u32[]{:S(2)}, u32[]{:S(2)}) collective-permute-start(bf16[512,512]{1,0:T(8,128)(2,1)} %close.1.g0), channel_id=1, source_target_pairs={{0,2},{1,3},{2,0},{3,1},{4,6},{5,7},{6,4},{7,5},{8,10},{9,11},{10,... | collective-permute-start | bytes 1572872 | tf_op jit(solution)/shard_map/ppermute | solution.py:686
  163.4 20.8 %collective-permute-start.28 = (bf16[512,512]{1,0:T(8,128)(2,1)}, bf16[512,512]{1,0:T(8,128)(2,1)S(1)}, u32[]{:S(2)}, u32[]{:S(2)}) collective-permute-start(bf16[512,512]{1,0:T(8,128)(2,1)} %close.1.g0), channel_id=1, source_target_pairs={{0,1},{1,0},{2,3},{3,2},{4,5},{5,4},{6,7},{7,6},{8,9},{9,8},{10,11... | collective-permute-start | bytes 1572872 | tf_op jit(solution)/shard_map/ppermute | solution.py:686
  164.4 7.0 %collective-permute-start.24 = (bf16[80,512]{1,0:T(8,128)(2,1)S(1)}, bf16[80,512]{1,0:T(8,128)(2,1)S(1)}, u32[]{:S(2)}, u32[]{:S(2)}) collective-permute-start(bf16[80,512]{1,0:T(8,128)(2,1)S(1)} %fusion.2), channel_id=1, source_target_pairs={{0,16},{4,20},{8,24},{12,28},{16,0},{20,4},{24,8},{28,12},{1,17},{... | collective-permute-start | bytes 245768 | tf_op jit(solution)/shard_map/ppermute | solution.py:686
  171.4 5.4 %collective-permute-start.25 = (bf16[160,512]{1,0:T(8,128)(2,1)S(1)}, bf16[160,512]{1,0:T(8,128)(2,1)S(1)}, u32[]{:S(2)}, u32[]{:S(2)}) collective-permute-start(bf16[160,512]{1,0:T(8,128)(2,1)S(1)} %pad_maximum_fusion.6), channel_id=1, source_target_pairs={{0,8},{4,12},{8,0},{12,4},{16,24},{20,28},{24,16},{28,20},{1,9},{5... | collective-permute-start | bytes 491528 | tf_op jit(solution)/shard_map/ppermute | solution.py:686
  176.9 2.8 %collective-permute-start.31 = (f32[5,512]{1,0:T(8,128)S(1)}, f32[5,512]{1,0:T(8,128)S(1)}, u32[]{:S(2)}, u32[]{:S(2)}) collective-permute-start(f32[5,512]{1,0:T(8,128)S(1)} %slice.145), channel_id=1, source_target_pairs={{0,1},{1,0},{2,3},{3,2},{4,5},{5,4},{6,7},{7,6},{8,9},{9,8},{10,11... | collective-permute-start | bytes 30728 | tf_op jit(solution)/shard_map/ppermute | solution.py:686
  178.6 10.1 %collective-permute-start.26 = (bf16[320,512]{1,0:T(8,128)(2,1)S(1)}, bf16[320,512]{1,0:T(8,128)(2,1)S(1)}, u32[]{:S(2)}, u32[]{:S(2)}) collective-permute-start(bf16[320,512]{1,0:T(8,128)(2,1)S(1)} %pad_maximum_fusion.3), channel_id=1, source_target_pairs={{0,4},{4,0},{8,12},{12,8},{16,20},{20,16},{24,28},{28,24},{1,5},{5... | collective-permute-start | bytes 983048 | tf_op jit(solution)/shard_map/ppermute | solution.py:686
  179.5 4.7 %collective-permute-start.30 = (bf16[512,512]{1,0:T(8,128)(2,1)S(1)}, bf16[512,512]{1,0:T(8,128)(2,1)S(1)}, u32[]{:S(2)}, u32[]{:S(2)}) collective-permute-start(bf16[512,512]{1,0:T(8,128)(2,1)S(1)} %collective-permute-done.29.g2), channel_id=1, source_target_pairs={{0,1},{1,0},{2,3},{3,2},{4,5},{5,4},{6,7},{7,6},{8,9},{9,8},{10,11... | collective-permute-start | bytes 1572872 | tf_op jit(solution)/shard_map/ppermute | solution.py:686
  179.7 3.8 %collective-permute-start.32 = (f32[5,512]{1,0:T(8,128)S(1)}, f32[5,512]{1,0:T(8,128)S(1)}, u32[]{:S(2)}, u32[]{:S(2)}) collective-permute-start(f32[5,512]{1,0:T(8,128)S(1)} %slice_add_fusion.7), channel_id=1, source_target_pairs={{0,2},{1,3},{2,0},{3,1},{4,6},{5,7},{6,4},{7,5},{8,10},{9,11},{10,... | collective-permute-start | bytes 30728 | tf_op jit(solution)/shard_map/ppermute | solution.py:686
  (15 other events, 55.6 us)

commit v3 on v2

--- a/solution.py
+++ b/solution.py
@@ -69,26 +69,27 @@
 
 def forward_body(
     block, half_rows,
-    kind, place, tokens, cot, gain, shift, wq, wk, wv, cbias, pbias, wp, st, ct, table, table_t,
-    tokens_own, cot_own, normed_out, qc_out, qp_out, v_out, ktt_out, p_out, ot_out, att_out,
-    linv_out,
-    wcat, kcat, vt, qa, s_scr, m_scr, l_scr, acc,
+    kind, tokens, gain, shift, wq, wk, wv, cbias, pbias, wp, st, ct, table,
+    normed_out, qc_out, qp_out, v_out, kt_out, p_out, ot_out, att_out, linv_out,
+    pbuf, puts, sems, wcat, kcat, vt, qa, s_scr, m_scr, l_scr, acc,
 ):
     ib = pl.program_id(0)
     here = pl.multiple_of(ib * block, block)
     width, cols = wp.shape
     half = width // 2
     mid = block // 2
-    own = tokens_own.shape[0]
+
+    def put(of, c, slot):
+        at = pl.multiple_of(c * block, block), pl.multiple_of(of * 2 * block, 2 * block)
+        target = p_out.at[pl.ds(at[0], block), pl.ds(at[1], 2 * block)]
+        return pltpu.make_async_copy(pbuf.at[slot], target, sems.at[slot])
 
     @pl.when(ib == 0)
     def start():
+        puts[0] = 0
         for n, ref in enumerate((wq, wk, wv)):
             wcat[:, n * cols : (n + 1) * cols] = ref[...]
 
-    at = pl.multiple_of(place[1] * own, own)
-    tokens_own[...] = tokens[pl.ds(at, own), :]
-    cot_own[...] = cot[pl.ds(at, own), :]
     normed, _ = norm_parts(tokens[...].astype(f32))
     normed_out[...] = normed.astype(bf16)
     hidden = (normed * gain[...] + shift[...]).astype(bf16)
@@ -100,10 +101,7 @@
     kcat[pl.ds(here, block), :width] = table[...]
     kcat[pl.ds(here, block), width:] = keys.astype(bf16)
     vt[:, pl.ds(here, block)] = values.T.astype(bf16)
-    keys_t = keys.T.astype(bf16)
-    ktt_out[:DH] = keys_t[:DH]
-    ktt_out[DH : DH + width] = table_t[...]
-    ktt_out[DH + width :] = keys_t[DH:]
+    kt_out[...] = keys.T.astype(bf16)
     queries_t = queries.T
     column = lambda row: jnp.broadcast_to(row, (8, row.shape[1])).T[:, :1]
     content = ((queries_t + column(cbias[...])) * (0.125 * LOG2E)).astype(bf16)
@@ -143,10 +141,17 @@
     lax.fori_loop(lo, ib, score_loop, 0)
     m_scr[...] = jnp.broadcast_to(jnp.max(m_scr[...], axis=0, keepdims=True), m_scr.shape)
 
+    done = puts[0]
+    slot = done & 1
+
+    @pl.when(done >= 2)
+    def free():
+        put(ib, ib, slot).wait()
+
     p = jnp.exp2(s_scr[first, :] - m_scr[0:1])
     l_scr[...] = fold(p, jnp.sum)
     low = p.astype(bf16)
-    p_out[first, :] = low
+    pbuf[slot, :mid] = low
     for h in range(2):
         rows = slice(DH * h, DH * h + DH)
         to = slice(h * block + mid, (h + 1) * block)
@@ -154,21 +159,30 @@
         p = jnp.exp2(s_scr[second, to] - m_scr[0:1, to])
         l_scr[:, to] += fold(p, jnp.sum)
         part = p.astype(bf16)
-        p_out[second, to] = part
+        pbuf[slot, mid:, to] = part
         acc[rows, mid:] += dot(vt[rows, second], part)
 
-    def prob_loop(c, carry):
+    put(ib, ib, slot).start()
+
+    def prob_loop(c, done):
+        slot = done & 1
+
+        @pl.when(done >= 2)
+        def free():
+            put(ib, c, slot).wait()
+
         rows = pl.ds(pl.multiple_of(c * block, block), block)
         p = jnp.exp2(s_scr[rows, :] - m_scr[0:1])
         l_scr[...] += fold(p, jnp.sum)
         low = p.astype(bf16)
-        p_out[rows, :] = low
+        pbuf[slot] = low
+        put(ib, c, slot).start()
         for h in range(2):
             heads = slice(DH * h, DH * h + DH)
             acc[heads] += dot(vt[heads, rows], low[:, h * block : (h + 1) * block])
-        return carry
-
-    lax.fori_loop(lo, ib, prob_loop, 0)
+        return done + 1
+
+    puts[0] = lax.fori_loop(lo, ib, prob_loop, done + 1)
     inverse = 1.0 / jnp.sum(l_scr[...], axis=0, keepdims=True)
     linv_out[...] = inverse
     attended = jnp.concatenate(
@@ -178,41 +192,46 @@
     ot_out[...] = attended
     att_out[...] = attended.T.astype(bf16)
 
+    @pl.when(ib == pl.num_programs(0) - 1)
+    def finish():
+        for slot in range(2):
+            put(ib, ib, slot).wait()
+
 
 def attention_forward(
-    kind, place, tokens, cot, gain, shift, wq, wk, wv, cbias, pbias, wp, st, ct, table, table_t,
-    block,
+    kind, tokens, gain, shift, wq, wk, wv, cbias, pbias, wp, st, ct, table, block
 ):
     length, width = table.shape
     cols = wp.shape[1]
     count = length // block
     row = lambda n, w: pl.BlockSpec((n, w), lambda i: (i, 0))
     col = lambda n, w: pl.BlockSpec((n, w), lambda i: (0, i))
-    smem = pl.BlockSpec(memory_space=pltpu.SMEM)
     shape = jax.ShapeDtypeStruct
     return pl.pallas_call(
         functools.partial(forward_body, block, length // 2),
         grid=(count,),
         in_specs=[
-            smem, smem, row(block, width), row(block, width),
+            pl.BlockSpec(memory_space=pltpu.SMEM), row(block, width),
             whole((1, width)), whole((1, width)), *[whole((width, cols))] * 3,
             whole((1, cols)), whole((1, cols)), whole((width, cols)),
-            col(width // 2, block), col(width // 2, block), row(block, width), col(width, block),
+            col(width // 2, block), col(width // 2, block), row(block, width),
         ],
         out_specs=[
-            row(block // 2, width), row(block // 2, width), row(block, width),
-            row(block, cols), row(block, cols), row(block, cols), col(cols + width, block),
-            col(length, 2 * block), col(cols, block), row(block, cols), col(1, 2 * block),
+            row(block, width), row(block, cols), row(block, cols), row(block, cols),
+            col(cols, block), pl.BlockSpec(memory_space=pl.ANY), col(cols, block),
+            row(block, cols), col(1, 2 * block),
         ],
         out_shape=[
-            shape((length // 2, width), bf16), shape((length // 2, width), bf16),
             shape((length, width), bf16),
             shape((length, cols), bf16), shape((length, cols), bf16), shape((length, cols), bf16),
-            shape((cols + width, length), bf16),
+            shape((cols, length), bf16),
             shape((length, 2 * length), bf16), shape((cols, length), f32),
             shape((length, cols), bf16), shape((1, 2 * length), f32),
         ],
         scratch_shapes=[
+            pltpu.VMEM((2, block, 2 * block), bf16),
+            pltpu.SMEM((1,), jnp.int32),
+            pltpu.SemaphoreType.DMA((2,)),
             pltpu.VMEM((width, 3 * cols), bf16),
             pltpu.VMEM((length, width + cols), bf16),
             pltpu.VMEM((cols, length), bf16),
@@ -225,17 +244,15 @@
         compiler_params=params(),
         cost_estimate=cost(25),
         name="attention_forward",
-    )(
-        kind, place, tokens, cot, gain, shift, wq, wk, wv, cbias, pbias, wp, st, ct, table, table_t
-    )
+    )(kind, tokens, gain, shift, wq, wk, wv, cbias, pbias, wp, st, ct, table)
 
 
 def backward_body(
     count, block, half_rows,
-    kind, place, p, d0, d1, d2, d3, ot, linv, qc, qp, v, ktt, wp, st, ct,
+    kind, place, p, d0, d1, d2, d3, ot, linv, qc, qp, v, kt, tt, wp, st, ct,
     wq, wk, wv, normed, gain, shift, sums,
-    last, small, near, mine,
-    wcat, acc, dk, dv, low, low_t, d_scr, dcat, dstack, qstack, delta, mom, colsum, dwp, cb, pb,
+    given, kept, small, near, mine,
+    last, ktt, wcat, acc, dk, dv, low, low_t, d_scr, dcat, dstack, qstack, delta, mom, colsum, dwp, cb, pb,
 ):
     step = pl.program_id(0)
     ib = count - 1 - step
@@ -250,6 +267,9 @@
             ref[...] = jnp.zeros(ref.shape, f32)
         for n, ref in enumerate((wq, wk, wv)):
             wcat[:, n * cols : (n + 1) * cols] = ref[...]
+        ktt[:DH] = kt[:DH]
+        ktt[DH : DH + width] = tt[...]
+        ktt[DH + width :] = kt[DH:]
         for n, ref in enumerate((d0, d1, d2, d3)):
             for part in range(2):
                 at = pl.multiple_of((4 * part + (place[0] ^ n)) * own, own)
@@ -357,10 +377,14 @@
         last[:cols] = jnp.zeros((cols, width), bf16)
         last[cols:, : 3 * cols] = full
         last[cols:, 3 * cols :] = dwp[...].astype(bf16)
+        rows = kept.shape[0]
+        given[:rows] = last[pl.ds(pl.multiple_of((1 - place[3]) * rows, rows), rows), :]
+        given[rows:] = small[...]
+        kept[...] = last[pl.ds(pl.multiple_of(place[3] * rows, rows), rows), :]
 
 
 def attention_backward(
-    kind, place, p, grads, ot, linv, qc, qp, v, ktt, wp, st, ct, wq, wk, wv, normed,
+    kind, place, p, grads, ot, linv, qc, qp, v, kt, tt, wp, st, ct, wq, wk, wv, normed,
     gain, shift, sums, block,
 ):
     length, width = normed.shape
@@ -370,7 +394,7 @@
     col = lambda n, w: pl.BlockSpec((n, w), lambda i: (0, count - 1 - i))
     row = lambda n, w: pl.BlockSpec((n, w), lambda i: (count - 1 - i, 0))
     smem = pl.BlockSpec(memory_space=pltpu.SMEM)
-    message = (cols + width, width)
+    rows = (cols + width) // 2
     return pl.pallas_call(
         functools.partial(backward_body, count, block, length // 2),
         grid=(count,),
@@ -378,21 +402,24 @@
             smem, smem, col(length, 2 * block),
             *[whole((quarter, cols))] * 4,
             col(cols, block), col(1, 2 * block), row(block, cols), row(block, cols),
-            whole(v.shape), whole(ktt.shape), whole(wp.shape),
+            whole(v.shape), whole(kt.shape), whole(tt.shape), whole(wp.shape),
             col(width // 2, block), col(width // 2, block),
             *[whole((width, cols))] * 3, row(block, width),
             whole(gain.shape), whole(shift.shape), whole(sums.shape),
         ],
         out_specs=[
-            whole(message), whole((16, width)), row(block // 2, width), row(block // 2, width)
+            whole((rows + 16, width)), whole((rows, width)), whole((16, width)), row(block // 2, width), row(block // 2, width)
         ],
         out_shape=[
-            jax.ShapeDtypeStruct(message, bf16),
+            jax.ShapeDtypeStruct((rows + 16, width), bf16),
+            jax.ShapeDtypeStruct((rows, width), bf16),
             jax.ShapeDtypeStruct((16, width), bf16),
             jax.ShapeDtypeStruct((length // 2, width), bf16),
             jax.ShapeDtypeStruct((length // 2, width), bf16),
         ],
         scratch_shapes=[
+            pltpu.VMEM((2 * rows, width), bf16),
+            pltpu.VMEM((cols + width, length), bf16),
             pltpu.VMEM((width, 3 * cols), bf16),
             pltpu.VMEM((2, DH + width, block), f32),
             pltpu.VMEM((length, cols), f32),
@@ -414,7 +441,7 @@
         cost_estimate=cost(8),
         name="attention_backward",
     )(
-        kind, place, p, *grads, ot, linv, qc, qp, v, ktt, wp, st, ct, wq, wk, wv, normed,
+        kind, place, p, *grads, ot, linv, qc, qp, v, kt, tt, wp, st, ct, wq, wk, wv, normed,
         gain, shift, sums,
     )
 
@@ -427,18 +454,18 @@
 ):
     step = pl.program_id(0)
     own, width = res_own.shape
-    steps = cots.shape[0] // own
+    steps = cots.shape[0] // (2 * own)
 
     @pl.when(step < steps)
     def rows():
-        c = cot[...]
-        residual = tokens[...].astype(f32)
-        residual = residual + dot(own_att[...].reshape(own_att.shape[-2:]), w0[...])
+        c = cot[...].reshape(2 * own, width)
+        residual = tokens[...].reshape(2 * own, width).astype(f32)
+        residual = residual + dot(own_att[...].reshape(2 * own, own_att.shape[-1]), w0[...])
         for att, wo in ((a1, w1), (a2, w2), (a3, w3)):
             residual = residual + dot(att[...], wo[...])
         normed, _ = norm_parts(residual)
         hidden = (normed * gain[...] + shift[...]).astype(bf16)
-        here = pl.ds(pl.multiple_of(step * own, own), own)
+        here = pl.ds(pl.multiple_of(step * 2 * own, 2 * own), 2 * own)
         cots[here, :] = c
         hidden_t[:, here] = hidden.T
         mixed = 0.5 * (residual + bu[...])
@@ -461,6 +488,10 @@
             back = back_n if back is None else back + back_n
         out[...] = mixed.astype(bf16)
         sums = jnp.concatenate(sums, axis=0)
+        low = place[2] == 0
+        res_own[...] = jnp.where(low, residual[:own], residual[own:])
+        back_keep[...] = jnp.where(low, back[:own], back[own:]).astype(bf16)
+        back_send[...] = jnp.where(low, back[own:], back[:own]).astype(bf16)
 
         @pl.when(step == 0)
         def first():
@@ -470,19 +501,9 @@
         def later():
             bias[...] += sums
 
-        @pl.when(step % 2 == place[2])
-        def mine():
-            res_own[...] = residual
-            back_keep[...] = back.astype(bf16)
-
-        @pl.when(step % 2 != place[2])
-        def other():
-            back_send[...] = back.astype(bf16)
-
-    for n, ref in ((1, near), (0, keep)):
-
-        @pl.when(step == steps + 1 - n)
-        def grads(n=n, ref=ref):
+    @pl.when(step == steps)
+    def grads():
+        for n, ref in ((1, near), (0, keep)):
             parts, length, _ = ref.shape
             share = length // 2
             inner = dot(hidden_t[...], pres[n]).astype(bf16)
@@ -493,25 +514,27 @@
 
 
 def feed(place, tokens, cot, own_att, atts, wos, wis, wus, bis, bu, gain, shift):
-    rows, width = tokens.shape
+    length, width = tokens.shape
     cols = own_att.shape[1]
     share = wis[0].shape[1]
+    rows = length // 2
     own = rows // 4
     spec = lambda s: pl.BlockSpec(s, lambda i, place: (0,) * len(s))
-    at = lambda i: jnp.minimum(i, 3)
-    step = lambda w: pl.BlockSpec((own, w), lambda i, place: (at(i), 0))
-    half = pl.BlockSpec((own, width), lambda i, place: (at(i) // 2, 0))
+    at = lambda i: jnp.minimum(i, 1)
+    step = lambda w: pl.BlockSpec((2 * own, w), lambda i, place: (at(i), 0))
+    half = pl.BlockSpec((own, width), lambda i, place: (at(i), 0))
     parts = first_parts()
     grad_shape = (parts, (width + share) // parts, width)
-    att = pl.BlockSpec((1, 1, own, cols), lambda i, place: (at(i), place[1], 0, 0))
+    mine = lambda w: pl.BlockSpec((2, 1, own, w), lambda i, place: (at(i), place[1], 0, 0))
+    split = lambda x: x.reshape(4, 2, own, x.shape[1])
     others = (*wos, *wis, *wus, *bis, bu, gain, shift)
     shape = jax.ShapeDtypeStruct
     return pl.pallas_call(
         feed_body,
         grid_spec=pltpu.PrefetchScalarGridSpec(
             num_scalar_prefetch=1,
-            grid=(6,),
-            in_specs=[step(width), step(width), att]
+            grid=(3,),
+            in_specs=[mine(width), mine(width), mine(cols)]
             + [step(cols)] * 3
             + [spec(o.shape) for o in others],
             out_specs=[
@@ -533,43 +556,31 @@
         compiler_params=params(),
         cost_estimate=cost(13),
         name="feed",
-    )(place, tokens, cot, own_att.reshape(4, 2, own, cols), *atts, *others)
+    )(place, split(tokens), split(cot), split(own_att), *atts, *others)
 
 
 def turn_body(
     place, keep, got, residual, cot, a0, a1, a2, a3, w0, w1, w2, w3, gain,
-    res_out, sums_out, g0, g1, g2, g3, o0, o1, o2, o3, total,
+    res_out, sums_out, g0, g1, g2, g3, o0, o1, o2, o3,
 ):
-    step = pl.program_id(0)
+    rows, width = keep.shape
     back = keep[...].astype(f32) + got[...].astype(f32)
-    c = cot[...].astype(f32)
+    c = cot[...].reshape(rows, width).astype(f32)
     normed, scale = norm_parts(residual[...])
     fold = lambda values: jnp.sum(values, axis=0, keepdims=True)
-    sums = jnp.concatenate([fold(back * normed), fold(back), fold(c)], axis=0)
+    sums_out[...] = jnp.concatenate([fold(back * normed), fold(back), fold(c)], axis=0)
     e = back * gain[...]
     inner = (
         e
         - jnp.mean(e, axis=-1, keepdims=True)
         - normed * jnp.mean(e * normed, axis=-1, keepdims=True)
     )
-    res = c + scale * inner
-    branch = res.astype(bf16)
+    branch = (c + scale * inner).astype(bf16)
     res_out[...] = branch
     for wo, out in ((w0, g0), (w1, g1), (w2, g2), (w3, g3)):
         out[...] = dot_nt(branch, wo[...]).astype(bf16)
-    products = [dot(att[...].T, branch) for att in (a0, a1, a2, a3)]
-
-    @pl.when(step == 0)
-    def first():
-        sums_out[...] = sums
-        for n in range(4):
-            total[n] = products[n]
-
-    @pl.when(step == 1)
-    def second():
-        sums_out[...] += sums
-        for n, out in enumerate((o0, o1, o2, o3)):
-            out[...] = (total[n] + products[n]).astype(out.dtype)
+    for att, out in ((a0, o0), (a1, o1), (a2, o2), (a3, o3)):
+        out[...] = dot(att[...].reshape(rows, out.shape[0]).T, branch).astype(out.dtype)
 
 
 def turn(place, keep, got, residual, cot, own_att, others, wos, gain):
@@ -577,8 +588,9 @@
     own = rows // 2
     cols = wos[0].shape[0]
     spec = lambda s: pl.BlockSpec(s, lambda i, place: (0,) * len(s))
-    step = lambda w: pl.BlockSpec((own, w), lambda i, place: (i, 0))
-    half = lambda w: pl.BlockSpec((own, w), lambda i, place: (2 * i + place[2], 0))
+    mine = lambda w: pl.BlockSpec((2, 1, own, w), lambda i, place: (0, place[0], 0, 0))
+    half = lambda w: pl.BlockSpec((2, 1, own, w), lambda i, place: (0, place[2], 0, 0))
+    split = lambda x: x.reshape(2, -1, own, x.shape[1])
     shapes = [((rows, width), bf16), ((3, width), f32)]
     shapes = shapes + [((rows, cols), bf16)] * 4
     shapes = shapes + [((cols, width), t) for t in (f32, bf16, bf16, bf16)]
@@ -586,22 +598,22 @@
         turn_body,
         grid_spec=pltpu.PrefetchScalarGridSpec(
             num_scalar_prefetch=1,
-            grid=(2,),
-            in_specs=[step(width), step(width), step(width), half(width)]
-            + [pl.BlockSpec((own, cols), lambda i, place: (4 * i + place[0], 0))]
+            grid=(1,),
+            in_specs=[spec(keep.shape)] * 3
+            + [mine(width), mine(cols)]
             + [half(cols)] * 3
             + [spec(w.shape) for w in wos]
             + [spec(gain.shape)],
-            out_specs=[step(width), spec((3, width))]
-            + [step(cols)] * 4
-            + [spec((cols, width))] * 4,
-            scratch_shapes=[pltpu.VMEM((4, cols, width), f32)],
+            out_specs=[spec(s) for s, _ in shapes],
         ),
         out_shape=[jax.ShapeDtypeStruct(s, t) for s, t in shapes],
         compiler_params=params(),
         cost_estimate=cost(60),
         name="turn",
-    )(place, keep, got, residual, cot, own_att, *others, *wos, gain)
+    )(
+        place, keep, got, residual, split(cot), split(own_att), *[split(x) for x in others],
+        *wos, gain,
+    )
 
 
 def close_body(place, keep0, keep1, near0, near1, got, t0, t1, res, gain, out):
@@ -623,6 +635,7 @@
     rows, width = got.shape
     own = rows // 2
     spec = pl.BlockSpec((rows, width), lambda i, place: (0, 0))
+    mine = lambda part: pl.BlockSpec((own, width), lambda i, place: (4 * part + place[0], 0))
     at = lambda part: pl.BlockSpec((own, width), lambda i, place: (2 * part + place[2], 0))
     return pl.pallas_call(
         close_body,
@@ -630,7 +643,7 @@
             num_scalar_prefetch=1,
             grid=(1,),
             in_specs=[
-                at(0), at(1), at(0), at(1), spec, at(0), at(1), spec,
+                at(0), at(1), at(0), at(1), spec, mine(0), mine(1), spec,
                 pl.BlockSpec((1, width), lambda i, place: (0, 0)),
             ],
             out_specs=spec,
@@ -761,9 +774,12 @@
 
 
 def halve_dp(value, small, mask, other=None):
-    got, other = lax.optimization_barrier((swap(give(value, small, mask), "dp", mask), other))
+    return take(give(value, small, mask), halves(value, mask)[1], small, mask, other)
+
+
+def take(given, kept, small, mask, other=None):
+    got, other = lax.optimization_barrier((swap(given, "dp", mask), other))
     got = got.astype(f32)
-    kept = halves(value, mask)[1]
     rows = kept.shape[0]
     value = (kept.astype(f32) + got[:rows]).astype(bf16)
     return value, (small.astype(f32) + got[rows:]).astype(bf16), other
@@ -801,7 +817,8 @@
     share = inner_weight.shape[1]
     mp = lax.axis_index("mp").astype(jnp.int32)
     core, high = mp & 1, mp >> 1
-    place = jnp.stack([mp, core, high])
+    low = lax.axis_index("dp").astype(jnp.int32) & 1
+    place = jnp.stack([mp, core, high, low])
     half = length // 2
     block = min(512, half)
     per_half = half // block
@@ -819,9 +836,9 @@
     wos = [output_weight] + [swap(output_weight, "mp", n) for n in (1, 2, 3)]
     bis = [inner_bias[None], swap(inner_bias[None], "mp", 1)]
     projections = (query_weight, key_weight, value_weight)
-    tokens_own, cot_own, normed, qc, qp, v, ktt, p, ot, attended, linv = attention_forward(
-        item_kind, place, tokens, cotangent, gain1, shift1, *projections, content_bias[None],
-        position_bias[None], position_weight, st, ct, table, table_t, block,
+    normed, qc, qp, v, kt, p, ot, attended, linv = attention_forward(
+        item_kind, tokens, gain1, shift1, *projections, content_bias[None], position_bias[None],
+        position_weight, st, ct, table, block,
     )
     blocks = attended.reshape(4, 2, own, cols)
     pick = lambda c: lax.dynamic_index_in_dim(blocks, c, 1, False).reshape(4 * own, cols)
@@ -831,7 +848,7 @@
     wus = [outer_weight, swap(wu, "mp", 1)]
     atts = [swap(near, "mp", 1), swap(far, "mp", 2), swap(near, "mp", 3)]
     back_keep, back_send, out, residual, bias, near, keep = feed(
-        place, tokens_own, cot_own, attended, atts, wos, wis, wus, bis, bu, gain2, shift2
+        place, tokens, cotangent, attended, atts, wos, wis, wus, bis, bu, gain2, shift2
     )
     back_got = swap(back_send, "mp", 2)
     near_got = swap(near, "mp", 1)
@@ -839,35 +856,41 @@
     feed_got = start_dp(feed_sum)
 
     res, sums, *turned = turn(
-        place, back_keep, back_got, residual, cot_own, attended, atts, wos, gain2
+        place, back_keep, back_got, residual, cotangent, attended, atts, wos, gain2
     )
     grads, weight_parts = turned[:4], turned[4:]
     grads = [grads[0]] + [swap(grads[n], "mp", n) for n in (1, 2, 3)]
     sums = jnp.concatenate([sums, bias[:1] + swap(bias[1:], "mp", 1)], axis=0)
-    grads, weight_parts, out_send, sums = tie((grads, weight_parts, out, sums))
+    out_send = after(out, grads[1])
+    weight_parts = after(weight_parts, grads[1])
     weight_parts = [weight_parts[0]] + [swap(weight_parts[n], "mp", n) for n in (1, 2, 3)]
     out_got = swap(out_send, "mp", 2)
 
-    last, small, near, keep = attention_backward(
-        item_kind, place, p, grads, ot, linv, qc, qp, v, ktt, position_weight,
+    given, kept, small, near, keep = attention_backward(
+        item_kind, place, p, grads, ot, linv, qc, qp, v, kt, table_t, position_weight,
         st, ct, *projections, normed, gain1, shift1, sums, block,
     )
-    last, small, near, keep, weight_parts, out_got, feed_got = tie(
-        (last, small, near, keep, weight_parts, out_got, feed_got)
+    given, kept, small, near, keep, weight_parts, out_got, feed_got = tie(
+        (given, kept, small, near, keep, weight_parts, out_got, feed_got)
     )
     near = swap(near, "mp", 1)
-    out_sum = sum(x.astype(f32) for x in weight_parts).astype(bf16)
-    last = lax.dynamic_update_slice(last, out_sum, (0, 0))
+    out_sum = sum(x.astype(f32) for x in weight_parts)
+    fill = lambda value, there: (
+        value.astype(f32)
+        + jnp.pad(out_sum * there.astype(f32), ((0, value.shape[0] - cols), (0, 0)))
+    ).astype(bf16)
+    given = fill(given, low)
+    kept = fill(kept, 1 - low)
     pick = lambda x: lax.dynamic_index_in_dim(x.reshape(2, 2, own, width), 1 - high, 1, False)
     far = (pick(keep).astype(f32) + pick(near).astype(f32)).astype(bf16).reshape(2 * own, width)
     first, *middle = masks()
-    feed_total = fold_dp(after(feed_got, give(last, small, first), far))
+    feed_total = fold_dp(after(feed_got, given, far))
     far = swap(far, "mp", 2)
 
-    last, small, far = halve_dp(last, small, first, far)
+    last, small, far = take(given, kept, small, first, far)
     mixed = (out.astype(f32) + out_got.astype(f32)).astype(bf16)
     mixed = [mixed, swap(mixed, "mp", 1)]
-    grad = close(place, keep, near, far, tokens_own, res, gain1)
+    grad = close(place, keep, near, far, tokens, res, gain1)
     beyond = swap(grad, "mp", 2)
     for mask in reversed(masks()):
         feed_total, _ = double_dp(feed_total, mask)

time: 191 us -> 185 us (0.969)
  Pallas kernels: 71.9 us -> 66.4 us
  starting transfers between devices: 40.3 us -> 44.4 us
  waiting for transfers between devices: 54.2 us -> 51.7 us
    all_to_all x1, starting transfers between devices: 9.15 us -> 12.6 us  [exchange(): lax.all_to_all(value, 'dp', split_axis=0, concat_axis=0, tiled=True, axis...]
    pallas_call x1, Pallas kernels: 19.8 us -> 16.9 us  [attention_forward(): pl.pallas_call(functools.partial(forward_body, block, length // 2), grid=...]
    ppermute x36, waiting for transfers between devices: 54.2 us -> 51.7 us  [swap(): return lax.ppermute(value, axis, [(i, i ^ mask) for i in range(size)])]
    pallas_call x1, Pallas kernels: 17.7 us -> 15.6 us  [feed(): pl.pallas_call(feed_body, grid_spec=pltpu.PrefetchScalarGridSpec(num_scal...]
  transfers between devices with their start and end apart: 37 -> 37, of which waited for: 16 -> 14; matrix products, arithmetic and copies ran while one was open for 8% -> 8% of each run, Pallas kernels for 28% -> 27%
where the time goes in v3:
time: 185 us; the launch traced here: 186 us
  Pallas kernels  66.4 us (36%)
  waiting for transfers between devices  51.7 us (28%)
  starting transfers between devices  44.4 us (24%)
  other arithmetic  11.9 us (6%)
  local copies, waits for them, and re-layouts  9.5 us (5%)
  between operations  1.91 us (1%)
    ppermute x36, waiting for transfers between devices, swap(): return lax.ppermute(value, axis, [(i, i ^ mask) for i in range(size)])  51.7 us
    ppermute x36, starting transfers between devices, swap(): return lax.ppermute(value, axis, [(i, i ^ mask) for i in range(size)])  31.8 us
    pallas_call x1, Pallas kernels, attention_backward(): pl.pallas_call(functools.partial(backward_body, count, block, length // 2...  22.2 us
    pallas_call x1, Pallas kernels, attention_forward(): pl.pallas_call(functools.partial(forward_body, block, length // 2), grid=...  16.9 us
    pallas_call x1, Pallas kernels, feed(): pl.pallas_call(feed_body, grid_spec=pltpu.PrefetchScalarGridSpec(num_scal...  15.6 us
    all_to_all x1, starting transfers between devices, exchange(): lax.all_to_all(value, 'dp', split_axis=0, concat_axis=0, tiled=True, axis...  12.6 us
    pallas_call x1, Pallas kernels, turn(): pl.pallas_call(turn_body, grid_spec=pltpu.PrefetchScalarGridSpec(num_scal...  5.15 us
    pallas_call x1, Pallas kernels, close(): pl.pallas_call(close_body, grid_spec=pltpu.PrefetchScalarGridSpec(num_sca...  3.95 us
  transfers between devices with their start and end apart: 37, of which 14 were waited for; matrix products, arithmetic and copies ran while one was open for 8% of the time, Pallas kernels for 27%

profile of v3, /device:TPU:0, one launch (start us, length us, event | category | flops | bytes accessed | tf_op | source)
XLA Modules:
  0.0 185.9 jit_solution(1447528443128704429)
XLA Ops:
  1.2 2.6 %collective-permute-start.1 = (bf16[128,512]{1,0:T(8,128)(2,1)}, bf16[128,512]{1,0:T(8,128)(2,1)S(1)}, u32[]{:S(2)}, u32[]{:S(2)}) collective-permute-start(bf16[128,512]{1,0:T(8,128)(2,1)} %w0.1), channel_id=1, source_target_pairs={{0,2},{1,3},{2,0},{3,1},{4,6},{5,7},{6,4},{7,5},{8,10},{9,11},{10,... | collective-permute-start | bytes 393224 | tf_op jit(solution)/shard_map/ppermute | solution.py:699
  4.7 16.9 %attention_forward.1 = (bf16[2048,512]{1,0:T(8,128)(2,1)}, bf16[2048,128]{1,0:T(8,128)(2,1)}, bf16[2048,128]{1,0:T(8,128)(2,1)}, bf16[2048,128]{1,0:T(8,128)(2,1...) custom-call(s32[1]{0:T(128)S(6)} %copy.48.kind, ...), custom_call_target="tpu_custom_call" | custom-call | flops 27499999232 | bytes 1024 | tf_op jit(solution)/shard_map/attention_forward/pallas_call | solution.py:210
  21.6 1.1 constant_dynamic-slice_fusion
  22.7 0.6 copy-done.20
  24.3 1.7 collective-permute-start.6
  26.1 0.6 pad_add_fusion.place
  26.7 5.9 %collective-permute-done.6.a3 = bf16[1024,128]{1,0:T(8,128)(2,1)S(1)} collective-permute-done((bf16[1024,128]{1,0:T(8,128)(2,1)S(1)}, bf16[1024,128]{1,0:T(8,128)(2,1)S(1)}, u32[]{:S(2)}, u32[]{:S(2)}) %collective-permute-start.6) | collective-permute-done | bytes 262176 | tf_op jit(solution)/shard_map/ppermute | solution.py:699
  32.6 5.9 %collective-permute-done.5.a2 = bf16[1024,128]{1,0:T(8,128)(2,1)S(1)} collective-permute-done((bf16[1024,128]{1,0:T(8,128)(2,1)S(1)}, bf16[1024,128]{1,0:T(8,128)(2,1)S(1)}, u32[]{:S(2)}, u32[]{:S(2)}) %collective-permute-start.5) | collective-permute-done | bytes 262176 | tf_op jit(solution)/shard_map/ppermute | solution.py:699
  38.6 0.6 copy-done.18
  39.6 15.6 %feed.1 = (bf16[512,512]{1,0:T(8,128)(2,1)}, bf16[512,512]{1,0:T(8,128)(2,1)}, bf16[1024,512]{1,0:T(8,128)(2,1)}, f32[512,512]{1,0:T(8,128)}, f32[2,512]{1,0:T(2...) custom-call(s32[4]{0:T(128)} %pad_add_fusion.place, bf16[4,2,256,512]{3,2,1,0:T(8,128)(2,1)} %bitcast.47, ...), custom_call_target="tpu_custom_call" | custom-call | flops 14300000256 | bytes 1024 | tf_op jit(solution)/shard_map/feed/pallas_call | solution.py:532
  55.2 1.8 collective-permute-start.9
  57.0 1.1 collective-permute-done.18
  58.1 2.5 %add_convert_fusion.1 = bf16[8,128,512]{2,1,0:T(8,128)(2,1)} fusion(bf16[8,128,512]{2,1,0:T(8,128)(2,1)S(1)} %collective-permute-done.18, bf16[8,128,512]{2,1,0:T(8,128)(2,1)} %get-tuple-element.126), kind=kLoop, calls=%fused_computation.2 | loop fusion | flops 2097152 | bytes 3145728 | tf_op jit(solution)/shard_map/convert_element_type | solution.py:855
  60.6 12.6 %all-to-all-start = ((bf16[8,128,512]{2,1,0:T(8,128)(2,1)}), bf16[8,128,512]{2,1,0:T(8,128)(2,1)S(1)}, u32[]{:S(2)}, u32[]{:S(2)}) async-start(bf16[8,128,512]{2,1,0:T(8,128)(2,1)} %add_convert_fusion.1), calls=%async_computation | async-start | bytes 2097152 | tf_op jit(solution)/shard_map/all_to_all | solution.py:728
  73.2 0.8 copy-done.15
  74.0 5.2 %turn.1 = (bf16[512,512]{1,0:T(8,128)(2,1)}, f32[3,512]{1,0:T(4,128)}, bf16[512,128]{1,0:T(8,128)(2,1)}, bf16[512,128]{1,0:T(8,128)(2,1)}, bf16[512,128]{1,0:T(8...) custom-call(s32[4]{0:T(128)} %pad_add_fusion.place, ...), custom_call_target="tpu_custom_call" | custom-call | flops 65999998976 | bytes 1024 | tf_op jit(solution)/shard_map/turn/pallas_call | solution.py:597
  79.7 1.5 collective-permute-start.11
  81.3 1.5 collective-permute-start.17
  82.7 1.3 pad_maximum_fusion.7.sums
  85.0 1.3 collective-permute-done.11.d2
  86.3 1.9 %collective-permute-done.12.d3 = bf16[512,128]{1,0:T(8,128)(2,1)S(1)} collective-permute-done((bf16[512,128]{1,0:T(8,128)(2,1)}, bf16[512,128]{1,0:T(8,128)(2,1)S(1)}, u32[]{:S(2)}, u32[]{:S(2)}) %collective-permute-start.12) | collective-permute-done | bytes 131104 | tf_op jit(solution)/shard_map/ppermute | solution.py:699
  88.2 0.6 copy-done.24
  88.9 22.2 %attention_backward.1 = (bf16[336,512]{1,0:T(8,128)(2,1)}, bf16[320,512]{1,0:T(8,128)(2,1)}, bf16[16,512]{1,0:T(8,128)(2,1)}, bf16[1024,512]{1,0:T(8,128)(2,1)}, bf16[1024,512]{1,0:T(8,128)(2,1)}) custom-call(s32[1]{0:T(128)S(6)} %copy.48.kind, s32[4]{0:T(128)} %pad_add_fusion.place, bf16[2048,4096]{1,0:T(8,128)(2,1)} %get-tuple-element.83.p, ...), custom_call_target="tpu_custom_call" | custom-call | flops 8800000000 | bytes 1024 | tf_op jit(solution)/shard_map/attention_backward/pallas_call | solution.py:398
  111.1 3.3 %collective-permute-done.15 = bf16[128,512]{1,0:T(8,128)(2,1)S(1)} collective-permute-done((bf16[128,512]{1,0:T(8,128)(2,1)}, bf16[128,512]{1,0:T(8,128)(2,1)S(1)}, u32[]{:S(2)}, u32[]{:S(2)}) %collective-permute-start.15) | collective-permute-done | bytes 131104 | tf_op jit(solution)/shard_map/ppermute | solution.py:699
  114.4 1.1 collective-permute-done.16
  115.5 0.7 collective-permute-start.20
  116.2 1.2 broadcast_multiply_fusion.1
  117.4 1.8 add_convert_fusion.3
  119.2 1.0 add_convert_fusion.2
  120.3 8.1 %collective-permute-start.33 = (bf16[128,512]{1,0:T(8,128)(2,1)S(1)}, bf16[128,512]{1,0:T(8,128)(2,1)S(1)}, u32[]{:S(2)}, u32[]{:S(2)}) collective-permute-start(bf16[128,512]{1,0:T(8,128)(2,1)S(1)} %reduce_sum.12), channel_id=1, source_target_pairs={{0,16},{4,20},{8,24},{12,28},{16,0},{20,4},{24,8},{28,12},{1,17},{... | collective-permute-start | bytes 393224 | tf_op jit(solution)/shard_map/ppermute | solution.py:699
  128.5 1.5 collective-permute-start.21
  130.0 5.5 %collective-permute-done.33 = bf16[128,512]{1,0:T(8,128)(2,1)S(1)} collective-permute-done((bf16[128,512]{1,0:T(8,128)(2,1)S(1)}, bf16[128,512]{1,0:T(8,128)(2,1)S(1)}, u32[]{:S(2)}, u32[]{:S(2)}) %collective-permute-start.33) | collective-permute-done | bytes 131104 | tf_op jit(solution)/shard_map/ppermute | solution.py:699
  135.6 0.8 collective-permute-start.34
  136.4 1.8 add_convert_fusion.m0
  138.3 5.5 %collective-permute-done.34 = bf16[256,512]{1,0:T(8,128)(2,1)S(1)} collective-permute-done((bf16[256,512]{1,0:T(8,128)(2,1)S(1)}, bf16[256,512]{1,0:T(8,128)(2,1)S(1)}, u32[]{:S(2)}, u32[]{:S(2)}) %collective-permute-start.34) | collective-permute-done | bytes 262176 | tf_op jit(solution)/shard_map/ppermute | solution.py:699
  144.2 2.1 %collective-permute-start.22 = (bf16[176,512]{1,0:T(8,128)(2,1)S(1)}, bf16[176,512]{1,0:T(8,128)(2,1)S(1)}, u32[]{:S(2)}, u32[]{:S(2)}) collective-permute-start(bf16[176,512]{1,0:T(8,128)(2,1)S(1)} %pad_maximum_fusion.4), channel_id=1, source_target_pairs={{0,8},{4,12},{8,0},{12,4},{16,24},{20,28},{24,16},{28,20},{1,9},{5... | collective-permute-start | bytes 540680 | tf_op jit(solution)/shard_map/ppermute | solution.py:699
  146.8 3.4 %collective-permute-done.22 = bf16[176,512]{1,0:T(8,128)(2,1)S(1)} collective-permute-done((bf16[176,512]{1,0:T(8,128)(2,1)S(1)}, bf16[176,512]{1,0:T(8,128)(2,1)S(1)}, u32[]{:S(2)}, u32[]{:S(2)}) %collective-permute-start.22) | collective-permute-done | bytes 180256 | tf_op jit(solution)/shard_map/ppermute | solution.py:699
  150.3 2.6 %collective-permute-start.23 = (bf16[96,512]{1,0:T(8,128)(2,1)S(1)}, bf16[96,512]{1,0:T(8,128)(2,1)S(1)}, u32[]{:S(2)}, u32[]{:S(2)}) collective-permute-start(bf16[96,512]{1,0:T(8,128)(2,1)S(1)} %pad_maximum_fusion.6), channel_id=1, source_target_pairs={{0,16},{4,20},{8,24},{12,28},{16,0},{20,4},{24,8},{28,12},{1,17},{... | collective-permute-start | bytes 294920 | tf_op jit(solution)/shard_map/ppermute | solution.py:699
  152.9 3.9 %close.1.g0 = bf16[512,512]{1,0:T(8,128)(2,1)} custom-call(s32[4]{0:T(128)} %pad_add_fusion.place, bf16[1024,512]{1,0:T(8,128)(2,1)} %get-tuple-element.134.keep0.keep1, bf16[1024,512]{1,0:T(8,128)(2,1)} %get-tuple-element.134.keep0.keep1, bf16[1024,512]{1,0:T(8,128)(2,1)} %copy-done.3, bf16[1024,512]{1,0:T(8,128)(2,1)} %copy-done.3, ...), custom_call_target="tpu_custom_call" | custom-call | flops 2200000000 | bytes 1024 | tf_op jit(solution)/shard_map/close/pallas_call | solution.py:640
  156.9 1.5 collective-permute-start.29
  158.9 7.1 %collective-permute-done.24 = bf16[80,512]{1,0:T(8,128)(2,1)S(1)} collective-permute-done((bf16[80,512]{1,0:T(8,128)(2,1)S(1)}, bf16[80,512]{1,0:T(8,128)(2,1)S(1)}, u32[]{:S(2)}, u32[]{:S(2)}) %collective-permute-start.24) | collective-permute-done | bytes 81952 | tf_op jit(solution)/shard_map/ppermute | solution.py:699
  166.9 5.1 %collective-permute-done.25 = bf16[160,512]{1,0:T(8,128)(2,1)S(1)} collective-permute-done((bf16[160,512]{1,0:T(8,128)(2,1)S(1)}, bf16[160,512]{1,0:T(8,128)(2,1)S(1)}, u32[]{:S(2)}, u32[]{:S(2)}) %collective-permute-start.25) | collective-permute-done | bytes 163872 | tf_op jit(solution)/shard_map/ppermute | solution.py:699
  172.2 1.6 fusion.6
  176.0 2.1 %collective-permute-done.32 = f32[5,512]{1,0:T(8,128)S(1)} collective-permute-done((f32[5,512]{1,0:T(8,128)S(1)}, f32[5,512]{1,0:T(8,128)S(1)}, u32[]{:S(2)}, u32[]{:S(2)}) %collective-permute-start.32) | collective-permute-done | bytes 10272 | tf_op jit(solution)/shard_map/ppermute | solution.py:699
  178.8 2.7 %collect.1 = (bf16[2048,512]{1,0:T(8,128)(2,1)}, bf16[2048,512]{1,0:T(8,128)(2,1)}) custom-call(s32[4]{0:T(128)S(1)} %copy-done.1, bf16[1024,512]{1,0:T(8,128)(2,1)S(1)} %add_convert_fusion.m0, bf16[1024,512]{1,0:T(8,128)(2,1)S(1)} %collective-permute-done.27.m1, bf16[512,512]{1,0:T(8,128)(2,1)S(1)} %copy-done, ...), custom_call_target="tpu_custom_call" | custom-call | flops 3300000000 | bytes 1024 | tf_op jit(solution)/shard_map/collect/pallas_call | solution.py:684
  181.5 2.4 %collective-permute-done.26 = bf16[320,512]{1,0:T(8,128)(2,1)S(1)} collective-permute-done((bf16[320,512]{1,0:T(8,128)(2,1)S(1)}, bf16[320,512]{1,0:T(8,128)(2,1)S(1)}, u32[]{:S(2)}, u32[]{:S(2)}) %collective-permute-start.26) | collective-permute-done | bytes 327712 | tf_op jit(solution)/shard_map/ppermute | solution.py:699
  184.2 1.0 fusion.7
  185.2 0.7 slice.140
  (132 shorter events, 9.4 us)
Async XLA Ops:
  0.7 22.0 %collective-permute-start = (bf16[128,512]{1,0:T(8,128)(2,1)}, bf16[128,512]{1,0:T(8,128)(2,1)S(1)}, u32[]{:S(2)}, u32[]{:S(2)}) collective-permute-start(bf16[128,512]{1,0:T(8,128)(2,1)} %w0.1), channel_id=1, source_target_pairs={{0,1},{1,0},{2,3},{3,2},{4,5},{5,4},{6,7},{7,6},{8,9},{9,8},{10,11... | collective-permute-start | bytes 393224 | tf_op jit(solution)/shard_map/ppermute | solution.py:699
  1.2 21.5 %collective-permute-start.1 = (bf16[128,512]{1,0:T(8,128)(2,1)}, bf16[128,512]{1,0:T(8,128)(2,1)S(1)}, u32[]{:S(2)}, u32[]{:S(2)}) collective-permute-start(bf16[128,512]{1,0:T(8,128)(2,1)} %w0.1), channel_id=1, source_target_pairs={{0,2},{1,3},{2,0},{3,1},{4,6},{5,7},{6,4},{7,5},{8,10},{9,11},{10,... | collective-permute-start | bytes 393224 | tf_op jit(solution)/shard_map/ppermute | solution.py:699
  3.8 18.9 %collective-permute-start.2 = (bf16[128,512]{1,0:T(8,128)(2,1)}, bf16[128,512]{1,0:T(8,128)(2,1)S(1)}, u32[]{:S(2)}, u32[]{:S(2)}) collective-permute-start(bf16[128,512]{1,0:T(8,128)(2,1)} %w0.1), channel_id=1, source_target_pairs={{0,3},{1,2},{2,1},{3,0},{4,7},{5,6},{6,5},{7,4},{8,11},{9,10},{10,... | collective-permute-start | bytes 393224 | tf_op jit(solution)/shard_map/ppermute | solution.py:699
  3.8 18.8 %collective-permute-start.3 = (f32[1,512]{1,0:T(1,128)}, f32[1,512]{1,0:T(1,128)S(1)}, u32[]{:S(2)}, u32[]{:S(2)}) collective-permute-start(f32[1,512]{1,0:T(1,128)} %bitcast.74), channel_id=1, source_target_pairs={{0,1},{1,0},{2,3},{3,2},{4,5},{5,4},{6,7},{7,6},{8,9},{9,8},{10,11... | collective-permute-start | bytes 6152 | tf_op jit(solution)/shard_map/ppermute | solution.py:699
  4.6 18.8 %copy-start.11 = (bf16[512,512]{1,0:T(8,128)(2,1)S(1)}, bf16[512,512]{1,0:T(8,128)(2,1)}, u32[]{:S(2)}) copy-start(bf16[512,512]{1,0:T(8,128)(2,1)} %i0.1) | copy-start | bytes 1572868
  4.6 19.2 %copy-start.12 = (bf16[512,512]{1,0:T(8,128)(2,1)S(1)}, bf16[512,512]{1,0:T(8,128)(2,1)}, u32[]{:S(2)}) copy-start(bf16[512,512]{1,0:T(8,128)(2,1)} %u0.1) | copy-start | bytes 1572868
  22.7 15.9 %copy-start.25 = (f32[1,512]{1,0:T(1,128)}, f32[1,512]{1,0:T(1,128)S(1)}, u32[]{:S(2)}) copy-start(f32[1,512]{1,0:T(1,128)S(1)} %collective-permute-done.3.b1) | copy-start | bytes 6148
  22.7 15.9 %copy-start.19 = (bf16[128,512]{1,0:T(8,128)(2,1)}, bf16[128,512]{1,0:T(8,128)(2,1)S(1)}, u32[]{:S(2)}) copy-start(bf16[128,512]{1,0:T(8,128)(2,1)S(1)} %collective-permute-done.w1) | copy-start | bytes 393220
  23.4 15.1 %collective-permute-start.7 = (bf16[512,512]{1,0:T(8,128)(2,1)S(1)}, bf16[512,512]{1,0:T(8,128)(2,1)S(1)}, u32[]{:S(2)}, u32[]{:S(2)}) collective-permute-start(bf16[512,512]{1,0:T(8,128)(2,1)S(1)} %copy-done.11), channel_id=1, source_target_pairs={{0,1},{1,0},{2,3},{3,2},{4,5},{5,4},{6,7},{7,6},{8,9},{9,8},{10,11... | collective-permute-start | bytes 1572872 | tf_op jit(solution)/shard_map/ppermute | solution.py:699
  23.8 14.7 %collective-permute-start.8 = (bf16[512,512]{1,0:T(8,128)(2,1)S(1)}, bf16[512,512]{1,0:T(8,128)(2,1)S(1)}, u32[]{:S(2)}, u32[]{:S(2)}) collective-permute-start(bf16[512,512]{1,0:T(8,128)(2,1)S(1)} %copy-done.12), channel_id=1, source_target_pairs={{0,1},{1,0},{2,3},{3,2},{4,5},{5,4},{6,7},{7,6},{8,9},{9,8},{10,11... | collective-permute-start | bytes 1572872 | tf_op jit(solution)/shard_map/ppermute | solution.py:699
  24.0 2.8 %collective-permute-start.4 = (bf16[1024,128]{1,0:T(8,128)(2,1)S(1)}, bf16[1024,128]{1,0:T(8,128)(2,1)S(1)}, u32[]{:S(2)}, u32[]{:S(2)}) collective-permute-start(bf16[1024,128]{1,0:T(8,128)(2,1)S(1)} %bitcast.58), channel_id=1, source_target_pairs={{0,1},{1,0},{2,3},{3,2},{4,5},{5,4},{6,7},{7,6},{8,9},{9,8},{10,11... | collective-permute-start | bytes 786440 | tf_op jit(solution)/shard_map/ppermute | solution.py:699
  24.3 8.3 %collective-permute-start.6 = (bf16[1024,128]{1,0:T(8,128)(2,1)S(1)}, bf16[1024,128]{1,0:T(8,128)(2,1)S(1)}, u32[]{:S(2)}, u32[]{:S(2)}) collective-permute-start(bf16[1024,128]{1,0:T(8,128)(2,1)S(1)} %bitcast.59), channel_id=1, source_target_pairs={{0,3},{1,2},{2,1},{3,0},{4,7},{5,6},{6,5},{7,4},{8,11},{9,10},{10,... | collective-permute-start | bytes 786440 | tf_op jit(solution)/shard_map/ppermute | solution.py:699
  26.0 12.5 %collective-permute-start.5 = (bf16[1024,128]{1,0:T(8,128)(2,1)S(1)}, bf16[1024,128]{1,0:T(8,128)(2,1)S(1)}, u32[]{:S(2)}, u32[]{:S(2)}) collective-permute-start(bf16[1024,128]{1,0:T(8,128)(2,1)S(1)} %bitcast.57), channel_id=1, source_target_pairs={{0,2},{1,3},{2,0},{3,1},{4,6},{5,7},{6,4},{7,5},{8,10},{9,11},{10,... | collective-permute-start | bytes 786440 | tf_op jit(solution)/shard_map/ppermute | solution.py:699
  26.7 11.9 %copy-start.16 = (bf16[1024,128]{1,0:T(8,128)(2,1)}, bf16[1024,128]{1,0:T(8,128)(2,1)S(1)}, u32[]{:S(2)}) copy-start(bf16[1024,128]{1,0:T(8,128)(2,1)S(1)} %collective-permute-done.4.a1) | copy-start | bytes 786436
  55.2 2.9 %collective-permute-start.18 = (bf16[8,128,512]{2,1,0:T(8,128)(2,1)}, bf16[8,128,512]{2,1,0:T(8,128)(2,1)S(1)}, u32[]{:S(2)}, u32[]{:S(2)}) collective-permute-start(bf16[8,128,512]{2,1,0:T(8,128)(2,1)} %get-tuple-element.127), channel_id=1, source_target_pairs={{0,1},{1,0},{2,3},{3,2},{4,5},{5,4},{6,7},{7,6},{8,9},{9,8},{10,11... | collective-permute-start | bytes 3145736 | tf_op jit(solution)/shard_map/ppermute | solution.py:699
  55.2 18.0 %collective-permute-start.9 = (bf16[512,512]{1,0:T(8,128)(2,1)}, bf16[512,512]{1,0:T(8,128)(2,1)S(1)}, u32[]{:S(2)}, u32[]{:S(2)}) collective-permute-start(bf16[512,512]{1,0:T(8,128)(2,1)} %get-tuple-element.96), channel_id=1, source_target_pairs={{0,2},{1,3},{2,0},{3,1},{4,6},{5,7},{6,4},{7,5},{8,10},{9,11},{10,... | collective-permute-start | bytes 1572872 | tf_op jit(solution)/shard_map/ppermute | solution.py:699
  60.6 54.8 %all-to-all-start = ((bf16[8,128,512]{2,1,0:T(8,128)(2,1)}), bf16[8,128,512]{2,1,0:T(8,128)(2,1)S(1)}, u32[]{:S(2)}, u32[]{:S(2)}) async-start(bf16[8,128,512]{2,1,0:T(8,128)(2,1)} %add_convert_fusion.1), calls=%async_computation | async-start | bytes 2097152 | tf_op jit(solution)/shard_map/all_to_all | solution.py:728
  74.0 7.2 %copy-start.4 = (bf16[1024,512]{1,0:T(8,128)(2,1)S(1)}, bf16[1024,512]{1,0:T(8,128)(2,1)}, u32[]{:S(2)}) copy-start(bf16[1024,512]{1,0:T(8,128)(2,1)} %get-tuple-element.125) | copy-start | bytes 3145732
  79.2 2.0 %collective-permute-start.10 = (bf16[512,128]{1,0:T(8,128)(2,1)}, bf16[512,128]{1,0:T(8,128)(2,1)S(1)}, u32[]{:S(2)}, u32[]{:S(2)}) collective-permute-start(bf16[512,128]{1,0:T(8,128)(2,1)} %get-tuple-element.99), channel_id=1, source_target_pairs={{0,1},{1,0},{2,3},{3,2},{4,5},{5,4},{6,7},{7,6},{8,9},{9,8},{10,11... | collective-permute-start | bytes 393224 | tf_op jit(solution)/shard_map/ppermute | solution.py:699
  79.2 3.5 %collective-permute-start.13 = (f32[1,512]{1,0:T(1,128)S(1)}, f32[1,512]{1,0:T(1,128)S(1)}, u32[]{:S(2)}, u32[]{:S(2)}) collective-permute-start(f32[1,512]{1,0:T(1,128)S(1)} %slice.94), channel_id=1, source_target_pairs={{0,1},{1,0},{2,3},{3,2},{4,5},{5,4},{6,7},{7,6},{8,9},{9,8},{10,11... | collective-permute-start | bytes 6152 | tf_op jit(solution)/shard_map/ppermute | solution.py:699
  79.7 6.6 %collective-permute-start.11 = (bf16[512,128]{1,0:T(8,128)(2,1)}, bf16[512,128]{1,0:T(8,128)(2,1)S(1)}, u32[]{:S(2)}, u32[]{:S(2)}) collective-permute-start(bf16[512,128]{1,0:T(8,128)(2,1)} %get-tuple-element.100), channel_id=1, source_target_pairs={{0,2},{1,3},{2,0},{3,1},{4,6},{5,7},{6,4},{7,5},{8,10},{9,11},{10,... | collective-permute-start | bytes 393224 | tf_op jit(solution)/shard_map/ppermute | solution.py:699
  81.2 7.0 %collective-permute-start.12 = (bf16[512,128]{1,0:T(8,128)(2,1)}, bf16[512,128]{1,0:T(8,128)(2,1)S(1)}, u32[]{:S(2)}, u32[]{:S(2)}) collective-permute-start(bf16[512,128]{1,0:T(8,128)(2,1)} %get-tuple-element.101), channel_id=1, source_target_pairs={{0,3},{1,2},{2,1},{3,0},{4,7},{5,6},{6,5},{7,4},{8,11},{9,10},{10,... | collective-permute-start | bytes 393224 | tf_op jit(solution)/shard_map/ppermute | solution.py:699
  81.2 7.0 %copy-start.22 = (bf16[512,128]{1,0:T(8,128)(2,1)}, bf16[512,128]{1,0:T(8,128)(2,1)S(1)}, u32[]{:S(2)}) copy-start(bf16[512,128]{1,0:T(8,128)(2,1)S(1)} %collective-permute-done.10.d1) | copy-start | bytes 393220
  81.3 34.2 %collective-permute-start.17 = (bf16[1024,512]{1,0:T(8,128)(2,1)S(1)}, bf16[1024,512]{1,0:T(8,128)(2,1)}, u32[]{:S(2)}, u32[]{:S(2)}) collective-permute-start(bf16[1024,512]{1,0:T(8,128)(2,1)S(1)} %copy-done.4), channel_id=1, source_target_pairs={{0,2},{1,3},{2,0},{3,1},{4,6},{5,7},{6,4},{7,5},{8,10},{9,11},{10,... | collective-permute-start | bytes 3145736 | tf_op jit(solution)/shard_map/ppermute | solution.py:699
  84.0 27.0 %collective-permute-start.14 = (bf16[128,512]{1,0:T(8,128)(2,1)}, bf16[128,512]{1,0:T(8,128)(2,1)S(1)}, u32[]{:S(2)}, u32[]{:S(2)}) collective-permute-start(bf16[128,512]{1,0:T(8,128)(2,1)} %get-tuple-element.121), channel_id=1, source_target_pairs={{0,1},{1,0},{2,3},{3,2},{4,5},{5,4},{6,7},{7,6},{8,9},{9,8},{10,11... | collective-permute-start | bytes 393224 | tf_op jit(solution)/shard_map/ppermute | solution.py:699
  84.5 29.9 %collective-permute-start.15 = (bf16[128,512]{1,0:T(8,128)(2,1)}, bf16[128,512]{1,0:T(8,128)(2,1)S(1)}, u32[]{:S(2)}, u32[]{:S(2)}) collective-permute-start(bf16[128,512]{1,0:T(8,128)(2,1)} %get-tuple-element.122), channel_id=1, source_target_pairs={{0,2},{1,3},{2,0},{3,1},{4,6},{5,7},{6,4},{7,5},{8,10},{9,11},{10,... | collective-permute-start | bytes 393224 | tf_op jit(solution)/shard_map/ppermute | solution.py:699
  86.3 29.2 %collective-permute-start.16 = (bf16[128,512]{1,0:T(8,128)(2,1)}, bf16[128,512]{1,0:T(8,128)(2,1)S(1)}, u32[]{:S(2)}, u32[]{:S(2)}) collective-permute-start(bf16[128,512]{1,0:T(8,128)(2,1)} %get-tuple-element.123), channel_id=1, source_target_pairs={{0,3},{1,2},{2,1},{3,0},{4,7},{5,6},{6,5},{7,4},{8,11},{9,10},{10,... | collective-permute-start | bytes 393224 | tf_op jit(solution)/shard_map/ppermute | solution.py:699
  111.1 8.1 %copy-start.2 = (bf16[1024,512]{1,0:T(8,128)(2,1)S(1)}, bf16[1024,512]{1,0:T(8,128)(2,1)}, u32[]{:S(2)}) copy-start(bf16[1024,512]{1,0:T(8,128)(2,1)} %get-tuple-element.134.keep0.keep1) | copy-start | bytes 3145732
  115.5 3.7 %collective-permute-start.20 = (bf16[1024,512]{1,0:T(8,128)(2,1)}, bf16[1024,512]{1,0:T(8,128)(2,1)S(1)}, u32[]{:S(2)}, u32[]{:S(2)}) collective-permute-start(bf16[1024,512]{1,0:T(8,128)(2,1)} %get-tuple-element.135), channel_id=1, source_target_pairs={{0,1},{1,0},{2,3},{3,2},{4,5},{5,4},{6,7},{7,6},{8,9},{9,8},{10,11... | collective-permute-start | bytes 3145736 | tf_op jit(solution)/shard_map/ppermute | solution.py:699
  119.1 16.4 %copy-start.3 = (bf16[1024,512]{1,0:T(8,128)(2,1)}, bf16[1024,512]{1,0:T(8,128)(2,1)S(1)}, u32[]{:S(2)}) copy-start(bf16[1024,512]{1,0:T(8,128)(2,1)S(1)} %collective-permute-done.20.near0.near1) | copy-start | bytes 3145732
  120.3 15.2 %collective-permute-start.33 = (bf16[128,512]{1,0:T(8,128)(2,1)S(1)}, bf16[128,512]{1,0:T(8,128)(2,1)S(1)}, u32[]{:S(2)}, u32[]{:S(2)}) collective-permute-start(bf16[128,512]{1,0:T(8,128)(2,1)S(1)} %reduce_sum.12), channel_id=1, source_target_pairs={{0,16},{4,20},{8,24},{12,28},{16,0},{20,4},{24,8},{28,12},{1,17},{... | collective-permute-start | bytes 393224 | tf_op jit(solution)/shard_map/ppermute | solution.py:699
  128.5 15.4 %collective-permute-start.19 = (bf16[336,512]{1,0:T(8,128)(2,1)}, bf16[336,512]{1,0:T(8,128)(2,1)S(1)}, u32[]{:S(2)}, u32[]{:S(2)}) collective-permute-start(bf16[336,512]{1,0:T(8,128)(2,1)} %add_convert_fusion.3), channel_id=1, source_target_pairs={{0,4},{4,0},{8,12},{12,8},{16,20},{20,16},{24,28},{28,24},{1,5},{5... | collective-permute-start | bytes 1032200 | tf_op jit(solution)/shard_map/ppermute | solution.py:699
  128.5 15.4 %collective-permute-start.21 = (bf16[512,512]{1,0:T(8,128)(2,1)}, bf16[512,512]{1,0:T(8,128)(2,1)S(1)}, u32[]{:S(2)}, u32[]{:S(2)}) collective-permute-start(bf16[512,512]{1,0:T(8,128)(2,1)} %bitcast.56), channel_id=1, source_target_pairs={{0,2},{1,3},{2,0},{3,1},{4,6},{5,7},{6,4},{7,5},{8,10},{9,11},{10,... | collective-permute-start | bytes 1572872 | tf_op jit(solution)/shard_map/ppermute | solution.py:699
  135.6 8.4 %copy-start.9 = (bf16[16,512]{1,0:T(8,128)(2,1)S(1)}, bf16[16,512]{1,0:T(8,128)(2,1)}, u32[]{:S(2)}) copy-start(bf16[16,512]{1,0:T(8,128)(2,1)} %get-tuple-element.137) | copy-start | bytes 49156
  135.6 8.4 %copy-start.6 = (bf16[320,512]{1,0:T(8,128)(2,1)S(1)}, bf16[320,512]{1,0:T(8,128)(2,1)}, u32[]{:S(2)}) copy-start(bf16[320,512]{1,0:T(8,128)(2,1)} %get-tuple-element.128) | copy-start | bytes 983044
  135.6 8.3 %collective-permute-start.34 = (bf16[256,512]{1,0:T(8,128)(2,1)S(1)}, bf16[256,512]{1,0:T(8,128)(2,1)S(1)}, u32[]{:S(2)}, u32[]{:S(2)}) collective-permute-start(bf16[256,512]{1,0:T(8,128)(2,1)S(1)} %pad_maximum_fusion.3), channel_id=1, source_target_pairs={{0,8},{4,12},{8,0},{12,4},{16,24},{20,28},{24,16},{28,20},{1,9},{5... | collective-permute-start | bytes 786440 | tf_op jit(solution)/shard_map/ppermute | solution.py:699
  138.3 40.5 %collective-permute-start.27 = (bf16[1024,512]{1,0:T(8,128)(2,1)S(1)}, bf16[1024,512]{1,0:T(8,128)(2,1)S(1)}, u32[]{:S(2)}, u32[]{:S(2)}) collective-permute-start(bf16[1024,512]{1,0:T(8,128)(2,1)S(1)} %add_convert_fusion.m0), channel_id=1, source_target_pairs={{0,1},{1,0},{2,3},{3,2},{4,5},{5,4},{6,7},{7,6},{8,9},{9,8},{10,11... | collective-permute-start | bytes 3145736 | tf_op jit(solution)/shard_map/ppermute | solution.py:699
  144.2 6.0 %collective-permute-start.22 = (bf16[176,512]{1,0:T(8,128)(2,1)S(1)}, bf16[176,512]{1,0:T(8,128)(2,1)S(1)}, u32[]{:S(2)}, u32[]{:S(2)}) collective-permute-start(bf16[176,512]{1,0:T(8,128)(2,1)S(1)} %pad_maximum_fusion.4), channel_id=1, source_target_pairs={{0,8},{4,12},{8,0},{12,4},{16,24},{20,28},{24,16},{28,20},{1,9},{5... | collective-permute-start | bytes 540680 | tf_op jit(solution)/shard_map/ppermute | solution.py:699
  146.4 19.8 %collective-permute-start.35 = (bf16[512,512]{1,0:T(8,128)(2,1)S(1)}, bf16[512,512]{1,0:T(8,128)(2,1)S(1)}, u32[]{:S(2)}, u32[]{:S(2)}) collective-permute-start(bf16[512,512]{1,0:T(8,128)(2,1)S(1)} %pad_maximum_fusion.1), channel_id=1, source_target_pairs={{0,4},{4,0},{8,12},{12,8},{16,20},{20,16},{24,28},{28,24},{1,5},{5... | collective-permute-start | bytes 1572872 | tf_op jit(solution)/shard_map/ppermute | solution.py:699
  150.3 8.1 %collective-permute-start.23 = (bf16[96,512]{1,0:T(8,128)(2,1)S(1)}, bf16[96,512]{1,0:T(8,128)(2,1)S(1)}, u32[]{:S(2)}, u32[]{:S(2)}) collective-permute-start(bf16[96,512]{1,0:T(8,128)(2,1)S(1)} %pad_maximum_fusion.6), channel_id=1, source_target_pairs={{0,16},{4,20},{8,24},{12,28},{16,0},{20,4},{24,8},{28,12},{1,17},{... | collective-permute-start | bytes 294920 | tf_op jit(solution)/shard_map/ppermute | solution.py:699
  156.9 16.9 %collective-permute-start.29 = (bf16[512,512]{1,0:T(8,128)(2,1)}, bf16[512,512]{1,0:T(8,128)(2,1)S(1)}, u32[]{:S(2)}, u32[]{:S(2)}) collective-permute-start(bf16[512,512]{1,0:T(8,128)(2,1)} %close.1.g0), channel_id=1, source_target_pairs={{0,2},{1,3},{2,0},{3,1},{4,6},{5,7},{6,4},{7,5},{8,10},{9,11},{10,... | collective-permute-start | bytes 1572872 | tf_op jit(solution)/shard_map/ppermute | solution.py:699
  158.4 20.4 %collective-permute-start.28 = (bf16[512,512]{1,0:T(8,128)(2,1)}, bf16[512,512]{1,0:T(8,128)(2,1)S(1)}, u32[]{:S(2)}, u32[]{:S(2)}) collective-permute-start(bf16[512,512]{1,0:T(8,128)(2,1)} %close.1.g0), channel_id=1, source_target_pairs={{0,1},{1,0},{2,3},{3,2},{4,5},{5,4},{6,7},{7,6},{8,9},{9,8},{10,11... | collective-permute-start | bytes 1572872 | tf_op jit(solution)/shard_map/ppermute | solution.py:699
  158.5 7.6 %collective-permute-start.24 = (bf16[80,512]{1,0:T(8,128)(2,1)S(1)}, bf16[80,512]{1,0:T(8,128)(2,1)S(1)}, u32[]{:S(2)}, u32[]{:S(2)}) collective-permute-start(bf16[80,512]{1,0:T(8,128)(2,1)S(1)} %fusion.2), channel_id=1, source_target_pairs={{0,16},{4,20},{8,24},{12,28},{16,0},{20,4},{24,8},{28,12},{1,17},{... | collective-permute-start | bytes 245768 | tf_op jit(solution)/shard_map/ppermute | solution.py:699
  166.1 5.9 %collective-permute-start.25 = (bf16[160,512]{1,0:T(8,128)(2,1)S(1)}, bf16[160,512]{1,0:T(8,128)(2,1)S(1)}, u32[]{:S(2)}, u32[]{:S(2)}) collective-permute-start(bf16[160,512]{1,0:T(8,128)(2,1)S(1)} %pad_maximum_fusion.5), channel_id=1, source_target_pairs={{0,8},{4,12},{8,0},{12,4},{16,24},{20,28},{24,16},{28,20},{1,9},{5... | collective-permute-start | bytes 491528 | tf_op jit(solution)/shard_map/ppermute | solution.py:699
  172.1 2.3 %collective-permute-start.31 = (f32[5,512]{1,0:T(8,128)S(1)}, f32[5,512]{1,0:T(8,128)S(1)}, u32[]{:S(2)}, u32[]{:S(2)}) collective-permute-start(f32[5,512]{1,0:T(8,128)S(1)} %slice.131), channel_id=1, source_target_pairs={{0,1},{1,0},{2,3},{3,2},{4,5},{5,4},{6,7},{7,6},{8,9},{9,8},{10,11... | collective-permute-start | bytes 30728 | tf_op jit(solution)/shard_map/ppermute | solution.py:699
  173.8 10.1 %collective-permute-start.26 = (bf16[320,512]{1,0:T(8,128)(2,1)S(1)}, bf16[320,512]{1,0:T(8,128)(2,1)S(1)}, u32[]{:S(2)}, u32[]{:S(2)}) collective-permute-start(bf16[320,512]{1,0:T(8,128)(2,1)S(1)} %pad_maximum_fusion.2), channel_id=1, source_target_pairs={{0,4},{4,0},{8,12},{12,8},{16,20},{20,16},{24,28},{28,24},{1,5},{5... | collective-permute-start | bytes 983048 | tf_op jit(solution)/shard_map/ppermute | solution.py:699
  173.8 5.0 %collective-permute-start.30 = (bf16[512,512]{1,0:T(8,128)(2,1)S(1)}, bf16[512,512]{1,0:T(8,128)(2,1)S(1)}, u32[]{:S(2)}, u32[]{:S(2)}) collective-permute-start(bf16[512,512]{1,0:T(8,128)(2,1)S(1)} %collective-permute-done.29.g2), channel_id=1, source_target_pairs={{0,1},{1,0},{2,3},{3,2},{4,5},{5,4},{6,7},{7,6},{8,9},{9,8},{10,11... | collective-permute-start | bytes 1572872 | tf_op jit(solution)/shard_map/ppermute | solution.py:699
  174.3 3.8 %collective-permute-start.32 = (f32[5,512]{1,0:T(8,128)S(1)}, f32[5,512]{1,0:T(8,128)S(1)}, u32[]{:S(2)}, u32[]{:S(2)}) collective-permute-start(f32[5,512]{1,0:T(8,128)S(1)} %slice_add_fusion.7), channel_id=1, source_target_pairs={{0,2},{1,3},{2,0},{3,1},{4,6},{5,7},{6,4},{7,5},{8,10},{9,11},{10,... | collective-permute-start | bytes 30728 | tf_op jit(solution)/shard_map/ppermute | solution.py:699
  (15 other events, 36.8 us)

commit v4 on v3

--- a/solution.py
+++ b/solution.py
@@ -38,7 +38,7 @@
     return pl.BlockSpec(shape, lambda *ids: (0,) * len(shape))
 
 
-def params(mib=60):
+def params(mib=57):
     return pltpu.CompilerParams(
         vmem_limit_bytes=mib * 2**20, dimension_semantics=("arbitrary",)
     )
@@ -70,7 +70,7 @@
 def forward_body(
     block, half_rows,
     kind, tokens, gain, shift, wq, wk, wv, cbias, pbias, wp, st, ct, table,
-    normed_out, qc_out, qp_out, v_out, kt_out, p_out, ot_out, att_out, linv_out,
+    normed_out, qc_out, qp_out, v_out, kt_out, p_out, ot_out, near_out, far_out, linv_out,
     pbuf, puts, sems, wcat, kcat, vt, qa, s_scr, m_scr, l_scr, acc,
 ):
     ib = pl.program_id(0)
@@ -142,9 +142,9 @@
     m_scr[...] = jnp.broadcast_to(jnp.max(m_scr[...], axis=0, keepdims=True), m_scr.shape)
 
     done = puts[0]
-    slot = done & 1
-
-    @pl.when(done >= 2)
+    slot = done & 3
+
+    @pl.when(done >= 4)
     def free():
         put(ib, ib, slot).wait()
 
@@ -165,9 +165,9 @@
     put(ib, ib, slot).start()
 
     def prob_loop(c, done):
-        slot = done & 1
-
-        @pl.when(done >= 2)
+        slot = done & 3
+
+        @pl.when(done >= 4)
         def free():
             put(ib, c, slot).wait()
 
@@ -190,11 +190,14 @@
         axis=0,
     )
     ot_out[...] = attended
-    att_out[...] = attended.T.astype(bf16)
+    rows = attended.T.astype(bf16)
+    even = (lax.axis_index("mp") & 1) == 0
+    near_out[...] = jnp.where(even, rows[mid:], rows[:mid])
+    far_out[...] = jnp.where(even, rows[:mid], rows[mid:])
 
     @pl.when(ib == pl.num_programs(0) - 1)
     def finish():
-        for slot in range(2):
+        for slot in range(4):
             put(ib, ib, slot).wait()
 
 
@@ -219,19 +222,20 @@
         out_specs=[
             row(block, width), row(block, cols), row(block, cols), row(block, cols),
             col(cols, block), pl.BlockSpec(memory_space=pl.ANY), col(cols, block),
-            row(block, cols), col(1, 2 * block),
+            row(block // 2, cols), row(block // 2, cols), col(1, 2 * block),
         ],
         out_shape=[
             shape((length, width), bf16),
             shape((length, cols), bf16), shape((length, cols), bf16), shape((length, cols), bf16),
             shape((cols, length), bf16),
             shape((length, 2 * length), bf16), shape((cols, length), f32),
-            shape((length, cols), bf16), shape((1, 2 * length), f32),
+            shape((length // 2, cols), bf16), shape((length // 2, cols), bf16),
+            shape((1, 2 * length), f32),
         ],
         scratch_shapes=[
-            pltpu.VMEM((2, block, 2 * block), bf16),
+            pltpu.VMEM((4, block, 2 * block), bf16),
             pltpu.SMEM((1,), jnp.int32),
-            pltpu.SemaphoreType.DMA((2,)),
+            pltpu.SemaphoreType.DMA((4,)),
             pltpu.VMEM((width, 3 * cols), bf16),
             pltpu.VMEM((length, width + cols), bf16),
             pltpu.VMEM((cols, length), bf16),
@@ -460,8 +464,7 @@
     def rows():
         c = cot[...].reshape(2 * own, width)
         residual = tokens[...].reshape(2 * own, width).astype(f32)
-        residual = residual + dot(own_att[...].reshape(2 * own, own_att.shape[-1]), w0[...])
-        for att, wo in ((a1, w1), (a2, w2), (a3, w3)):
+        for att, wo in ((own_att, w0), (a1, w1), (a2, w2), (a3, w3)):
             residual = residual + dot(att[...], wo[...])
         normed, _ = norm_parts(residual)
         hidden = (normed * gain[...] + shift[...]).astype(bf16)
@@ -534,8 +537,8 @@
         grid_spec=pltpu.PrefetchScalarGridSpec(
             num_scalar_prefetch=1,
             grid=(3,),
-            in_specs=[mine(width), mine(width), mine(cols)]
-            + [step(cols)] * 3
+            in_specs=[mine(width), mine(width)]
+            + [step(cols)] * 4
             + [spec(o.shape) for o in others],
             out_specs=[
                 half, half, step(width), half, spec((2, share)), spec(grad_shape),
@@ -556,7 +559,7 @@
         compiler_params=params(),
         cost_estimate=cost(13),
         name="feed",
-    )(place, split(tokens), split(cot), split(own_att), *atts, *others)
+    )(place, split(tokens), split(cot), own_att, *atts, *others)
 
 
 def turn_body(
@@ -600,8 +603,8 @@
             num_scalar_prefetch=1,
             grid=(1,),
             in_specs=[spec(keep.shape)] * 3
-            + [mine(width), mine(cols)]
-            + [half(cols)] * 3
+            + [mine(width)]
+            + [half(cols)] * 4
             + [spec(w.shape) for w in wos]
             + [spec(gain.shape)],
             out_specs=[spec(s) for s, _ in shapes],
@@ -836,19 +839,17 @@
     wos = [output_weight] + [swap(output_weight, "mp", n) for n in (1, 2, 3)]
     bis = [inner_bias[None], swap(inner_bias[None], "mp", 1)]
     projections = (query_weight, key_weight, value_weight)
-    normed, qc, qp, v, kt, p, ot, attended, linv = attention_forward(
+    normed, qc, qp, v, kt, p, ot, near, far, linv = attention_forward(
         item_kind, tokens, gain1, shift1, *projections, content_bias[None], position_bias[None],
         position_weight, st, ct, table, block,
     )
-    blocks = attended.reshape(4, 2, own, cols)
-    pick = lambda c: lax.dynamic_index_in_dim(blocks, c, 1, False).reshape(4 * own, cols)
-    near, far = pick(1 - core), pick(core)
     near, far, wi, wu, wos, bis = tie((near, far, inner_weight, outer_weight, wos, bis))
     wis = [inner_weight, swap(wi, "mp", 1)]
     wus = [outer_weight, swap(wu, "mp", 1)]
     atts = [swap(near, "mp", 1), swap(far, "mp", 2), swap(near, "mp", 3)]
+    attended = far
     back_keep, back_send, out, residual, bias, near, keep = feed(
-        place, tokens, cotangent, attended, atts, wos, wis, wus, bis, bu, gain2, shift2
+        place, tokens, cotangent, far, atts, wos, wis, wus, bis, bu, gain2, shift2
     )
     back_got = swap(back_send, "mp", 2)
     near_got = swap(near, "mp", 1)

time: 185 us -> 183 us (0.989)
  waiting for transfers between devices: 51.7 us -> 43.4 us
  starting transfers between devices: 44.4 us -> 50.3 us
    ppermute x36, waiting for transfers between devices: 51.7 us -> 43.4 us  [swap(): return lax.ppermute(value, axis, [(i, i ^ mask) for i in range(size)])]
    ppermute x36, starting transfers between devices: 31.8 us -> 38.5 us  [swap(): return lax.ppermute(value, axis, [(i, i ^ mask) for i in range(size)])]
  transfers between devices with their start and end apart: 37 -> 37, of which waited for: 14 -> 14; matrix products, arithmetic and copies ran while one was open for 8% -> 8% of each run, Pallas kernels for 27% -> 28%
where the time goes in v4:
time: 183 us; the launch traced here: 182 us
  Pallas kernels  66.4 us (36%)
  starting transfers between devices  50.3 us (27%)
  waiting for transfers between devices  43.4 us (24%)
  other arithmetic  11.9 us (7%)
  local copies, waits for them, and re-layouts  8.31 us (5%)
  between operations  1.87 us (1%)
    ppermute x36, waiting for transfers between devices, swap(): return lax.ppermute(value, axis, [(i, i ^ mask) for i in range(size)])  43.4 us
    ppermute x36, starting transfers between devices, swap(): return lax.ppermute(value, axis, [(i, i ^ mask) for i in range(size)])  38.5 us
    pallas_call x1, Pallas kernels, attention_backward(): pl.pallas_call(functools.partial(backward_body, count, block, length // 2...  22.2 us
    pallas_call x1, Pallas kernels, attention_forward(): pl.pallas_call(functools.partial(forward_body, block, length // 2), grid=...  16.9 us
    pallas_call x1, Pallas kernels, feed(): pl.pallas_call(feed_body, grid_spec=pltpu.PrefetchScalarGridSpec(num_scal...  15.6 us
    all_to_all x1, starting transfers between devices, exchange(): lax.all_to_all(value, 'dp', split_axis=0, concat_axis=0, tiled=True, axis...  11.7 us
    pallas_call x1, Pallas kernels, turn(): pl.pallas_call(turn_body, grid_spec=pltpu.PrefetchScalarGridSpec(num_scal...  5.13 us
    pallas_call x1, Pallas kernels, close(): pl.pallas_call(close_body, grid_spec=pltpu.PrefetchScalarGridSpec(num_sca...  3.95 us
  transfers between devices with their start and end apart: 37, of which 14 were waited for; matrix products, arithmetic and copies ran while one was open for 8% of the time, Pallas kernels for 28%

profile of v4, /device:TPU:0, one launch (start us, length us, event | category | flops | bytes accessed | tf_op | source)
XLA Modules:
  0.0 182.1 jit_solution(11408536583414262925)
XLA Ops:
  1.2 2.6 %collective-permute-start.1 = (bf16[128,512]{1,0:T(8,128)(2,1)}, bf16[128,512]{1,0:T(8,128)(2,1)S(1)}, u32[]{:S(2)}, u32[]{:S(2)}) collective-permute-start(bf16[128,512]{1,0:T(8,128)(2,1)} %w0.1), channel_id=1, source_target_pairs={{0,2},{1,3},{2,0},{3,1},{4,6},{5,7},{6,4},{7,5},{8,10},{9,11},{10,... | collective-permute-start | bytes 393224 | tf_op jit(solution)/shard_map/ppermute | solution.py:702
  4.7 16.9 %attention_forward.1 = (bf16[2048,512]{1,0:T(8,128)(2,1)}, bf16[2048,128]{1,0:T(8,128)(2,1)}, bf16[2048,128]{1,0:T(8,128)(2,1)}, bf16[2048,128]{1,0:T(8,128)(2,1...) custom-call(s32[1]{0:T(128)S(6)} %copy.48.kind, ...), custom_call_target="tpu_custom_call" | custom-call | flops 27499999232 | bytes 1024 | tf_op jit(solution)/shard_map/attention_forward/pallas_call | solution.py:213
  22.3 1.9 %collective-permute-start.5 = (bf16[1024,128]{1,0:T(8,128)(2,1)}, bf16[1024,128]{1,0:T(8,128)(2,1)S(1)}, u32[]{:S(2)}, u32[]{:S(2)}) collective-permute-start(bf16[1024,128]{1,0:T(8,128)(2,1)} %get-tuple-element.87.own_att), channel_id=1, source_target_pairs={{0,2},{1,3},{2,0},{3,1},{4,6},{5,7},{6,4},{7,5},{8,10},{9,11},{10,... | collective-permute-start | bytes 786440 | tf_op jit(solution)/shard_map/ppermute | solution.py:702
  25.0 6.6 %collective-permute-done.5.a2 = bf16[1024,128]{1,0:T(8,128)(2,1)S(1)} collective-permute-done((bf16[1024,128]{1,0:T(8,128)(2,1)}, bf16[1024,128]{1,0:T(8,128)(2,1)S(1)}, u32[]{:S(2)}, u32[]{:S(2)}) %collective-permute-start.5) | collective-permute-done | bytes 262176 | tf_op jit(solution)/shard_map/ppermute | solution.py:702
  31.6 4.5 %collective-permute-done.6.a3 = bf16[1024,128]{1,0:T(8,128)(2,1)S(1)} collective-permute-done((bf16[1024,128]{1,0:T(8,128)(2,1)}, bf16[1024,128]{1,0:T(8,128)(2,1)S(1)}, u32[]{:S(2)}, u32[]{:S(2)}) %collective-permute-start.6) | collective-permute-done | bytes 262176 | tf_op jit(solution)/shard_map/ppermute | solution.py:702
  37.2 15.6 %feed.1 = (bf16[512,512]{1,0:T(8,128)(2,1)}, bf16[512,512]{1,0:T(8,128)(2,1)}, bf16[1024,512]{1,0:T(8,128)(2,1)}, f32[512,512]{1,0:T(8,128)}, f32[2,512]{1,0:T(2...) custom-call(s32[4]{0:T(128)} %pad_add_fusion.place, bf16[4,2,256,512]{3,2,1,0:T(8,128)(2,1)} %bitcast.44, ...), custom_call_target="tpu_custom_call" | custom-call | flops 14300000256 | bytes 1024 | tf_op jit(solution)/shard_map/feed/pallas_call | solution.py:535
  53.2 1.7 collective-permute-start.9
  54.9 0.8 collective-permute-done.18
  55.7 2.5 %add_convert_fusion.1 = bf16[8,128,512]{2,1,0:T(8,128)(2,1)} fusion(bf16[8,128,512]{2,1,0:T(8,128)(2,1)S(1)} %collective-permute-done.18, bf16[8,128,512]{2,1,0:T(8,128)(2,1)} %get-tuple-element.128), kind=kLoop, calls=%fused_computation.2 | loop fusion | flops 2097152 | bytes 3145728 | tf_op jit(solution)/shard_map/convert_element_type | solution.py:856
  58.2 11.7 %all-to-all-start = ((bf16[8,128,512]{2,1,0:T(8,128)(2,1)}), bf16[8,128,512]{2,1,0:T(8,128)(2,1)S(1)}, u32[]{:S(2)}, u32[]{:S(2)}) async-start(bf16[8,128,512]{2,1,0:T(8,128)(2,1)} %add_convert_fusion.1), calls=%async_computation | async-start | bytes 2097152 | tf_op jit(solution)/shard_map/all_to_all | solution.py:731
  69.9 0.8 copy-done.15
  70.7 5.1 %turn.1 = (bf16[512,512]{1,0:T(8,128)(2,1)}, f32[3,512]{1,0:T(4,128)}, bf16[512,128]{1,0:T(8,128)(2,1)}, bf16[512,128]{1,0:T(8,128)(2,1)}, bf16[512,128]{1,0:T(8...) custom-call(s32[4]{0:T(128)} %pad_add_fusion.place, ...), custom_call_target="tpu_custom_call" | custom-call | flops 65999998976 | bytes 1024 | tf_op jit(solution)/shard_map/turn/pallas_call | solution.py:600
  76.4 1.5 collective-permute-start.11
  77.9 1.5 collective-permute-start.17
  79.5 1.3 pad_maximum_fusion.7.sums
  81.7 1.3 collective-permute-done.11.d2
  83.0 1.9 %collective-permute-done.12.d3 = bf16[512,128]{1,0:T(8,128)(2,1)S(1)} collective-permute-done((bf16[512,128]{1,0:T(8,128)(2,1)}, bf16[512,128]{1,0:T(8,128)(2,1)S(1)}, u32[]{:S(2)}, u32[]{:S(2)}) %collective-permute-start.12) | collective-permute-done | bytes 131104 | tf_op jit(solution)/shard_map/ppermute | solution.py:702
  84.9 0.6 copy-done.24
  85.6 22.2 %attention_backward.1 = (bf16[336,512]{1,0:T(8,128)(2,1)}, bf16[320,512]{1,0:T(8,128)(2,1)}, bf16[16,512]{1,0:T(8,128)(2,1)}, bf16[1024,512]{1,0:T(8,128)(2,1)}, bf16[1024,512]{1,0:T(8,128)(2,1)}) custom-call(s32[1]{0:T(128)S(6)} %copy.48.kind, s32[4]{0:T(128)} %pad_add_fusion.place, bf16[2048,4096]{1,0:T(8,128)(2,1)} %get-tuple-element.84.p, ...), custom_call_target="tpu_custom_call" | custom-call | flops 8800000000 | bytes 1024 | tf_op jit(solution)/shard_map/attention_backward/pallas_call | solution.py:402
  107.8 3.3 %collective-permute-done.15 = bf16[128,512]{1,0:T(8,128)(2,1)S(1)} collective-permute-done((bf16[128,512]{1,0:T(8,128)(2,1)}, bf16[128,512]{1,0:T(8,128)(2,1)S(1)}, u32[]{:S(2)}, u32[]{:S(2)}) %collective-permute-start.15) | collective-permute-done | bytes 131104 | tf_op jit(solution)/shard_map/ppermute | solution.py:702
  111.0 1.2 collective-permute-done.16
  112.2 0.6 copy-done.8
  112.9 0.6 collective-permute-start.20
  113.5 1.2 broadcast_multiply_fusion.1
  114.7 1.8 add_convert_fusion.3
  116.5 1.0 add_convert_fusion.2
  117.7 3.0 %collective-permute-start.33 = (bf16[128,512]{1,0:T(8,128)(2,1)S(1)}, bf16[128,512]{1,0:T(8,128)(2,1)S(1)}, u32[]{:S(2)}, u32[]{:S(2)}) collective-permute-start(bf16[128,512]{1,0:T(8,128)(2,1)S(1)} %reduce_sum.12), channel_id=1, source_target_pairs={{0,16},{4,20},{8,24},{12,28},{16,0},{20,4},{24,8},{28,12},{1,17},{... | collective-permute-start | bytes 393224 | tf_op jit(solution)/shard_map/ppermute | solution.py:702
  120.6 6.5 %collective-permute-start.19 = (bf16[336,512]{1,0:T(8,128)(2,1)}, bf16[336,512]{1,0:T(8,128)(2,1)S(1)}, u32[]{:S(2)}, u32[]{:S(2)}) collective-permute-start(bf16[336,512]{1,0:T(8,128)(2,1)} %add_convert_fusion.3), channel_id=1, source_target_pairs={{0,4},{4,0},{8,12},{12,8},{16,20},{20,16},{24,28},{28,24},{1,5},{5... | collective-permute-start | bytes 1032200 | tf_op jit(solution)/shard_map/ppermute | solution.py:702
  127.2 1.5 collective-permute-start.21
  128.8 2.3 %collective-permute-start.34 = (bf16[256,512]{1,0:T(8,128)(2,1)S(1)}, bf16[256,512]{1,0:T(8,128)(2,1)S(1)}, u32[]{:S(2)}, u32[]{:S(2)}) collective-permute-start(bf16[256,512]{1,0:T(8,128)(2,1)S(1)} %pad_maximum_fusion.3), channel_id=1, source_target_pairs={{0,8},{4,12},{8,0},{12,4},{16,24},{20,28},{24,16},{28,20},{1,9},{5... | collective-permute-start | bytes 786440 | tf_op jit(solution)/shard_map/ppermute | solution.py:702
  131.1 1.8 %add_convert_fusion.m0 = bf16[1024,512]{1,0:T(8,128)(2,1)S(1)} fusion(bf16[1024,512]{1,0:T(8,128)(2,1)} %collective-permute-done.17, bf16[1024,512]{1,0:T(8,128)(2,1)} %get-tuple-element.127), kind=kLoop, calls=%fused_computation.1 | loop fusion | flops 2097152 | bytes 3145728 | tf_op jit(solution)/shard_map/convert_element_type | solution.py:892
  133.0 4.0 %collective-permute-done.34 = bf16[256,512]{1,0:T(8,128)(2,1)S(1)} collective-permute-done((bf16[256,512]{1,0:T(8,128)(2,1)S(1)}, bf16[256,512]{1,0:T(8,128)(2,1)S(1)}, u32[]{:S(2)}, u32[]{:S(2)}) %collective-permute-start.34) | collective-permute-done | bytes 262176 | tf_op jit(solution)/shard_map/ppermute | solution.py:702
  137.0 3.6 %collective-permute-done.21.got = bf16[512,512]{1,0:T(8,128)(2,1)S(1)} collective-permute-done((bf16[512,512]{1,0:T(8,128)(2,1)}, bf16[512,512]{1,0:T(8,128)(2,1)S(1)}, u32[]{:S(2)}, u32[]{:S(2)}) %collective-permute-start.21) | collective-permute-done | bytes 524320 | tf_op jit(solution)/shard_map/ppermute | solution.py:702
  140.9 1.9 %collective-permute-start.22 = (bf16[176,512]{1,0:T(8,128)(2,1)S(1)}, bf16[176,512]{1,0:T(8,128)(2,1)S(1)}, u32[]{:S(2)}, u32[]{:S(2)}) collective-permute-start(bf16[176,512]{1,0:T(8,128)(2,1)S(1)} %pad_maximum_fusion.4), channel_id=1, source_target_pairs={{0,8},{4,12},{8,0},{12,4},{16,24},{20,28},{24,16},{28,20},{1,9},{5... | collective-permute-start | bytes 540680 | tf_op jit(solution)/shard_map/ppermute | solution.py:702
  143.4 3.1 %collective-permute-done.22 = bf16[176,512]{1,0:T(8,128)(2,1)S(1)} collective-permute-done((bf16[176,512]{1,0:T(8,128)(2,1)S(1)}, bf16[176,512]{1,0:T(8,128)(2,1)S(1)}, u32[]{:S(2)}, u32[]{:S(2)}) %collective-permute-start.22) | collective-permute-done | bytes 180256 | tf_op jit(solution)/shard_map/ppermute | solution.py:702
  146.7 0.7 collective-permute-start.23
  147.4 3.9 %close.1.g0 = bf16[512,512]{1,0:T(8,128)(2,1)} custom-call(s32[4]{0:T(128)} %pad_add_fusion.place, bf16[1024,512]{1,0:T(8,128)(2,1)} %get-tuple-element.136.keep0.keep1, bf16[1024,512]{1,0:T(8,128)(2,1)} %get-tuple-element.136.keep0.keep1, bf16[1024,512]{1,0:T(8,128)(2,1)} %copy-done.3, bf16[1024,512]{1,0:T(8,128)(2,1)} %copy-done.3, ...), custom_call_target="tpu_custom_call" | custom-call | flops 2200000000 | bytes 1024 | tf_op jit(solution)/shard_map/close/pallas_call | solution.py:643
  151.3 1.5 collective-permute-start.29
  152.9 2.4 %collective-permute-start.24 = (bf16[80,512]{1,0:T(8,128)(2,1)S(1)}, bf16[80,512]{1,0:T(8,128)(2,1)S(1)}, u32[]{:S(2)}, u32[]{:S(2)}) collective-permute-start(bf16[80,512]{1,0:T(8,128)(2,1)S(1)} %fusion.2), channel_id=1, source_target_pairs={{0,16},{4,20},{8,24},{12,28},{16,0},{20,4},{24,8},{28,12},{1,17},{... | collective-permute-start | bytes 245768 | tf_op jit(solution)/shard_map/ppermute | solution.py:702
  155.3 5.2 %collective-permute-done.24 = bf16[80,512]{1,0:T(8,128)(2,1)S(1)} collective-permute-done((bf16[80,512]{1,0:T(8,128)(2,1)S(1)}, bf16[80,512]{1,0:T(8,128)(2,1)S(1)}, u32[]{:S(2)}, u32[]{:S(2)}) %collective-permute-start.24) | collective-permute-done | bytes 81952 | tf_op jit(solution)/shard_map/ppermute | solution.py:702
  161.7 4.7 %collective-permute-done.25 = bf16[160,512]{1,0:T(8,128)(2,1)S(1)} collective-permute-done((bf16[160,512]{1,0:T(8,128)(2,1)S(1)}, bf16[160,512]{1,0:T(8,128)(2,1)S(1)}, u32[]{:S(2)}, u32[]{:S(2)}) %collective-permute-start.25) | collective-permute-done | bytes 163872 | tf_op jit(solution)/shard_map/ppermute | solution.py:702
  166.6 1.6 fusion.6
  168.2 3.6 %collective-permute-start.26 = (bf16[320,512]{1,0:T(8,128)(2,1)S(1)}, bf16[320,512]{1,0:T(8,128)(2,1)S(1)}, u32[]{:S(2)}, u32[]{:S(2)}) collective-permute-start(bf16[320,512]{1,0:T(8,128)(2,1)S(1)} %pad_maximum_fusion.2), channel_id=1, source_target_pairs={{0,4},{4,0},{8,12},{12,8},{16,20},{20,16},{24,28},{28,24},{1,5},{5... | collective-permute-start | bytes 983048 | tf_op jit(solution)/shard_map/ppermute | solution.py:702
  173.7 2.1 %collective-permute-done.32 = f32[5,512]{1,0:T(8,128)S(1)} collective-permute-done((f32[5,512]{1,0:T(8,128)S(1)}, f32[5,512]{1,0:T(8,128)S(1)}, u32[]{:S(2)}, u32[]{:S(2)}) %collective-permute-start.32) | collective-permute-done | bytes 10272 | tf_op jit(solution)/shard_map/ppermute | solution.py:702
  176.5 2.7 %collect.1 = (bf16[2048,512]{1,0:T(8,128)(2,1)}, bf16[2048,512]{1,0:T(8,128)(2,1)}) custom-call(s32[4]{0:T(128)S(1)} %copy-done.1, bf16[1024,512]{1,0:T(8,128)(2,1)S(1)} %add_convert_fusion.m0, bf16[1024,512]{1,0:T(8,128)(2,1)S(1)} %collective-permute-done.27.m1, bf16[512,512]{1,0:T(8,128)(2,1)S(1)} %copy-done, ...), custom_call_target="tpu_custom_call" | custom-call | flops 3300000000 | bytes 1024 | tf_op jit(solution)/shard_map/collect/pallas_call | solution.py:687
  179.2 0.9 collective-permute-done.26
  180.4 1.0 fusion.7
  181.4 0.7 slice.140
  (131 shorter events, 10.4 us)
Async XLA Ops:
  0.7 21.0 %collective-permute-start = (bf16[128,512]{1,0:T(8,128)(2,1)}, bf16[128,512]{1,0:T(8,128)(2,1)S(1)}, u32[]{:S(2)}, u32[]{:S(2)}) collective-permute-start(bf16[128,512]{1,0:T(8,128)(2,1)} %w0.1), channel_id=1, source_target_pairs={{0,1},{1,0},{2,3},{3,2},{4,5},{5,4},{6,7},{7,6},{8,9},{9,8},{10,11... | collective-permute-start | bytes 393224 | tf_op jit(solution)/shard_map/ppermute | solution.py:702
  1.2 20.5 %collective-permute-start.1 = (bf16[128,512]{1,0:T(8,128)(2,1)}, bf16[128,512]{1,0:T(8,128)(2,1)S(1)}, u32[]{:S(2)}, u32[]{:S(2)}) collective-permute-start(bf16[128,512]{1,0:T(8,128)(2,1)} %w0.1), channel_id=1, source_target_pairs={{0,2},{1,3},{2,0},{3,1},{4,6},{5,7},{6,4},{7,5},{8,10},{9,11},{10,... | collective-permute-start | bytes 393224 | tf_op jit(solution)/shard_map/ppermute | solution.py:702
  3.8 17.9 %collective-permute-start.2 = (bf16[128,512]{1,0:T(8,128)(2,1)}, bf16[128,512]{1,0:T(8,128)(2,1)S(1)}, u32[]{:S(2)}, u32[]{:S(2)}) collective-permute-start(bf16[128,512]{1,0:T(8,128)(2,1)} %w0.1), channel_id=1, source_target_pairs={{0,3},{1,2},{2,1},{3,0},{4,7},{5,6},{6,5},{7,4},{8,11},{9,10},{10,... | collective-permute-start | bytes 393224 | tf_op jit(solution)/shard_map/ppermute | solution.py:702
  3.8 17.8 %collective-permute-start.3 = (f32[1,512]{1,0:T(1,128)}, f32[1,512]{1,0:T(1,128)S(1)}, u32[]{:S(2)}, u32[]{:S(2)}) collective-permute-start(f32[1,512]{1,0:T(1,128)} %bitcast.66), channel_id=1, source_target_pairs={{0,1},{1,0},{2,3},{3,2},{4,5},{5,4},{6,7},{7,6},{8,9},{9,8},{10,11... | collective-permute-start | bytes 6152 | tf_op jit(solution)/shard_map/ppermute | solution.py:702
  4.6 17.1 %copy-start.11 = (bf16[512,512]{1,0:T(8,128)(2,1)S(1)}, bf16[512,512]{1,0:T(8,128)(2,1)}, u32[]{:S(2)}) copy-start(bf16[512,512]{1,0:T(8,128)(2,1)} %i0.1) | copy-start | bytes 1572868
  4.6 17.5 %copy-start.12 = (bf16[512,512]{1,0:T(8,128)(2,1)S(1)}, bf16[512,512]{1,0:T(8,128)(2,1)}, u32[]{:S(2)}) copy-start(bf16[512,512]{1,0:T(8,128)(2,1)} %u0.1) | copy-start | bytes 1572868
  21.6 14.5 %copy-start.25 = (f32[1,512]{1,0:T(1,128)}, f32[1,512]{1,0:T(1,128)S(1)}, u32[]{:S(2)}) copy-start(f32[1,512]{1,0:T(1,128)S(1)} %collective-permute-done.3.b1) | copy-start | bytes 6148
  21.6 14.5 %copy-start.19 = (bf16[128,512]{1,0:T(8,128)(2,1)}, bf16[128,512]{1,0:T(8,128)(2,1)S(1)}, u32[]{:S(2)}) copy-start(bf16[128,512]{1,0:T(8,128)(2,1)S(1)} %collective-permute-done.w1) | copy-start | bytes 393220
  21.7 14.5 %copy-start.20 = (bf16[128,512]{1,0:T(8,128)(2,1)}, bf16[128,512]{1,0:T(8,128)(2,1)S(1)}, u32[]{:S(2)}) copy-start(bf16[128,512]{1,0:T(8,128)(2,1)S(1)} %collective-permute-done.1.w2) | copy-start | bytes 393220
  21.7 14.5 %copy-start.21 = (bf16[128,512]{1,0:T(8,128)(2,1)}, bf16[128,512]{1,0:T(8,128)(2,1)S(1)}, u32[]{:S(2)}) copy-start(bf16[128,512]{1,0:T(8,128)(2,1)S(1)} %collective-permute-done.2.w3) | copy-start | bytes 393220
  21.7 14.4 %collective-permute-start.7 = (bf16[512,512]{1,0:T(8,128)(2,1)S(1)}, bf16[512,512]{1,0:T(8,128)(2,1)S(1)}, u32[]{:S(2)}, u32[]{:S(2)}) collective-permute-start(bf16[512,512]{1,0:T(8,128)(2,1)S(1)} %copy-done.11), channel_id=1, source_target_pairs={{0,1},{1,0},{2,3},{3,2},{4,5},{5,4},{6,7},{7,6},{8,9},{9,8},{10,11... | collective-permute-start | bytes 1572872 | tf_op jit(solution)/shard_map/ppermute | solution.py:702
  22.1 14.0 %collective-permute-start.8 = (bf16[512,512]{1,0:T(8,128)(2,1)S(1)}, bf16[512,512]{1,0:T(8,128)(2,1)S(1)}, u32[]{:S(2)}, u32[]{:S(2)}) collective-permute-start(bf16[512,512]{1,0:T(8,128)(2,1)S(1)} %copy-done.12), channel_id=1, source_target_pairs={{0,1},{1,0},{2,3},{3,2},{4,5},{5,4},{6,7},{7,6},{8,9},{9,8},{10,11... | collective-permute-start | bytes 1572872 | tf_op jit(solution)/shard_map/ppermute | solution.py:702
  22.3 9.3 %collective-permute-start.5 = (bf16[1024,128]{1,0:T(8,128)(2,1)}, bf16[1024,128]{1,0:T(8,128)(2,1)S(1)}, u32[]{:S(2)}, u32[]{:S(2)}) collective-permute-start(bf16[1024,128]{1,0:T(8,128)(2,1)} %get-tuple-element.87.own_att), channel_id=1, source_target_pairs={{0,2},{1,3},{2,0},{3,1},{4,6},{5,7},{6,4},{7,5},{8,10},{9,11},{10,... | collective-permute-start | bytes 786440 | tf_op jit(solution)/shard_map/ppermute | solution.py:702
  24.2 7.4 %collective-permute-start.4 = (bf16[1024,128]{1,0:T(8,128)(2,1)}, bf16[1024,128]{1,0:T(8,128)(2,1)S(1)}, u32[]{:S(2)}, u32[]{:S(2)}) collective-permute-start(bf16[1024,128]{1,0:T(8,128)(2,1)} %get-tuple-element.88), channel_id=1, source_target_pairs={{0,1},{1,0},{2,3},{3,2},{4,5},{5,4},{6,7},{7,6},{8,9},{9,8},{10,11... | collective-permute-start | bytes 786440 | tf_op jit(solution)/shard_map/ppermute | solution.py:702
  24.2 11.9 %collective-permute-start.6 = (bf16[1024,128]{1,0:T(8,128)(2,1)}, bf16[1024,128]{1,0:T(8,128)(2,1)S(1)}, u32[]{:S(2)}, u32[]{:S(2)}) collective-permute-start(bf16[1024,128]{1,0:T(8,128)(2,1)} %get-tuple-element.88), channel_id=1, source_target_pairs={{0,3},{1,2},{2,1},{3,0},{4,7},{5,6},{6,5},{7,4},{8,11},{9,10},{10,... | collective-permute-start | bytes 786440 | tf_op jit(solution)/shard_map/ppermute | solution.py:702
  52.7 2.9 %collective-permute-start.18 = (bf16[8,128,512]{2,1,0:T(8,128)(2,1)}, bf16[8,128,512]{2,1,0:T(8,128)(2,1)S(1)}, u32[]{:S(2)}, u32[]{:S(2)}) collective-permute-start(bf16[8,128,512]{2,1,0:T(8,128)(2,1)} %get-tuple-element.129), channel_id=1, source_target_pairs={{0,1},{1,0},{2,3},{3,2},{4,5},{5,4},{6,7},{7,6},{8,9},{9,8},{10,11... | collective-permute-start | bytes 3145736 | tf_op jit(solution)/shard_map/ppermute | solution.py:702
  53.2 16.8 %collective-permute-start.9 = (bf16[512,512]{1,0:T(8,128)(2,1)}, bf16[512,512]{1,0:T(8,128)(2,1)S(1)}, u32[]{:S(2)}, u32[]{:S(2)}) collective-permute-start(bf16[512,512]{1,0:T(8,128)(2,1)} %get-tuple-element.98), channel_id=1, source_target_pairs={{0,2},{1,3},{2,0},{3,1},{4,6},{5,7},{6,4},{7,5},{8,10},{9,11},{10,... | collective-permute-start | bytes 1572872 | tf_op jit(solution)/shard_map/ppermute | solution.py:702
  58.2 54.0 %all-to-all-start = ((bf16[8,128,512]{2,1,0:T(8,128)(2,1)}), bf16[8,128,512]{2,1,0:T(8,128)(2,1)S(1)}, u32[]{:S(2)}, u32[]{:S(2)}) async-start(bf16[8,128,512]{2,1,0:T(8,128)(2,1)} %add_convert_fusion.1), calls=%async_computation | async-start | bytes 2097152 | tf_op jit(solution)/shard_map/all_to_all | solution.py:731
  75.9 2.1 %collective-permute-start.10 = (bf16[512,128]{1,0:T(8,128)(2,1)}, bf16[512,128]{1,0:T(8,128)(2,1)S(1)}, u32[]{:S(2)}, u32[]{:S(2)}) collective-permute-start(bf16[512,128]{1,0:T(8,128)(2,1)} %get-tuple-element.101), channel_id=1, source_target_pairs={{0,1},{1,0},{2,3},{3,2},{4,5},{5,4},{6,7},{7,6},{8,9},{9,8},{10,11... | collective-permute-start | bytes 393224 | tf_op jit(solution)/shard_map/ppermute | solution.py:702
  76.0 3.5 %collective-permute-start.13 = (f32[1,512]{1,0:T(1,128)S(1)}, f32[1,512]{1,0:T(1,128)S(1)}, u32[]{:S(2)}, u32[]{:S(2)}) collective-permute-start(f32[1,512]{1,0:T(1,128)S(1)} %slice.94), channel_id=1, source_target_pairs={{0,1},{1,0},{2,3},{3,2},{4,5},{5,4},{6,7},{7,6},{8,9},{9,8},{10,11... | collective-permute-start | bytes 6152 | tf_op jit(solution)/shard_map/ppermute | solution.py:702
  76.4 6.6 %collective-permute-start.11 = (bf16[512,128]{1,0:T(8,128)(2,1)}, bf16[512,128]{1,0:T(8,128)(2,1)S(1)}, u32[]{:S(2)}, u32[]{:S(2)}) collective-permute-start(bf16[512,128]{1,0:T(8,128)(2,1)} %get-tuple-element.102), channel_id=1, source_target_pairs={{0,2},{1,3},{2,0},{3,1},{4,6},{5,7},{6,4},{7,5},{8,10},{9,11},{10,... | collective-permute-start | bytes 393224 | tf_op jit(solution)/shard_map/ppermute | solution.py:702
  77.9 7.0 %collective-permute-start.12 = (bf16[512,128]{1,0:T(8,128)(2,1)}, bf16[512,128]{1,0:T(8,128)(2,1)S(1)}, u32[]{:S(2)}, u32[]{:S(2)}) collective-permute-start(bf16[512,128]{1,0:T(8,128)(2,1)} %get-tuple-element.103), channel_id=1, source_target_pairs={{0,3},{1,2},{2,1},{3,0},{4,7},{5,6},{6,5},{7,4},{8,11},{9,10},{10,... | collective-permute-start | bytes 393224 | tf_op jit(solution)/shard_map/ppermute | solution.py:702
  77.9 34.3 %collective-permute-start.17 = (bf16[1024,512]{1,0:T(8,128)(2,1)S(1)}, bf16[1024,512]{1,0:T(8,128)(2,1)}, u32[]{:S(2)}, u32[]{:S(2)}) collective-permute-start(bf16[1024,512]{1,0:T(8,128)(2,1)S(1)} %copy-done.4), channel_id=1, source_target_pairs={{0,2},{1,3},{2,0},{3,1},{4,6},{5,7},{6,4},{7,5},{8,10},{9,11},{10,... | collective-permute-start | bytes 3145736 | tf_op jit(solution)/shard_map/ppermute | solution.py:702
  80.8 27.0 %collective-permute-start.14 = (bf16[128,512]{1,0:T(8,128)(2,1)}, bf16[128,512]{1,0:T(8,128)(2,1)S(1)}, u32[]{:S(2)}, u32[]{:S(2)}) collective-permute-start(bf16[128,512]{1,0:T(8,128)(2,1)} %get-tuple-element.123), channel_id=1, source_target_pairs={{0,1},{1,0},{2,3},{3,2},{4,5},{5,4},{6,7},{7,6},{8,9},{9,8},{10,11... | collective-permute-start | bytes 393224 | tf_op jit(solution)/shard_map/ppermute | solution.py:702
  81.2 29.9 %collective-permute-start.15 = (bf16[128,512]{1,0:T(8,128)(2,1)}, bf16[128,512]{1,0:T(8,128)(2,1)S(1)}, u32[]{:S(2)}, u32[]{:S(2)}) collective-permute-start(bf16[128,512]{1,0:T(8,128)(2,1)} %get-tuple-element.124), channel_id=1, source_target_pairs={{0,2},{1,3},{2,0},{3,1},{4,6},{5,7},{6,4},{7,5},{8,10},{9,11},{10,... | collective-permute-start | bytes 393224 | tf_op jit(solution)/shard_map/ppermute | solution.py:702
  83.0 29.3 %collective-permute-start.16 = (bf16[128,512]{1,0:T(8,128)(2,1)}, bf16[128,512]{1,0:T(8,128)(2,1)S(1)}, u32[]{:S(2)}, u32[]{:S(2)}) collective-permute-start(bf16[128,512]{1,0:T(8,128)(2,1)} %get-tuple-element.125), channel_id=1, source_target_pairs={{0,3},{1,2},{2,1},{3,0},{4,7},{5,6},{6,5},{7,4},{8,11},{9,10},{10,... | collective-permute-start | bytes 393224 | tf_op jit(solution)/shard_map/ppermute | solution.py:702
  112.9 3.6 %collective-permute-start.20 = (bf16[1024,512]{1,0:T(8,128)(2,1)}, bf16[1024,512]{1,0:T(8,128)(2,1)S(1)}, u32[]{:S(2)}, u32[]{:S(2)}) collective-permute-start(bf16[1024,512]{1,0:T(8,128)(2,1)} %get-tuple-element.137), channel_id=1, source_target_pairs={{0,1},{1,0},{2,3},{3,2},{4,5},{5,4},{6,7},{7,6},{8,9},{9,8},{10,11... | collective-permute-start | bytes 3145736 | tf_op jit(solution)/shard_map/ppermute | solution.py:702
  116.5 16.4 %copy-start.3 = (bf16[1024,512]{1,0:T(8,128)(2,1)}, bf16[1024,512]{1,0:T(8,128)(2,1)S(1)}, u32[]{:S(2)}) copy-start(bf16[1024,512]{1,0:T(8,128)(2,1)S(1)} %collective-permute-done.20.near0.near1) | copy-start | bytes 3145732
  117.7 11.0 %collective-permute-start.33 = (bf16[128,512]{1,0:T(8,128)(2,1)S(1)}, bf16[128,512]{1,0:T(8,128)(2,1)S(1)}, u32[]{:S(2)}, u32[]{:S(2)}) collective-permute-start(bf16[128,512]{1,0:T(8,128)(2,1)S(1)} %reduce_sum.12), channel_id=1, source_target_pairs={{0,16},{4,20},{8,24},{12,28},{16,0},{20,4},{24,8},{28,12},{1,17},{... | collective-permute-start | bytes 393224 | tf_op jit(solution)/shard_map/ppermute | solution.py:702
  120.6 16.4 %collective-permute-start.19 = (bf16[336,512]{1,0:T(8,128)(2,1)}, bf16[336,512]{1,0:T(8,128)(2,1)S(1)}, u32[]{:S(2)}, u32[]{:S(2)}) collective-permute-start(bf16[336,512]{1,0:T(8,128)(2,1)} %add_convert_fusion.3), channel_id=1, source_target_pairs={{0,4},{4,0},{8,12},{12,8},{16,20},{20,16},{24,28},{28,24},{1,5},{5... | collective-permute-start | bytes 1032200 | tf_op jit(solution)/shard_map/ppermute | solution.py:702
  127.2 13.5 %collective-permute-start.21 = (bf16[512,512]{1,0:T(8,128)(2,1)}, bf16[512,512]{1,0:T(8,128)(2,1)S(1)}, u32[]{:S(2)}, u32[]{:S(2)}) collective-permute-start(bf16[512,512]{1,0:T(8,128)(2,1)} %bitcast.50), channel_id=1, source_target_pairs={{0,2},{1,3},{2,0},{3,1},{4,6},{5,7},{6,4},{7,5},{8,10},{9,11},{10,... | collective-permute-start | bytes 1572872 | tf_op jit(solution)/shard_map/ppermute | solution.py:702
  128.7 12.0 %copy-start.9 = (bf16[16,512]{1,0:T(8,128)(2,1)S(1)}, bf16[16,512]{1,0:T(8,128)(2,1)}, u32[]{:S(2)}) copy-start(bf16[16,512]{1,0:T(8,128)(2,1)} %get-tuple-element.139) | copy-start | bytes 49156
  128.7 12.0 %copy-start.6 = (bf16[320,512]{1,0:T(8,128)(2,1)S(1)}, bf16[320,512]{1,0:T(8,128)(2,1)}, u32[]{:S(2)}) copy-start(bf16[320,512]{1,0:T(8,128)(2,1)} %get-tuple-element.130) | copy-start | bytes 983044
  128.8 8.2 %collective-permute-start.34 = (bf16[256,512]{1,0:T(8,128)(2,1)S(1)}, bf16[256,512]{1,0:T(8,128)(2,1)S(1)}, u32[]{:S(2)}, u32[]{:S(2)}) collective-permute-start(bf16[256,512]{1,0:T(8,128)(2,1)S(1)} %pad_maximum_fusion.3), channel_id=1, source_target_pairs={{0,8},{4,12},{8,0},{12,4},{16,24},{20,28},{24,16},{28,20},{1,9},{5... | collective-permute-start | bytes 786440 | tf_op jit(solution)/shard_map/ppermute | solution.py:702
  132.9 43.5 %collective-permute-start.27 = (bf16[1024,512]{1,0:T(8,128)(2,1)S(1)}, bf16[1024,512]{1,0:T(8,128)(2,1)S(1)}, u32[]{:S(2)}, u32[]{:S(2)}) collective-permute-start(bf16[1024,512]{1,0:T(8,128)(2,1)S(1)} %add_convert_fusion.m0), channel_id=1, source_target_pairs={{0,1},{1,0},{2,3},{3,2},{4,5},{5,4},{6,7},{7,6},{8,9},{9,8},{10,11... | collective-permute-start | bytes 3145736 | tf_op jit(solution)/shard_map/ppermute | solution.py:702
  140.9 5.6 %collective-permute-start.22 = (bf16[176,512]{1,0:T(8,128)(2,1)S(1)}, bf16[176,512]{1,0:T(8,128)(2,1)S(1)}, u32[]{:S(2)}, u32[]{:S(2)}) collective-permute-start(bf16[176,512]{1,0:T(8,128)(2,1)S(1)} %pad_maximum_fusion.4), channel_id=1, source_target_pairs={{0,8},{4,12},{8,0},{12,4},{16,24},{20,28},{24,16},{28,20},{1,9},{5... | collective-permute-start | bytes 540680 | tf_op jit(solution)/shard_map/ppermute | solution.py:702
  143.0 17.9 %collective-permute-start.35 = (bf16[512,512]{1,0:T(8,128)(2,1)S(1)}, bf16[512,512]{1,0:T(8,128)(2,1)S(1)}, u32[]{:S(2)}, u32[]{:S(2)}) collective-permute-start(bf16[512,512]{1,0:T(8,128)(2,1)S(1)} %pad_maximum_fusion.1), channel_id=1, source_target_pairs={{0,4},{4,0},{8,12},{12,8},{16,20},{20,16},{24,28},{28,24},{1,5},{5... | collective-permute-start | bytes 1572872 | tf_op jit(solution)/shard_map/ppermute | solution.py:702
  146.7 6.2 %collective-permute-start.23 = (bf16[96,512]{1,0:T(8,128)(2,1)S(1)}, bf16[96,512]{1,0:T(8,128)(2,1)S(1)}, u32[]{:S(2)}, u32[]{:S(2)}) collective-permute-start(bf16[96,512]{1,0:T(8,128)(2,1)S(1)} %pad_maximum_fusion.6), channel_id=1, source_target_pairs={{0,16},{4,20},{8,24},{12,28},{16,0},{20,4},{24,8},{28,12},{1,17},{... | collective-permute-start | bytes 294920 | tf_op jit(solution)/shard_map/ppermute | solution.py:702
  151.3 20.5 %collective-permute-start.29 = (bf16[512,512]{1,0:T(8,128)(2,1)}, bf16[512,512]{1,0:T(8,128)(2,1)S(1)}, u32[]{:S(2)}, u32[]{:S(2)}) collective-permute-start(bf16[512,512]{1,0:T(8,128)(2,1)} %close.1.g0), channel_id=1, source_target_pairs={{0,2},{1,3},{2,0},{3,1},{4,6},{5,7},{6,4},{7,5},{8,10},{9,11},{10,... | collective-permute-start | bytes 1572872 | tf_op jit(solution)/shard_map/ppermute | solution.py:702
  152.8 23.6 %collective-permute-start.28 = (bf16[512,512]{1,0:T(8,128)(2,1)}, bf16[512,512]{1,0:T(8,128)(2,1)S(1)}, u32[]{:S(2)}, u32[]{:S(2)}) collective-permute-start(bf16[512,512]{1,0:T(8,128)(2,1)} %close.1.g0), channel_id=1, source_target_pairs={{0,1},{1,0},{2,3},{3,2},{4,5},{5,4},{6,7},{7,6},{8,9},{9,8},{10,11... | collective-permute-start | bytes 1572872 | tf_op jit(solution)/shard_map/ppermute | solution.py:702
  152.9 7.6 %collective-permute-start.24 = (bf16[80,512]{1,0:T(8,128)(2,1)S(1)}, bf16[80,512]{1,0:T(8,128)(2,1)S(1)}, u32[]{:S(2)}, u32[]{:S(2)}) collective-permute-start(bf16[80,512]{1,0:T(8,128)(2,1)S(1)} %fusion.2), channel_id=1, source_target_pairs={{0,16},{4,20},{8,24},{12,28},{16,0},{20,4},{24,8},{28,12},{1,17},{... | collective-permute-start | bytes 245768 | tf_op jit(solution)/shard_map/ppermute | solution.py:702
  160.5 5.9 %collective-permute-start.25 = (bf16[160,512]{1,0:T(8,128)(2,1)S(1)}, bf16[160,512]{1,0:T(8,128)(2,1)S(1)}, u32[]{:S(2)}, u32[]{:S(2)}) collective-permute-start(bf16[160,512]{1,0:T(8,128)(2,1)S(1)} %pad_maximum_fusion.5), channel_id=1, source_target_pairs={{0,8},{4,12},{8,0},{12,4},{16,24},{20,28},{24,16},{28,20},{1,9},{5... | collective-permute-start | bytes 491528 | tf_op jit(solution)/shard_map/ppermute | solution.py:702
  166.5 5.5 %collective-permute-start.31 = (f32[5,512]{1,0:T(8,128)S(1)}, f32[5,512]{1,0:T(8,128)S(1)}, u32[]{:S(2)}, u32[]{:S(2)}) collective-permute-start(f32[5,512]{1,0:T(8,128)S(1)} %slice.131), channel_id=1, source_target_pairs={{0,1},{1,0},{2,3},{3,2},{4,5},{5,4},{6,7},{7,6},{8,9},{9,8},{10,11... | collective-permute-start | bytes 30728 | tf_op jit(solution)/shard_map/ppermute | solution.py:702
  166.6 9.9 %copy-start = (bf16[512,512]{1,0:T(8,128)(2,1)S(1)}, bf16[512,512]{1,0:T(8,128)(2,1)}, u32[]{:S(2)}) copy-start(bf16[512,512]{1,0:T(8,128)(2,1)} %close.1.g0) | copy-start | bytes 1572868
  166.6 9.9 %copy-start.1 = (s32[4]{0:T(128)S(1)}, s32[4]{0:T(128)}, u32[]{:S(2)}) copy-start(s32[4]{0:T(128)} %pad_add_fusion.place) | copy-start | bytes 52
  168.2 11.9 %collective-permute-start.26 = (bf16[320,512]{1,0:T(8,128)(2,1)S(1)}, bf16[320,512]{1,0:T(8,128)(2,1)S(1)}, u32[]{:S(2)}, u32[]{:S(2)}) collective-permute-start(bf16[320,512]{1,0:T(8,128)(2,1)S(1)} %pad_maximum_fusion.2), channel_id=1, source_target_pairs={{0,4},{4,0},{8,12},{12,8},{16,20},{20,16},{24,28},{28,24},{1,5},{5... | collective-permute-start | bytes 983048 | tf_op jit(solution)/shard_map/ppermute | solution.py:702
  171.8 4.7 %collective-permute-start.30 = (bf16[512,512]{1,0:T(8,128)(2,1)S(1)}, bf16[512,512]{1,0:T(8,128)(2,1)S(1)}, u32[]{:S(2)}, u32[]{:S(2)}) collective-permute-start(bf16[512,512]{1,0:T(8,128)(2,1)S(1)} %collective-permute-done.29.g2), channel_id=1, source_target_pairs={{0,1},{1,0},{2,3},{3,2},{4,5},{5,4},{6,7},{7,6},{8,9},{9,8},{10,11... | collective-permute-start | bytes 1572872 | tf_op jit(solution)/shard_map/ppermute | solution.py:702
  172.0 3.8 %collective-permute-start.32 = (f32[5,512]{1,0:T(8,128)S(1)}, f32[5,512]{1,0:T(8,128)S(1)}, u32[]{:S(2)}, u32[]{:S(2)}) collective-permute-start(f32[5,512]{1,0:T(8,128)S(1)} %slice_add_fusion.7), channel_id=1, source_target_pairs={{0,2},{1,3},{2,0},{3,1},{4,6},{5,7},{6,4},{7,5},{8,10},{9,11},{10,... | collective-permute-start | bytes 30728 | tf_op jit(solution)/shard_map/ppermute | solution.py:702
  (15 other events, 47.5 us)

commit v5 on v4

--- a/solution.py
+++ b/solution.py
@@ -788,6 +788,13 @@
     return value, (small.astype(f32) + got[rows:]).astype(bf16), other
 
 
+def add_dp(value, small, mask):
+    got = swap(jnp.concatenate([value, small], axis=0), "dp", mask).astype(f32)
+    rows = value.shape[0]
+    value = (value.astype(f32) + got[:rows]).astype(bf16)
+    return value, (small.astype(f32) + got[rows:]).astype(bf16)
+
+
 def after(value, *others):
     return lax.optimization_barrier((value, others))[0]
 
@@ -895,9 +902,10 @@
     beyond = swap(grad, "mp", 2)
     for mask in reversed(masks()):
         feed_total, _ = double_dp(feed_total, mask)
-    for mask in middle:
+    for mask in middle[:-1]:
         last, small, _ = halve_dp(last, small, mask)
-    for mask in reversed(middle):
+    last, small = add_dp(last, small, middle[-1])
+    for mask in reversed(middle[:-1]):
         last, _ = double_dp(last, mask)
     tokens_grad = [grad, swap(grad, "mp", 1), beyond, swap(beyond, "mp", 1)]
     small = after(small, last)

time: 183 us -> 175 us (0.956)
  waiting for transfers between devices: 43.4 us -> 38.1 us
  starting transfers between devices: 50.3 us -> 47.2 us
    ppermute x36 -> x35, waiting for transfers between devices: 43.4 us -> 38.1 us  [swap(): return lax.ppermute(value, axis, [(i, i ^ mask) for i in range(size)])]
    all_to_all x1, starting transfers between devices: 11.7 us -> 9.7 us  [exchange(): lax.all_to_all(value, 'dp', split_axis=0, concat_axis=0, tiled=True, axis...]
    ppermute x36 -> x35, starting transfers between devices: 38.5 us -> 37.5 us  [swap(): return lax.ppermute(value, axis, [(i, i ^ mask) for i in range(size)])]
  transfers between devices with their start and end apart: 37 -> 36, of which waited for: 14 -> 14; matrix products, arithmetic and copies ran while one was open for 8% -> 8% of each run, Pallas kernels for 28% -> 29%
where the time goes in v5:
time: 175 us; the launch traced here: 174 us
  Pallas kernels  66.5 us (38%)
  starting transfers between devices  47.2 us (27%)
  waiting for transfers between devices  38.1 us (22%)
  other arithmetic  11.8 us (7%)
  local copies, waits for them, and re-layouts  8.31 us (5%)
  between operations  1.86 us (1%)
    ppermute x35, waiting for transfers between devices, swap(): return lax.ppermute(value, axis, [(i, i ^ mask) for i in range(size)])  38.1 us
    ppermute x35, starting transfers between devices, swap(): return lax.ppermute(value, axis, [(i, i ^ mask) for i in range(size)])  37.5 us
    pallas_call x1, Pallas kernels, attention_backward(): pl.pallas_call(functools.partial(backward_body, count, block, length // 2...  22.2 us
    pallas_call x1, Pallas kernels, attention_forward(): pl.pallas_call(functools.partial(forward_body, block, length // 2), grid=...  17 us
    pallas_call x1, Pallas kernels, feed(): pl.pallas_call(feed_body, grid_spec=pltpu.PrefetchScalarGridSpec(num_scal...  15.6 us
    all_to_all x1, starting transfers between devices, exchange(): lax.all_to_all(value, 'dp', split_axis=0, concat_axis=0, tiled=True, axis...  9.7 us
    pallas_call x1, Pallas kernels, turn(): pl.pallas_call(turn_body, grid_spec=pltpu.PrefetchScalarGridSpec(num_scal...  5.14 us
    pallas_call x1, Pallas kernels, close(): pl.pallas_call(close_body, grid_spec=pltpu.PrefetchScalarGridSpec(num_sca...  3.95 us
  transfers between devices with their start and end apart: 36, of which 14 were waited for; matrix products, arithmetic and copies ran while one was open for 8% of the time, Pallas kernels for 29%

profile of v5, /device:TPU:0, one launch (start us, length us, event | category | flops | bytes accessed | tf_op | source)
XLA Modules:
  0.0 173.8 jit_solution(7878443288674073634)
XLA Ops:
  1.2 2.6 %collective-permute-start.1 = (bf16[128,512]{1,0:T(8,128)(2,1)}, bf16[128,512]{1,0:T(8,128)(2,1)S(1)}, u32[]{:S(2)}, u32[]{:S(2)}) collective-permute-start(bf16[128,512]{1,0:T(8,128)(2,1)} %w0.1), channel_id=1, source_target_pairs={{0,2},{1,3},{2,0},{3,1},{4,6},{5,7},{6,4},{7,5},{8,10},{9,11},{10,... | collective-permute-start | bytes 393224 | tf_op jit(solution)/shard_map/ppermute | solution.py:702
  4.7 17.0 %attention_forward.1 = (bf16[2048,512]{1,0:T(8,128)(2,1)}, bf16[2048,128]{1,0:T(8,128)(2,1)}, bf16[2048,128]{1,0:T(8,128)(2,1)}, bf16[2048,128]{1,0:T(8,128)(2,1...) custom-call(s32[1]{0:T(128)S(6)} %copy.48.kind, ...), custom_call_target="tpu_custom_call" | custom-call | flops 27499999232 | bytes 1024 | tf_op jit(solution)/shard_map/attention_forward/pallas_call | solution.py:213
  22.4 1.9 %collective-permute-start.5 = (bf16[1024,128]{1,0:T(8,128)(2,1)}, bf16[1024,128]{1,0:T(8,128)(2,1)S(1)}, u32[]{:S(2)}, u32[]{:S(2)}) collective-permute-start(bf16[1024,128]{1,0:T(8,128)(2,1)} %get-tuple-element.87.own_att), channel_id=1, source_target_pairs={{0,2},{1,3},{2,0},{3,1},{4,6},{5,7},{6,4},{7,5},{8,10},{9,11},{10,... | collective-permute-start | bytes 786440 | tf_op jit(solution)/shard_map/ppermute | solution.py:702
  25.1 6.6 %collective-permute-done.5.a2 = bf16[1024,128]{1,0:T(8,128)(2,1)S(1)} collective-permute-done((bf16[1024,128]{1,0:T(8,128)(2,1)}, bf16[1024,128]{1,0:T(8,128)(2,1)S(1)}, u32[]{:S(2)}, u32[]{:S(2)}) %collective-permute-start.5) | collective-permute-done | bytes 262176 | tf_op jit(solution)/shard_map/ppermute | solution.py:702
  31.7 4.5 %collective-permute-done.6.a3 = bf16[1024,128]{1,0:T(8,128)(2,1)S(1)} collective-permute-done((bf16[1024,128]{1,0:T(8,128)(2,1)}, bf16[1024,128]{1,0:T(8,128)(2,1)S(1)}, u32[]{:S(2)}, u32[]{:S(2)}) %collective-permute-start.6) | collective-permute-done | bytes 262176 | tf_op jit(solution)/shard_map/ppermute | solution.py:702
  37.2 15.6 %feed.1 = (bf16[512,512]{1,0:T(8,128)(2,1)}, bf16[512,512]{1,0:T(8,128)(2,1)}, bf16[1024,512]{1,0:T(8,128)(2,1)}, f32[512,512]{1,0:T(8,128)}, f32[2,512]{1,0:T(2...) custom-call(s32[4]{0:T(128)} %pad_add_fusion.place, bf16[4,2,256,512]{3,2,1,0:T(8,128)(2,1)} %bitcast.44, ...), custom_call_target="tpu_custom_call" | custom-call | flops 14300000256 | bytes 1024 | tf_op jit(solution)/shard_map/feed/pallas_call | solution.py:535
  53.3 1.7 collective-permute-start.9
  55.0 0.8 collective-permute-done.18
  55.8 2.5 %add_convert_fusion.1 = bf16[8,128,512]{2,1,0:T(8,128)(2,1)} fusion(bf16[8,128,512]{2,1,0:T(8,128)(2,1)S(1)} %collective-permute-done.18, bf16[8,128,512]{2,1,0:T(8,128)(2,1)} %get-tuple-element.128), kind=kLoop, calls=%fused_computation.2 | loop fusion | flops 2097152 | bytes 3145728 | tf_op jit(solution)/shard_map/convert_element_type | solution.py:863
  58.3 9.7 %all-to-all-start = ((bf16[8,128,512]{2,1,0:T(8,128)(2,1)}), bf16[8,128,512]{2,1,0:T(8,128)(2,1)S(1)}, u32[]{:S(2)}, u32[]{:S(2)}) async-start(bf16[8,128,512]{2,1,0:T(8,128)(2,1)} %add_convert_fusion.1), calls=%async_computation | async-start | bytes 2097152 | tf_op jit(solution)/shard_map/all_to_all | solution.py:731
  68.0 0.8 copy-done.15
  68.8 5.1 %turn.1 = (bf16[512,512]{1,0:T(8,128)(2,1)}, f32[3,512]{1,0:T(4,128)}, bf16[512,128]{1,0:T(8,128)(2,1)}, bf16[512,128]{1,0:T(8,128)(2,1)}, bf16[512,128]{1,0:T(8...) custom-call(s32[4]{0:T(128)} %pad_add_fusion.place, ...), custom_call_target="tpu_custom_call" | custom-call | flops 65999998976 | bytes 1024 | tf_op jit(solution)/shard_map/turn/pallas_call | solution.py:600
  74.4 1.5 collective-permute-start.11
  76.0 1.5 collective-permute-start.17
  77.5 1.3 pad_maximum_fusion.6.sums
  79.7 1.3 collective-permute-done.11.d2
  81.0 1.9 %collective-permute-done.12.d3 = bf16[512,128]{1,0:T(8,128)(2,1)S(1)} collective-permute-done((bf16[512,128]{1,0:T(8,128)(2,1)}, bf16[512,128]{1,0:T(8,128)(2,1)S(1)}, u32[]{:S(2)}, u32[]{:S(2)}) %collective-permute-start.12) | collective-permute-done | bytes 131104 | tf_op jit(solution)/shard_map/ppermute | solution.py:702
  83.0 0.6 copy-done.24
  83.6 22.2 %attention_backward.1 = (bf16[336,512]{1,0:T(8,128)(2,1)}, bf16[320,512]{1,0:T(8,128)(2,1)}, bf16[16,512]{1,0:T(8,128)(2,1)}, bf16[1024,512]{1,0:T(8,128)(2,1)}, bf16[1024,512]{1,0:T(8,128)(2,1)}) custom-call(s32[1]{0:T(128)S(6)} %copy.48.kind, s32[4]{0:T(128)} %pad_add_fusion.place, bf16[2048,4096]{1,0:T(8,128)(2,1)} %get-tuple-element.84.p, ...), custom_call_target="tpu_custom_call" | custom-call | flops 8800000000 | bytes 1024 | tf_op jit(solution)/shard_map/attention_backward/pallas_call | solution.py:402
  105.8 3.3 %collective-permute-done.15 = bf16[128,512]{1,0:T(8,128)(2,1)S(1)} collective-permute-done((bf16[128,512]{1,0:T(8,128)(2,1)}, bf16[128,512]{1,0:T(8,128)(2,1)S(1)}, u32[]{:S(2)}, u32[]{:S(2)}) %collective-permute-start.15) | collective-permute-done | bytes 131104 | tf_op jit(solution)/shard_map/ppermute | solution.py:702
  109.1 1.2 collective-permute-done.16
  110.9 0.6 collective-permute-start.20
  111.6 1.2 broadcast_multiply_fusion.1
  112.7 1.8 %add_convert_fusion.3 = bf16[336,512]{1,0:T(8,128)(2,1)} fusion(f32[128,512]{1,0:T(8,128)S(1)} %get-tuple-element.162, bf16[336,512]{1,0:T(8,128)(2,1)} %get-tuple-element.135), kind=kLoop, calls=%fused_computation.5 | loop fusion | flops 516096 | bytes 950272 | tf_op jit(solution)/shard_map/convert_element_type | solution.py:889
  114.5 1.0 add_convert_fusion.2
  115.7 3.0 %collective-permute-start.32 = (bf16[128,512]{1,0:T(8,128)(2,1)S(1)}, bf16[128,512]{1,0:T(8,128)(2,1)S(1)}, u32[]{:S(2)}, u32[]{:S(2)}) collective-permute-start(bf16[128,512]{1,0:T(8,128)(2,1)S(1)} %reduce_sum.12), channel_id=1, source_target_pairs={{0,16},{4,20},{8,24},{12,28},{16,0},{20,4},{24,8},{28,12},{1,17},{... | collective-permute-start | bytes 393224 | tf_op jit(solution)/shard_map/ppermute | solution.py:702
  118.6 6.4 %collective-permute-start.19 = (bf16[336,512]{1,0:T(8,128)(2,1)}, bf16[336,512]{1,0:T(8,128)(2,1)S(1)}, u32[]{:S(2)}, u32[]{:S(2)}) collective-permute-start(bf16[336,512]{1,0:T(8,128)(2,1)} %add_convert_fusion.3), channel_id=1, source_target_pairs={{0,4},{4,0},{8,12},{12,8},{16,20},{20,16},{24,28},{28,24},{1,5},{5... | collective-permute-start | bytes 1032200 | tf_op jit(solution)/shard_map/ppermute | solution.py:702
  125.0 1.5 collective-permute-start.21
  126.6 1.3 collective-permute-start.33
  128.0 1.8 %add_convert_fusion.m0 = bf16[1024,512]{1,0:T(8,128)(2,1)S(1)} fusion(bf16[1024,512]{1,0:T(8,128)(2,1)} %collective-permute-done.17, bf16[1024,512]{1,0:T(8,128)(2,1)} %get-tuple-element.127), kind=kLoop, calls=%fused_computation.1 | loop fusion | flops 2097152 | bytes 3145728 | tf_op jit(solution)/shard_map/convert_element_type | solution.py:899
  129.9 4.4 %collective-permute-done.33 = bf16[256,512]{1,0:T(8,128)(2,1)S(1)} collective-permute-done((bf16[256,512]{1,0:T(8,128)(2,1)S(1)}, bf16[256,512]{1,0:T(8,128)(2,1)S(1)}, u32[]{:S(2)}, u32[]{:S(2)}) %collective-permute-start.33) | collective-permute-done | bytes 262176 | tf_op jit(solution)/shard_map/ppermute | solution.py:702
  134.3 4.4 %collective-permute-done.21.got = bf16[512,512]{1,0:T(8,128)(2,1)S(1)} collective-permute-done((bf16[512,512]{1,0:T(8,128)(2,1)}, bf16[512,512]{1,0:T(8,128)(2,1)S(1)}, u32[]{:S(2)}, u32[]{:S(2)}) %collective-permute-start.21) | collective-permute-done | bytes 524320 | tf_op jit(solution)/shard_map/ppermute | solution.py:702
  139.1 1.3 collective-permute-start.22
  140.6 2.0 %collective-permute-start.34 = (bf16[512,512]{1,0:T(8,128)(2,1)S(1)}, bf16[512,512]{1,0:T(8,128)(2,1)S(1)}, u32[]{:S(2)}, u32[]{:S(2)}) collective-permute-start(bf16[512,512]{1,0:T(8,128)(2,1)S(1)} %pad_maximum_fusion.1), channel_id=1, source_target_pairs={{0,4},{4,0},{8,12},{12,8},{16,20},{20,16},{24,28},{28,24},{1,5},{5... | collective-permute-start | bytes 1572872 | tf_op jit(solution)/shard_map/ppermute | solution.py:702
  142.6 2.0 %collective-permute-done.22 = bf16[176,512]{1,0:T(8,128)(2,1)S(1)} collective-permute-done((bf16[176,512]{1,0:T(8,128)(2,1)S(1)}, bf16[176,512]{1,0:T(8,128)(2,1)S(1)}, u32[]{:S(2)}, u32[]{:S(2)}) %collective-permute-start.22) | collective-permute-done | bytes 180256 | tf_op jit(solution)/shard_map/ppermute | solution.py:702
  144.8 2.6 %collective-permute-start.23 = (bf16[176,512]{1,0:T(8,128)(2,1)S(1)}, bf16[176,512]{1,0:T(8,128)(2,1)S(1)}, u32[]{:S(2)}, u32[]{:S(2)}) collective-permute-start(bf16[176,512]{1,0:T(8,128)(2,1)S(1)} %pad_maximum_fusion.5), channel_id=1, source_target_pairs={{0,16},{4,20},{8,24},{12,28},{16,0},{20,4},{24,8},{28,12},{1,17},{... | collective-permute-start | bytes 540680 | tf_op jit(solution)/shard_map/ppermute | solution.py:702
  147.4 3.9 %close.1.g0 = bf16[512,512]{1,0:T(8,128)(2,1)} custom-call(s32[4]{0:T(128)} %pad_add_fusion.place, bf16[1024,512]{1,0:T(8,128)(2,1)} %get-tuple-element.136.keep0.keep1, bf16[1024,512]{1,0:T(8,128)(2,1)} %get-tuple-element.136.keep0.keep1, bf16[1024,512]{1,0:T(8,128)(2,1)} %copy-done.3, bf16[1024,512]{1,0:T(8,128)(2,1)} %copy-done.3, ...), custom_call_target="tpu_custom_call" | custom-call | flops 2200000000 | bytes 1024 | tf_op jit(solution)/shard_map/close/pallas_call | solution.py:643
  151.4 1.5 collective-permute-start.28
  152.9 0.9 collective-permute-done.23
  155.1 4.6 %collective-permute-done.24 = bf16[160,512]{1,0:T(8,128)(2,1)S(1)} collective-permute-done((bf16[160,512]{1,0:T(8,128)(2,1)S(1)}, bf16[160,512]{1,0:T(8,128)(2,1)S(1)}, u32[]{:S(2)}, u32[]{:S(2)}) %collective-permute-start.24) | collective-permute-done | bytes 163872 | tf_op jit(solution)/shard_map/ppermute | solution.py:702
  159.8 1.6 fusion.6
  161.4 2.0 %collective-permute-start.25 = (bf16[320,512]{1,0:T(8,128)(2,1)S(1)}, bf16[320,512]{1,0:T(8,128)(2,1)S(1)}, u32[]{:S(2)}, u32[]{:S(2)}) collective-permute-start(bf16[320,512]{1,0:T(8,128)(2,1)S(1)} %pad_maximum_fusion.2), channel_id=1, source_target_pairs={{0,4},{4,0},{8,12},{12,8},{16,20},{20,16},{24,28},{28,24},{1,5},{5... | collective-permute-start | bytes 983048 | tf_op jit(solution)/shard_map/ppermute | solution.py:702
  163.7 1.6 collective-permute-start.31
  166.4 1.1 collective-permute-done.31
  168.2 2.7 %collect.1 = (bf16[2048,512]{1,0:T(8,128)(2,1)}, bf16[2048,512]{1,0:T(8,128)(2,1)}) custom-call(s32[4]{0:T(128)S(1)} %copy-done.1, bf16[1024,512]{1,0:T(8,128)(2,1)S(1)} %add_convert_fusion.m0, bf16[1024,512]{1,0:T(8,128)(2,1)S(1)} %collective-permute-done.26.m1, bf16[512,512]{1,0:T(8,128)(2,1)S(1)} %copy-done, ...), custom_call_target="tpu_custom_call" | custom-call | flops 3300000000 | bytes 1024 | tf_op jit(solution)/shard_map/collect/pallas_call | solution.py:687
  170.8 0.9 collective-permute-done.25
  172.1 1.0 fusion.7
  173.1 0.7 slice.128
  (126 shorter events, 10.1 us)
Async XLA Ops:
  0.7 21.1 %collective-permute-start = (bf16[128,512]{1,0:T(8,128)(2,1)}, bf16[128,512]{1,0:T(8,128)(2,1)S(1)}, u32[]{:S(2)}, u32[]{:S(2)}) collective-permute-start(bf16[128,512]{1,0:T(8,128)(2,1)} %w0.1), channel_id=1, source_target_pairs={{0,1},{1,0},{2,3},{3,2},{4,5},{5,4},{6,7},{7,6},{8,9},{9,8},{10,11... | collective-permute-start | bytes 393224 | tf_op jit(solution)/shard_map/ppermute | solution.py:702
  1.2 20.6 %collective-permute-start.1 = (bf16[128,512]{1,0:T(8,128)(2,1)}, bf16[128,512]{1,0:T(8,128)(2,1)S(1)}, u32[]{:S(2)}, u32[]{:S(2)}) collective-permute-start(bf16[128,512]{1,0:T(8,128)(2,1)} %w0.1), channel_id=1, source_target_pairs={{0,2},{1,3},{2,0},{3,1},{4,6},{5,7},{6,4},{7,5},{8,10},{9,11},{10,... | collective-permute-start | bytes 393224 | tf_op jit(solution)/shard_map/ppermute | solution.py:702
  3.8 18.0 %collective-permute-start.2 = (bf16[128,512]{1,0:T(8,128)(2,1)}, bf16[128,512]{1,0:T(8,128)(2,1)S(1)}, u32[]{:S(2)}, u32[]{:S(2)}) collective-permute-start(bf16[128,512]{1,0:T(8,128)(2,1)} %w0.1), channel_id=1, source_target_pairs={{0,3},{1,2},{2,1},{3,0},{4,7},{5,6},{6,5},{7,4},{8,11},{9,10},{10,... | collective-permute-start | bytes 393224 | tf_op jit(solution)/shard_map/ppermute | solution.py:702
  3.8 17.9 %collective-permute-start.3 = (f32[1,512]{1,0:T(1,128)}, f32[1,512]{1,0:T(1,128)S(1)}, u32[]{:S(2)}, u32[]{:S(2)}) collective-permute-start(f32[1,512]{1,0:T(1,128)} %bitcast.66), channel_id=1, source_target_pairs={{0,1},{1,0},{2,3},{3,2},{4,5},{5,4},{6,7},{7,6},{8,9},{9,8},{10,11... | collective-permute-start | bytes 6152 | tf_op jit(solution)/shard_map/ppermute | solution.py:702
  4.6 17.1 %copy-start.11 = (bf16[512,512]{1,0:T(8,128)(2,1)S(1)}, bf16[512,512]{1,0:T(8,128)(2,1)}, u32[]{:S(2)}) copy-start(bf16[512,512]{1,0:T(8,128)(2,1)} %i0.1) | copy-start | bytes 1572868
  4.6 17.6 %copy-start.12 = (bf16[512,512]{1,0:T(8,128)(2,1)S(1)}, bf16[512,512]{1,0:T(8,128)(2,1)}, u32[]{:S(2)}) copy-start(bf16[512,512]{1,0:T(8,128)(2,1)} %u0.1) | copy-start | bytes 1572868
  21.7 14.5 %copy-start.25 = (f32[1,512]{1,0:T(1,128)}, f32[1,512]{1,0:T(1,128)S(1)}, u32[]{:S(2)}) copy-start(f32[1,512]{1,0:T(1,128)S(1)} %collective-permute-done.3.b1) | copy-start | bytes 6148
  21.7 14.5 %copy-start.19 = (bf16[128,512]{1,0:T(8,128)(2,1)}, bf16[128,512]{1,0:T(8,128)(2,1)S(1)}, u32[]{:S(2)}) copy-start(bf16[128,512]{1,0:T(8,128)(2,1)S(1)} %collective-permute-done.w1) | copy-start | bytes 393220
  21.7 14.5 %copy-start.20 = (bf16[128,512]{1,0:T(8,128)(2,1)}, bf16[128,512]{1,0:T(8,128)(2,1)S(1)}, u32[]{:S(2)}) copy-start(bf16[128,512]{1,0:T(8,128)(2,1)S(1)} %collective-permute-done.1.w2) | copy-start | bytes 393220
  21.8 14.5 %copy-start.21 = (bf16[128,512]{1,0:T(8,128)(2,1)}, bf16[128,512]{1,0:T(8,128)(2,1)S(1)}, u32[]{:S(2)}) copy-start(bf16[128,512]{1,0:T(8,128)(2,1)S(1)} %collective-permute-done.2.w3) | copy-start | bytes 393220
  21.8 14.4 %collective-permute-start.7 = (bf16[512,512]{1,0:T(8,128)(2,1)S(1)}, bf16[512,512]{1,0:T(8,128)(2,1)S(1)}, u32[]{:S(2)}, u32[]{:S(2)}) collective-permute-start(bf16[512,512]{1,0:T(8,128)(2,1)S(1)} %copy-done.11), channel_id=1, source_target_pairs={{0,1},{1,0},{2,3},{3,2},{4,5},{5,4},{6,7},{7,6},{8,9},{9,8},{10,11... | collective-permute-start | bytes 1572872 | tf_op jit(solution)/shard_map/ppermute | solution.py:702
  22.2 14.0 %collective-permute-start.8 = (bf16[512,512]{1,0:T(8,128)(2,1)S(1)}, bf16[512,512]{1,0:T(8,128)(2,1)S(1)}, u32[]{:S(2)}, u32[]{:S(2)}) collective-permute-start(bf16[512,512]{1,0:T(8,128)(2,1)S(1)} %copy-done.12), channel_id=1, source_target_pairs={{0,1},{1,0},{2,3},{3,2},{4,5},{5,4},{6,7},{7,6},{8,9},{9,8},{10,11... | collective-permute-start | bytes 1572872 | tf_op jit(solution)/shard_map/ppermute | solution.py:702
  22.4 9.3 %collective-permute-start.5 = (bf16[1024,128]{1,0:T(8,128)(2,1)}, bf16[1024,128]{1,0:T(8,128)(2,1)S(1)}, u32[]{:S(2)}, u32[]{:S(2)}) collective-permute-start(bf16[1024,128]{1,0:T(8,128)(2,1)} %get-tuple-element.87.own_att), channel_id=1, source_target_pairs={{0,2},{1,3},{2,0},{3,1},{4,6},{5,7},{6,4},{7,5},{8,10},{9,11},{10,... | collective-permute-start | bytes 786440 | tf_op jit(solution)/shard_map/ppermute | solution.py:702
  24.3 7.4 %collective-permute-start.4 = (bf16[1024,128]{1,0:T(8,128)(2,1)}, bf16[1024,128]{1,0:T(8,128)(2,1)S(1)}, u32[]{:S(2)}, u32[]{:S(2)}) collective-permute-start(bf16[1024,128]{1,0:T(8,128)(2,1)} %get-tuple-element.88), channel_id=1, source_target_pairs={{0,1},{1,0},{2,3},{3,2},{4,5},{5,4},{6,7},{7,6},{8,9},{9,8},{10,11... | collective-permute-start | bytes 786440 | tf_op jit(solution)/shard_map/ppermute | solution.py:702
  24.3 11.9 %collective-permute-start.6 = (bf16[1024,128]{1,0:T(8,128)(2,1)}, bf16[1024,128]{1,0:T(8,128)(2,1)S(1)}, u32[]{:S(2)}, u32[]{:S(2)}) collective-permute-start(bf16[1024,128]{1,0:T(8,128)(2,1)} %get-tuple-element.88), channel_id=1, source_target_pairs={{0,3},{1,2},{2,1},{3,0},{4,7},{5,6},{6,5},{7,4},{8,11},{9,10},{10,... | collective-permute-start | bytes 786440 | tf_op jit(solution)/shard_map/ppermute | solution.py:702
  52.8 2.9 %collective-permute-start.18 = (bf16[8,128,512]{2,1,0:T(8,128)(2,1)}, bf16[8,128,512]{2,1,0:T(8,128)(2,1)S(1)}, u32[]{:S(2)}, u32[]{:S(2)}) collective-permute-start(bf16[8,128,512]{2,1,0:T(8,128)(2,1)} %get-tuple-element.129), channel_id=1, source_target_pairs={{0,1},{1,0},{2,3},{3,2},{4,5},{5,4},{6,7},{7,6},{8,9},{9,8},{10,11... | collective-permute-start | bytes 3145736 | tf_op jit(solution)/shard_map/ppermute | solution.py:702
  53.3 14.7 %collective-permute-start.9 = (bf16[512,512]{1,0:T(8,128)(2,1)}, bf16[512,512]{1,0:T(8,128)(2,1)S(1)}, u32[]{:S(2)}, u32[]{:S(2)}) collective-permute-start(bf16[512,512]{1,0:T(8,128)(2,1)} %get-tuple-element.98), channel_id=1, source_target_pairs={{0,2},{1,3},{2,0},{3,1},{4,6},{5,7},{6,4},{7,5},{8,10},{9,11},{10,... | collective-permute-start | bytes 1572872 | tf_op jit(solution)/shard_map/ppermute | solution.py:702
  58.3 52.0 %all-to-all-start = ((bf16[8,128,512]{2,1,0:T(8,128)(2,1)}), bf16[8,128,512]{2,1,0:T(8,128)(2,1)S(1)}, u32[]{:S(2)}, u32[]{:S(2)}) async-start(bf16[8,128,512]{2,1,0:T(8,128)(2,1)} %add_convert_fusion.1), calls=%async_computation | async-start | bytes 2097152 | tf_op jit(solution)/shard_map/all_to_all | solution.py:731
  73.9 2.1 %collective-permute-start.10 = (bf16[512,128]{1,0:T(8,128)(2,1)}, bf16[512,128]{1,0:T(8,128)(2,1)S(1)}, u32[]{:S(2)}, u32[]{:S(2)}) collective-permute-start(bf16[512,128]{1,0:T(8,128)(2,1)} %get-tuple-element.101), channel_id=1, source_target_pairs={{0,1},{1,0},{2,3},{3,2},{4,5},{5,4},{6,7},{7,6},{8,9},{9,8},{10,11... | collective-permute-start | bytes 393224 | tf_op jit(solution)/shard_map/ppermute | solution.py:702
  74.0 3.5 %collective-permute-start.13 = (f32[1,512]{1,0:T(1,128)S(1)}, f32[1,512]{1,0:T(1,128)S(1)}, u32[]{:S(2)}, u32[]{:S(2)}) collective-permute-start(f32[1,512]{1,0:T(1,128)S(1)} %slice.86), channel_id=1, source_target_pairs={{0,1},{1,0},{2,3},{3,2},{4,5},{5,4},{6,7},{7,6},{8,9},{9,8},{10,11... | collective-permute-start | bytes 6152 | tf_op jit(solution)/shard_map/ppermute | solution.py:702
  74.4 6.6 %collective-permute-start.11 = (bf16[512,128]{1,0:T(8,128)(2,1)}, bf16[512,128]{1,0:T(8,128)(2,1)S(1)}, u32[]{:S(2)}, u32[]{:S(2)}) collective-permute-start(bf16[512,128]{1,0:T(8,128)(2,1)} %get-tuple-element.102), channel_id=1, source_target_pairs={{0,2},{1,3},{2,0},{3,1},{4,6},{5,7},{6,4},{7,5},{8,10},{9,11},{10,... | collective-permute-start | bytes 393224 | tf_op jit(solution)/shard_map/ppermute | solution.py:702
  76.0 7.0 %collective-permute-start.12 = (bf16[512,128]{1,0:T(8,128)(2,1)}, bf16[512,128]{1,0:T(8,128)(2,1)S(1)}, u32[]{:S(2)}, u32[]{:S(2)}) collective-permute-start(bf16[512,128]{1,0:T(8,128)(2,1)} %get-tuple-element.103), channel_id=1, source_target_pairs={{0,3},{1,2},{2,1},{3,0},{4,7},{5,6},{6,5},{7,4},{8,11},{9,10},{10,... | collective-permute-start | bytes 393224 | tf_op jit(solution)/shard_map/ppermute | solution.py:702
  76.0 34.3 %collective-permute-start.17 = (bf16[1024,512]{1,0:T(8,128)(2,1)S(1)}, bf16[1024,512]{1,0:T(8,128)(2,1)}, u32[]{:S(2)}, u32[]{:S(2)}) collective-permute-start(bf16[1024,512]{1,0:T(8,128)(2,1)S(1)} %copy-done.4), channel_id=1, source_target_pairs={{0,2},{1,3},{2,0},{3,1},{4,6},{5,7},{6,4},{7,5},{8,10},{9,11},{10,... | collective-permute-start | bytes 3145736 | tf_op jit(solution)/shard_map/ppermute | solution.py:702
  78.8 27.0 %collective-permute-start.14 = (bf16[128,512]{1,0:T(8,128)(2,1)}, bf16[128,512]{1,0:T(8,128)(2,1)S(1)}, u32[]{:S(2)}, u32[]{:S(2)}) collective-permute-start(bf16[128,512]{1,0:T(8,128)(2,1)} %get-tuple-element.123), channel_id=1, source_target_pairs={{0,1},{1,0},{2,3},{3,2},{4,5},{5,4},{6,7},{7,6},{8,9},{9,8},{10,11... | collective-permute-start | bytes 393224 | tf_op jit(solution)/shard_map/ppermute | solution.py:702
  79.2 29.9 %collective-permute-start.15 = (bf16[128,512]{1,0:T(8,128)(2,1)}, bf16[128,512]{1,0:T(8,128)(2,1)S(1)}, u32[]{:S(2)}, u32[]{:S(2)}) collective-permute-start(bf16[128,512]{1,0:T(8,128)(2,1)} %get-tuple-element.124), channel_id=1, source_target_pairs={{0,2},{1,3},{2,0},{3,1},{4,6},{5,7},{6,4},{7,5},{8,10},{9,11},{10,... | collective-permute-start | bytes 393224 | tf_op jit(solution)/shard_map/ppermute | solution.py:702
  81.0 29.3 %collective-permute-start.16 = (bf16[128,512]{1,0:T(8,128)(2,1)}, bf16[128,512]{1,0:T(8,128)(2,1)S(1)}, u32[]{:S(2)}, u32[]{:S(2)}) collective-permute-start(bf16[128,512]{1,0:T(8,128)(2,1)} %get-tuple-element.125), channel_id=1, source_target_pairs={{0,3},{1,2},{2,1},{3,0},{4,7},{5,6},{6,5},{7,4},{8,11},{9,10},{10,... | collective-permute-start | bytes 393224 | tf_op jit(solution)/shard_map/ppermute | solution.py:702
  105.8 8.7 %copy-start.2 = (bf16[1024,512]{1,0:T(8,128)(2,1)S(1)}, bf16[1024,512]{1,0:T(8,128)(2,1)}, u32[]{:S(2)}) copy-start(bf16[1024,512]{1,0:T(8,128)(2,1)} %get-tuple-element.136.keep0.keep1) | copy-start | bytes 3145732
  110.9 3.6 %collective-permute-start.20 = (bf16[1024,512]{1,0:T(8,128)(2,1)}, bf16[1024,512]{1,0:T(8,128)(2,1)S(1)}, u32[]{:S(2)}, u32[]{:S(2)}) collective-permute-start(bf16[1024,512]{1,0:T(8,128)(2,1)} %get-tuple-element.137), channel_id=1, source_target_pairs={{0,1},{1,0},{2,3},{3,2},{4,5},{5,4},{6,7},{7,6},{8,9},{9,8},{10,11... | collective-permute-start | bytes 3145736 | tf_op jit(solution)/shard_map/ppermute | solution.py:702
  114.5 15.3 %copy-start.3 = (bf16[1024,512]{1,0:T(8,128)(2,1)}, bf16[1024,512]{1,0:T(8,128)(2,1)S(1)}, u32[]{:S(2)}) copy-start(bf16[1024,512]{1,0:T(8,128)(2,1)S(1)} %collective-permute-done.20.near0.near1) | copy-start | bytes 3145732
  115.7 10.8 %collective-permute-start.32 = (bf16[128,512]{1,0:T(8,128)(2,1)S(1)}, bf16[128,512]{1,0:T(8,128)(2,1)S(1)}, u32[]{:S(2)}, u32[]{:S(2)}) collective-permute-start(bf16[128,512]{1,0:T(8,128)(2,1)S(1)} %reduce_sum.12), channel_id=1, source_target_pairs={{0,16},{4,20},{8,24},{12,28},{16,0},{20,4},{24,8},{28,12},{1,17},{... | collective-permute-start | bytes 393224 | tf_op jit(solution)/shard_map/ppermute | solution.py:702
  118.6 15.7 %collective-permute-start.19 = (bf16[336,512]{1,0:T(8,128)(2,1)}, bf16[336,512]{1,0:T(8,128)(2,1)S(1)}, u32[]{:S(2)}, u32[]{:S(2)}) collective-permute-start(bf16[336,512]{1,0:T(8,128)(2,1)} %add_convert_fusion.3), channel_id=1, source_target_pairs={{0,4},{4,0},{8,12},{12,8},{16,20},{20,16},{24,28},{28,24},{1,5},{5... | collective-permute-start | bytes 1032200 | tf_op jit(solution)/shard_map/ppermute | solution.py:702
  125.0 13.8 %collective-permute-start.21 = (bf16[512,512]{1,0:T(8,128)(2,1)}, bf16[512,512]{1,0:T(8,128)(2,1)S(1)}, u32[]{:S(2)}, u32[]{:S(2)}) collective-permute-start(bf16[512,512]{1,0:T(8,128)(2,1)} %bitcast.50), channel_id=1, source_target_pairs={{0,2},{1,3},{2,0},{3,1},{4,6},{5,7},{6,4},{7,5},{8,10},{9,11},{10,... | collective-permute-start | bytes 1572872 | tf_op jit(solution)/shard_map/ppermute | solution.py:702
  126.6 12.3 %copy-start.9 = (bf16[16,512]{1,0:T(8,128)(2,1)S(1)}, bf16[16,512]{1,0:T(8,128)(2,1)}, u32[]{:S(2)}) copy-start(bf16[16,512]{1,0:T(8,128)(2,1)} %get-tuple-element.139) | copy-start | bytes 49156
  126.6 12.3 %copy-start.6 = (bf16[320,512]{1,0:T(8,128)(2,1)S(1)}, bf16[320,512]{1,0:T(8,128)(2,1)}, u32[]{:S(2)}) copy-start(bf16[320,512]{1,0:T(8,128)(2,1)} %get-tuple-element.130) | copy-start | bytes 983044
  126.6 7.7 %collective-permute-start.33 = (bf16[256,512]{1,0:T(8,128)(2,1)S(1)}, bf16[256,512]{1,0:T(8,128)(2,1)S(1)}, u32[]{:S(2)}, u32[]{:S(2)}) collective-permute-start(bf16[256,512]{1,0:T(8,128)(2,1)S(1)} %pad_maximum_fusion.3), channel_id=1, source_target_pairs={{0,8},{4,12},{8,0},{12,4},{16,24},{20,28},{24,16},{28,20},{1,9},{5... | collective-permute-start | bytes 786440 | tf_op jit(solution)/shard_map/ppermute | solution.py:702
  129.8 38.3 %collective-permute-start.26 = (bf16[1024,512]{1,0:T(8,128)(2,1)S(1)}, bf16[1024,512]{1,0:T(8,128)(2,1)S(1)}, u32[]{:S(2)}, u32[]{:S(2)}) collective-permute-start(bf16[1024,512]{1,0:T(8,128)(2,1)S(1)} %add_convert_fusion.m0), channel_id=1, source_target_pairs={{0,1},{1,0},{2,3},{3,2},{4,5},{5,4},{6,7},{7,6},{8,9},{9,8},{10,11... | collective-permute-start | bytes 3145736 | tf_op jit(solution)/shard_map/ppermute | solution.py:702
  139.1 5.6 %collective-permute-start.22 = (bf16[176,512]{1,0:T(8,128)(2,1)S(1)}, bf16[176,512]{1,0:T(8,128)(2,1)S(1)}, u32[]{:S(2)}, u32[]{:S(2)}) collective-permute-start(bf16[176,512]{1,0:T(8,128)(2,1)S(1)} %pad_maximum_fusion.4), channel_id=1, source_target_pairs={{0,8},{4,12},{8,0},{12,4},{16,24},{20,28},{24,16},{28,20},{1,9},{5... | collective-permute-start | bytes 540680 | tf_op jit(solution)/shard_map/ppermute | solution.py:702
  140.6 13.7 %collective-permute-start.34 = (bf16[512,512]{1,0:T(8,128)(2,1)S(1)}, bf16[512,512]{1,0:T(8,128)(2,1)S(1)}, u32[]{:S(2)}, u32[]{:S(2)}) collective-permute-start(bf16[512,512]{1,0:T(8,128)(2,1)S(1)} %pad_maximum_fusion.1), channel_id=1, source_target_pairs={{0,4},{4,0},{8,12},{12,8},{16,20},{20,16},{24,28},{28,24},{1,5},{5... | collective-permute-start | bytes 1572872 | tf_op jit(solution)/shard_map/ppermute | solution.py:702
  144.8 9.0 %collective-permute-start.23 = (bf16[176,512]{1,0:T(8,128)(2,1)S(1)}, bf16[176,512]{1,0:T(8,128)(2,1)S(1)}, u32[]{:S(2)}, u32[]{:S(2)}) collective-permute-start(bf16[176,512]{1,0:T(8,128)(2,1)S(1)} %pad_maximum_fusion.5), channel_id=1, source_target_pairs={{0,16},{4,20},{8,24},{12,28},{16,0},{20,4},{24,8},{28,12},{1,17},{... | collective-permute-start | bytes 540680 | tf_op jit(solution)/shard_map/ppermute | solution.py:702
  151.4 12.1 %collective-permute-start.28 = (bf16[512,512]{1,0:T(8,128)(2,1)}, bf16[512,512]{1,0:T(8,128)(2,1)S(1)}, u32[]{:S(2)}, u32[]{:S(2)}) collective-permute-start(bf16[512,512]{1,0:T(8,128)(2,1)} %close.1.g0), channel_id=1, source_target_pairs={{0,2},{1,3},{2,0},{3,1},{4,6},{5,7},{6,4},{7,5},{8,10},{9,11},{10,... | collective-permute-start | bytes 1572872 | tf_op jit(solution)/shard_map/ppermute | solution.py:702
  152.9 15.3 %collective-permute-start.27 = (bf16[512,512]{1,0:T(8,128)(2,1)}, bf16[512,512]{1,0:T(8,128)(2,1)S(1)}, u32[]{:S(2)}, u32[]{:S(2)}) collective-permute-start(bf16[512,512]{1,0:T(8,128)(2,1)} %close.1.g0), channel_id=1, source_target_pairs={{0,1},{1,0},{2,3},{3,2},{4,5},{5,4},{6,7},{7,6},{8,9},{9,8},{10,11... | collective-permute-start | bytes 1572872 | tf_op jit(solution)/shard_map/ppermute | solution.py:702
  153.8 5.8 %collective-permute-start.24 = (bf16[160,512]{1,0:T(8,128)(2,1)S(1)}, bf16[160,512]{1,0:T(8,128)(2,1)S(1)}, u32[]{:S(2)}, u32[]{:S(2)}) collective-permute-start(bf16[160,512]{1,0:T(8,128)(2,1)S(1)} %fusion.1), channel_id=1, source_target_pairs={{0,8},{4,12},{8,0},{12,4},{16,24},{20,28},{24,16},{28,20},{1,9},{5... | collective-permute-start | bytes 491528 | tf_op jit(solution)/shard_map/ppermute | solution.py:702
  159.7 4.0 %collective-permute-start.30 = (f32[5,512]{1,0:T(8,128)S(1)}, f32[5,512]{1,0:T(8,128)S(1)}, u32[]{:S(2)}, u32[]{:S(2)}) collective-permute-start(f32[5,512]{1,0:T(8,128)S(1)} %slice.119), channel_id=1, source_target_pairs={{0,1},{1,0},{2,3},{3,2},{4,5},{5,4},{6,7},{7,6},{8,9},{9,8},{10,11... | collective-permute-start | bytes 30728 | tf_op jit(solution)/shard_map/ppermute | solution.py:702
  159.8 8.3 %copy-start = (bf16[512,512]{1,0:T(8,128)(2,1)S(1)}, bf16[512,512]{1,0:T(8,128)(2,1)}, u32[]{:S(2)}) copy-start(bf16[512,512]{1,0:T(8,128)(2,1)} %close.1.g0) | copy-start | bytes 1572868
  159.8 8.3 %copy-start.1 = (s32[4]{0:T(128)S(1)}, s32[4]{0:T(128)}, u32[]{:S(2)}) copy-start(s32[4]{0:T(128)} %pad_add_fusion.place) | copy-start | bytes 52
  161.4 10.4 %collective-permute-start.25 = (bf16[320,512]{1,0:T(8,128)(2,1)S(1)}, bf16[320,512]{1,0:T(8,128)(2,1)S(1)}, u32[]{:S(2)}, u32[]{:S(2)}) collective-permute-start(bf16[320,512]{1,0:T(8,128)(2,1)S(1)} %pad_maximum_fusion.2), channel_id=1, source_target_pairs={{0,4},{4,0},{8,12},{12,8},{16,20},{20,16},{24,28},{28,24},{1,5},{5... | collective-permute-start | bytes 983048 | tf_op jit(solution)/shard_map/ppermute | solution.py:702
  163.5 4.7 %collective-permute-start.29 = (bf16[512,512]{1,0:T(8,128)(2,1)S(1)}, bf16[512,512]{1,0:T(8,128)(2,1)S(1)}, u32[]{:S(2)}, u32[]{:S(2)}) collective-permute-start(bf16[512,512]{1,0:T(8,128)(2,1)S(1)} %collective-permute-done.28.g2), channel_id=1, source_target_pairs={{0,1},{1,0},{2,3},{3,2},{4,5},{5,4},{6,7},{7,6},{8,9},{9,8},{10,11... | collective-permute-start | bytes 1572872 | tf_op jit(solution)/shard_map/ppermute | solution.py:702
  163.7 3.8 %collective-permute-start.31 = (f32[5,512]{1,0:T(8,128)S(1)}, f32[5,512]{1,0:T(8,128)S(1)}, u32[]{:S(2)}, u32[]{:S(2)}) collective-permute-start(f32[5,512]{1,0:T(8,128)S(1)} %slice_add_fusion.7), channel_id=1, source_target_pairs={{0,2},{1,3},{2,0},{3,1},{4,6},{5,7},{6,4},{7,5},{8,10},{9,11},{10,... | collective-permute-start | bytes 30728 | tf_op jit(solution)/shard_map/ppermute | solution.py:702
  (14 other events, 38.2 us)

commit v6 on v5

--- a/solution.py
+++ b/solution.py
@@ -492,7 +492,7 @@
         out[...] = mixed.astype(bf16)
         sums = jnp.concatenate(sums, axis=0)
         low = place[2] == 0
-        res_own[...] = jnp.where(low, residual[:own], residual[own:])
+        res_own[...] = jnp.where(low, residual[:own], residual[own:]).astype(bf16)
         back_keep[...] = jnp.where(low, back[:own], back[own:]).astype(bf16)
         back_send[...] = jnp.where(low, back[own:], back[:own]).astype(bf16)
 
@@ -553,7 +553,7 @@
         ),
         out_shape=[
             shape((2 * own, width), bf16), shape((2 * own, width), bf16),
-            shape((rows, width), bf16), shape((2 * own, width), f32), shape((2, share), f32),
+            shape((rows, width), bf16), shape((2 * own, width), bf16), shape((2, share), f32),
             shape(grad_shape, bf16), shape(grad_shape, bf16),
         ],
         compiler_params=params(),
@@ -569,7 +569,7 @@
     rows, width = keep.shape
     back = keep[...].astype(f32) + got[...].astype(f32)
     c = cot[...].reshape(rows, width).astype(f32)
-    normed, scale = norm_parts(residual[...])
+    normed, scale = norm_parts(residual[...].astype(f32))
     fold = lambda values: jnp.sum(values, axis=0, keepdims=True)
     sums_out[...] = jnp.concatenate([fold(back * normed), fold(back), fold(c)], axis=0)
     e = back * gain[...]

time: 175 us -> 176 us (level)
  starting transfers between devices: 47.2 us -> 34.5 us
  Pallas kernels: 66.5 us -> 78.3 us
  waiting for transfers between devices: 38.1 us -> 40.6 us
    ppermute x35, starting transfers between devices: 37.5 us -> 28.4 us  [swap(): return lax.ppermute(value, axis, [(i, i ^ mask) for i in range(size)])]
    pallas_call x1, Pallas kernels: 22.2 us -> 28.6 us  [attention_backward(): pl.pallas_call(functools.partial(backward_body, count, block, length // 2...]
    pallas_call x1, Pallas kernels: 17 us -> 22.7 us  [attention_forward(): pl.pallas_call(functools.partial(forward_body, block, length // 2), grid=...]
    all_to_all x1, starting transfers between devices: 9.7 us -> 6.03 us  [exchange(): lax.all_to_all(value, 'dp', split_axis=0, concat_axis=0, tiled=True, axis...]
    ppermute x35, waiting for transfers between devices: 38.1 us -> 40.6 us  [swap(): return lax.ppermute(value, axis, [(i, i ^ mask) for i in range(size)])]
  transfers between devices with their start and end apart: 36 -> 36, of which waited for: 14 -> 14; matrix products, arithmetic and copies ran while one was open for 8% -> 8% of each run, Pallas kernels for 29% -> 36%
where the time goes in v6:
time: 176 us
  Pallas kernels  78.3 us (44%)
  waiting for transfers between devices  40.6 us (23%)
  starting transfers between devices  34.5 us (20%)
  other arithmetic  11.9 us (7%)
  local copies, waits for them, and re-layouts  8.34 us (5%)
  between operations  1.94 us (1%)
    ppermute x35, waiting for transfers between devices, swap(): return lax.ppermute(value, axis, [(i, i ^ mask) for i in range(size)])  40.6 us
    pallas_call x1, Pallas kernels, attention_backward(): pl.pallas_call(functools.partial(backward_body, count, block, length // 2...  28.6 us
    ppermute x35, starting transfers between devices, swap(): return lax.ppermute(value, axis, [(i, i ^ mask) for i in range(size)])  28.4 us
    pallas_call x1, Pallas kernels, attention_forward(): pl.pallas_call(functools.partial(forward_body, block, length // 2), grid=...  22.7 us
    pallas_call x1, Pallas kernels, feed(): pl.pallas_call(feed_body, grid_spec=pltpu.PrefetchScalarGridSpec(num_scal...  15.4 us
    all_to_all x1, starting transfers between devices, exchange(): lax.all_to_all(value, 'dp', split_axis=0, concat_axis=0, tiled=True, axis...  6.03 us
    pallas_call x1, Pallas kernels, turn(): pl.pallas_call(turn_body, grid_spec=pltpu.PrefetchScalarGridSpec(num_scal...  5.03 us
    pallas_call x1, Pallas kernels, close(): pl.pallas_call(close_body, grid_spec=pltpu.PrefetchScalarGridSpec(num_sca...  3.95 us
  transfers between devices with their start and end apart: 36, of which 14 were waited for; matrix products, arithmetic and copies ran while one was open for 8% of the time, Pallas kernels for 36%

profile of v6, /device:TPU:0, one launch (start us, length us, event | category | flops | bytes accessed | tf_op | source)
XLA Modules:
  0.0 175.6 jit_solution(12024868677332913811)
XLA Ops:
  1.2 2.6 %collective-permute-start.1 = (bf16[128,512]{1,0:T(8,128)(2,1)}, bf16[128,512]{1,0:T(8,128)(2,1)S(1)}, u32[]{:S(2)}, u32[]{:S(2)}) collective-permute-start(bf16[128,512]{1,0:T(8,128)(2,1)} %w0.1), channel_id=1, source_target_pairs={{0,2},{1,3},{2,0},{3,1},{4,6},{5,7},{6,4},{7,5},{8,10},{9,11},{10,... | collective-permute-start | bytes 393224 | tf_op jit(solution)/shard_map/ppermute | solution.py:702
  4.7 22.7 %attention_forward.1 = (bf16[2048,512]{1,0:T(8,128)(2,1)}, bf16[2048,128]{1,0:T(8,128)(2,1)}, bf16[2048,128]{1,0:T(8,128)(2,1)}, bf16[2048,128]{1,0:T(8,128)(2,1...) custom-call(s32[1]{0:T(128)S(6)} %copy.48.kind, ...), custom_call_target="tpu_custom_call" | custom-call | flops 27499999232 | bytes 1024 | tf_op jit(solution)/shard_map/attention_forward/pallas_call | solution.py:213
  28.0 1.9 %collective-permute-start.5 = (bf16[1024,128]{1,0:T(8,128)(2,1)}, bf16[1024,128]{1,0:T(8,128)(2,1)S(1)}, u32[]{:S(2)}, u32[]{:S(2)}) collective-permute-start(bf16[1024,128]{1,0:T(8,128)(2,1)} %get-tuple-element.87.own_att), channel_id=1, source_target_pairs={{0,2},{1,3},{2,0},{3,1},{4,6},{5,7},{6,4},{7,5},{8,10},{9,11},{10,... | collective-permute-start | bytes 786440 | tf_op jit(solution)/shard_map/ppermute | solution.py:702
  30.8 6.6 %collective-permute-done.5.a2 = bf16[1024,128]{1,0:T(8,128)(2,1)S(1)} collective-permute-done((bf16[1024,128]{1,0:T(8,128)(2,1)}, bf16[1024,128]{1,0:T(8,128)(2,1)S(1)}, u32[]{:S(2)}, u32[]{:S(2)}) %collective-permute-start.5) | collective-permute-done | bytes 262176 | tf_op jit(solution)/shard_map/ppermute | solution.py:702
  37.4 4.5 %collective-permute-done.6.a3 = bf16[1024,128]{1,0:T(8,128)(2,1)S(1)} collective-permute-done((bf16[1024,128]{1,0:T(8,128)(2,1)}, bf16[1024,128]{1,0:T(8,128)(2,1)S(1)}, u32[]{:S(2)}, u32[]{:S(2)}) %collective-permute-start.6) | collective-permute-done | bytes 262176 | tf_op jit(solution)/shard_map/ppermute | solution.py:702
  41.9 0.6 copy-done.18
  42.9 15.4 %feed.1 = (bf16[512,512]{1,0:T(8,128)(2,1)}, bf16[512,512]{1,0:T(8,128)(2,1)}, bf16[1024,512]{1,0:T(8,128)(2,1)}, bf16[512,512]{1,0:T(8,128)(2,1)}, f32[2,512]{1...) custom-call(s32[4]{0:T(128)} %pad_add_fusion.place, bf16[4,2,256,512]{3,2,1,0:T(8,128)(2,1)} %bitcast.44, ...), custom_call_target="tpu_custom_call" | custom-call | flops 14300000256 | bytes 1024 | tf_op jit(solution)/shard_map/feed/pallas_call | solution.py:535
  58.7 1.7 collective-permute-start.9
  60.5 0.8 collective-permute-done.18
  61.2 2.5 %add_convert_fusion.1 = bf16[8,128,512]{2,1,0:T(8,128)(2,1)} fusion(bf16[8,128,512]{2,1,0:T(8,128)(2,1)S(1)} %collective-permute-done.18, bf16[8,128,512]{2,1,0:T(8,128)(2,1)} %get-tuple-element.128), kind=kLoop, calls=%fused_computation.2 | loop fusion | flops 2097152 | bytes 3145728 | tf_op jit(solution)/shard_map/convert_element_type | solution.py:863
  63.8 6.0 %all-to-all-start = ((bf16[8,128,512]{2,1,0:T(8,128)(2,1)}), bf16[8,128,512]{2,1,0:T(8,128)(2,1)S(1)}, u32[]{:S(2)}, u32[]{:S(2)}) async-start(bf16[8,128,512]{2,1,0:T(8,128)(2,1)} %add_convert_fusion.1), calls=%async_computation | async-start | bytes 2097152 | tf_op jit(solution)/shard_map/all_to_all | solution.py:731
  69.8 3.1 %collective-permute-done.9.got = bf16[512,512]{1,0:T(8,128)(2,1)S(1)} collective-permute-done((bf16[512,512]{1,0:T(8,128)(2,1)}, bf16[512,512]{1,0:T(8,128)(2,1)S(1)}, u32[]{:S(2)}, u32[]{:S(2)}) %collective-permute-start.9) | collective-permute-done | bytes 524320 | tf_op jit(solution)/shard_map/ppermute | solution.py:702
  72.9 0.8 copy-done.15
  73.7 5.0 %turn.1 = (bf16[512,512]{1,0:T(8,128)(2,1)}, f32[3,512]{1,0:T(4,128)}, bf16[512,128]{1,0:T(8,128)(2,1)}, bf16[512,128]{1,0:T(8,128)(2,1)}, bf16[512,128]{1,0:T(8...) custom-call(s32[4]{0:T(128)} %pad_add_fusion.place, ...), custom_call_target="tpu_custom_call" | custom-call | flops 65999998976 | bytes 1024 | tf_op jit(solution)/shard_map/turn/pallas_call | solution.py:600
  79.2 1.7 collective-permute-start.11
  81.0 1.5 collective-permute-start.17
  82.5 1.3 pad_maximum_fusion.6.sums
  84.5 1.2 collective-permute-done.11.d2
  85.7 2.2 %collective-permute-done.12.d3 = bf16[512,128]{1,0:T(8,128)(2,1)S(1)} collective-permute-done((bf16[512,128]{1,0:T(8,128)(2,1)}, bf16[512,128]{1,0:T(8,128)(2,1)S(1)}, u32[]{:S(2)}, u32[]{:S(2)}) %collective-permute-start.12) | collective-permute-done | bytes 131104 | tf_op jit(solution)/shard_map/ppermute | solution.py:702
  87.9 0.6 copy-done.24
  88.6 28.6 %attention_backward.1 = (bf16[336,512]{1,0:T(8,128)(2,1)}, bf16[320,512]{1,0:T(8,128)(2,1)}, bf16[16,512]{1,0:T(8,128)(2,1)}, bf16[1024,512]{1,0:T(8,128)(2,1)}, bf16[1024,512]{1,0:T(8,128)(2,1)}) custom-call(s32[1]{0:T(128)S(6)} %copy.48.kind, s32[4]{0:T(128)} %pad_add_fusion.place, bf16[2048,4096]{1,0:T(8,128)(2,1)} %get-tuple-element.84.p, ...), custom_call_target="tpu_custom_call" | custom-call | flops 8800000000 | bytes 1024 | tf_op jit(solution)/shard_map/attention_backward/pallas_call | solution.py:402
  117.3 0.6 copy-done.7
  118.0 0.7 collective-permute-start.20
  118.7 1.2 broadcast_multiply_fusion.1
  119.8 1.8 %add_convert_fusion.3 = bf16[336,512]{1,0:T(8,128)(2,1)} fusion(f32[128,512]{1,0:T(8,128)S(1)} %get-tuple-element.162, bf16[336,512]{1,0:T(8,128)(2,1)} %get-tuple-element.135), kind=kLoop, calls=%fused_computation.5 | loop fusion | flops 516096 | bytes 950272 | tf_op jit(solution)/shard_map/convert_element_type | solution.py:889
  121.6 1.0 add_convert_fusion.2
  122.9 4.0 %collective-permute-start.19 = (bf16[336,512]{1,0:T(8,128)(2,1)}, bf16[336,512]{1,0:T(8,128)(2,1)S(1)}, u32[]{:S(2)}, u32[]{:S(2)}) collective-permute-start(bf16[336,512]{1,0:T(8,128)(2,1)} %add_convert_fusion.3), channel_id=1, source_target_pairs={{0,4},{4,0},{8,12},{12,8},{16,20},{20,16},{24,28},{28,24},{1,5},{5... | collective-permute-start | bytes 1032200 | tf_op jit(solution)/shard_map/ppermute | solution.py:702
  126.9 1.5 collective-permute-start.21
  128.4 3.5 %collective-permute-done.32 = bf16[128,512]{1,0:T(8,128)(2,1)S(1)} collective-permute-done((bf16[128,512]{1,0:T(8,128)(2,1)S(1)}, bf16[128,512]{1,0:T(8,128)(2,1)S(1)}, u32[]{:S(2)}, u32[]{:S(2)}) %collective-permute-start.32) | collective-permute-done | bytes 131104 | tf_op jit(solution)/shard_map/ppermute | solution.py:702
  132.1 1.9 %add_convert_fusion.m0 = bf16[1024,512]{1,0:T(8,128)(2,1)S(1)} fusion(bf16[1024,512]{1,0:T(8,128)(2,1)} %collective-permute-done.17, bf16[1024,512]{1,0:T(8,128)(2,1)} %get-tuple-element.127), kind=kLoop, calls=%fused_computation.1 | loop fusion | flops 2097152 | bytes 3145728 | tf_op jit(solution)/shard_map/convert_element_type | solution.py:899
  134.1 5.4 %collective-permute-done.33 = bf16[256,512]{1,0:T(8,128)(2,1)S(1)} collective-permute-done((bf16[256,512]{1,0:T(8,128)(2,1)S(1)}, bf16[256,512]{1,0:T(8,128)(2,1)S(1)}, u32[]{:S(2)}, u32[]{:S(2)}) %collective-permute-start.33) | collective-permute-done | bytes 262176 | tf_op jit(solution)/shard_map/ppermute | solution.py:702
  139.5 0.9 collective-permute-done.21.got
  140.7 1.9 %collective-permute-start.22 = (bf16[176,512]{1,0:T(8,128)(2,1)S(1)}, bf16[176,512]{1,0:T(8,128)(2,1)S(1)}, u32[]{:S(2)}, u32[]{:S(2)}) collective-permute-start(bf16[176,512]{1,0:T(8,128)(2,1)S(1)} %pad_maximum_fusion.4), channel_id=1, source_target_pairs={{0,8},{4,12},{8,0},{12,4},{16,24},{20,28},{24,16},{28,20},{1,9},{5... | collective-permute-start | bytes 540680 | tf_op jit(solution)/shard_map/ppermute | solution.py:702
  143.1 3.1 %collective-permute-done.22 = bf16[176,512]{1,0:T(8,128)(2,1)S(1)} collective-permute-done((bf16[176,512]{1,0:T(8,128)(2,1)S(1)}, bf16[176,512]{1,0:T(8,128)(2,1)S(1)}, u32[]{:S(2)}, u32[]{:S(2)}) %collective-permute-start.22) | collective-permute-done | bytes 180256 | tf_op jit(solution)/shard_map/ppermute | solution.py:702
  146.4 0.7 collective-permute-start.23
  147.1 3.9 %close.1.g0 = bf16[512,512]{1,0:T(8,128)(2,1)} custom-call(s32[4]{0:T(128)} %pad_add_fusion.place, bf16[1024,512]{1,0:T(8,128)(2,1)} %get-tuple-element.136.keep0.keep1, bf16[1024,512]{1,0:T(8,128)(2,1)} %get-tuple-element.136.keep0.keep1, bf16[1024,512]{1,0:T(8,128)(2,1)} %copy-done.3, bf16[1024,512]{1,0:T(8,128)(2,1)} %copy-done.3, ...), custom_call_target="tpu_custom_call" | custom-call | flops 2200000000 | bytes 1024 | tf_op jit(solution)/shard_map/close/pallas_call | solution.py:643
  151.0 1.5 collective-permute-start.28
  152.6 2.6 %collective-permute-done.23 = bf16[176,512]{1,0:T(8,128)(2,1)S(1)} collective-permute-done((bf16[176,512]{1,0:T(8,128)(2,1)S(1)}, bf16[176,512]{1,0:T(8,128)(2,1)S(1)}, u32[]{:S(2)}, u32[]{:S(2)}) %collective-permute-start.23) | collective-permute-done | bytes 180256 | tf_op jit(solution)/shard_map/ppermute | solution.py:702
  156.1 4.5 %collective-permute-done.24 = bf16[160,512]{1,0:T(8,128)(2,1)S(1)} collective-permute-done((bf16[160,512]{1,0:T(8,128)(2,1)S(1)}, bf16[160,512]{1,0:T(8,128)(2,1)S(1)}, u32[]{:S(2)}, u32[]{:S(2)}) %collective-permute-start.24) | collective-permute-done | bytes 163872 | tf_op jit(solution)/shard_map/ppermute | solution.py:702
  160.8 1.6 fusion.6
  162.4 2.8 %collective-permute-start.25 = (bf16[320,512]{1,0:T(8,128)(2,1)S(1)}, bf16[320,512]{1,0:T(8,128)(2,1)S(1)}, u32[]{:S(2)}, u32[]{:S(2)}) collective-permute-start(bf16[320,512]{1,0:T(8,128)(2,1)S(1)} %pad_maximum_fusion.2), channel_id=1, source_target_pairs={{0,4},{4,0},{8,12},{12,8},{16,20},{20,16},{24,28},{28,24},{1,5},{5... | collective-permute-start | bytes 983048 | tf_op jit(solution)/shard_map/ppermute | solution.py:702
  165.5 1.6 collective-permute-start.31
  168.2 1.1 collective-permute-done.31
  169.3 0.6 fusion.8
  170.0 2.7 %collect.1 = (bf16[2048,512]{1,0:T(8,128)(2,1)}, bf16[2048,512]{1,0:T(8,128)(2,1)}) custom-call(s32[4]{0:T(128)S(1)} %copy-done.1, bf16[1024,512]{1,0:T(8,128)(2,1)S(1)} %add_convert_fusion.m0, bf16[1024,512]{1,0:T(8,128)(2,1)S(1)} %collective-permute-done.26.m1, bf16[512,512]{1,0:T(8,128)(2,1)S(1)} %copy-done, ...), custom_call_target="tpu_custom_call" | custom-call | flops 3300000000 | bytes 1024 | tf_op jit(solution)/shard_map/collect/pallas_call | solution.py:687
  172.7 0.9 collective-permute-done.25
  173.9 1.0 fusion.7
  174.9 0.7 slice.128
  (126 shorter events, 8.3 us)
Async XLA Ops:
  0.7 26.7 %collective-permute-start = (bf16[128,512]{1,0:T(8,128)(2,1)}, bf16[128,512]{1,0:T(8,128)(2,1)S(1)}, u32[]{:S(2)}, u32[]{:S(2)}) collective-permute-start(bf16[128,512]{1,0:T(8,128)(2,1)} %w0.1), channel_id=1, source_target_pairs={{0,1},{1,0},{2,3},{3,2},{4,5},{5,4},{6,7},{7,6},{8,9},{9,8},{10,11... | collective-permute-start | bytes 393224 | tf_op jit(solution)/shard_map/ppermute | solution.py:702
  1.2 26.2 %collective-permute-start.1 = (bf16[128,512]{1,0:T(8,128)(2,1)}, bf16[128,512]{1,0:T(8,128)(2,1)S(1)}, u32[]{:S(2)}, u32[]{:S(2)}) collective-permute-start(bf16[128,512]{1,0:T(8,128)(2,1)} %w0.1), channel_id=1, source_target_pairs={{0,2},{1,3},{2,0},{3,1},{4,6},{5,7},{6,4},{7,5},{8,10},{9,11},{10,... | collective-permute-start | bytes 393224 | tf_op jit(solution)/shard_map/ppermute | solution.py:702
  3.8 23.6 %collective-permute-start.2 = (bf16[128,512]{1,0:T(8,128)(2,1)}, bf16[128,512]{1,0:T(8,128)(2,1)S(1)}, u32[]{:S(2)}, u32[]{:S(2)}) collective-permute-start(bf16[128,512]{1,0:T(8,128)(2,1)} %w0.1), channel_id=1, source_target_pairs={{0,3},{1,2},{2,1},{3,0},{4,7},{5,6},{6,5},{7,4},{8,11},{9,10},{10,... | collective-permute-start | bytes 393224 | tf_op jit(solution)/shard_map/ppermute | solution.py:702
  3.8 23.5 %collective-permute-start.3 = (f32[1,512]{1,0:T(1,128)}, f32[1,512]{1,0:T(1,128)S(1)}, u32[]{:S(2)}, u32[]{:S(2)}) collective-permute-start(f32[1,512]{1,0:T(1,128)} %bitcast.66), channel_id=1, source_target_pairs={{0,1},{1,0},{2,3},{3,2},{4,5},{5,4},{6,7},{7,6},{8,9},{9,8},{10,11... | collective-permute-start | bytes 6152 | tf_op jit(solution)/shard_map/ppermute | solution.py:702
  4.6 22.8 %copy-start.11 = (bf16[512,512]{1,0:T(8,128)(2,1)S(1)}, bf16[512,512]{1,0:T(8,128)(2,1)}, u32[]{:S(2)}) copy-start(bf16[512,512]{1,0:T(8,128)(2,1)} %i0.1) | copy-start | bytes 1572868
  4.6 23.2 %copy-start.12 = (bf16[512,512]{1,0:T(8,128)(2,1)S(1)}, bf16[512,512]{1,0:T(8,128)(2,1)}, u32[]{:S(2)}) copy-start(bf16[512,512]{1,0:T(8,128)(2,1)} %u0.1) | copy-start | bytes 1572868
  27.4 14.5 %copy-start.25 = (f32[1,512]{1,0:T(1,128)}, f32[1,512]{1,0:T(1,128)S(1)}, u32[]{:S(2)}) copy-start(f32[1,512]{1,0:T(1,128)S(1)} %collective-permute-done.3.b1) | copy-start | bytes 6148
  27.4 14.5 %copy-start.19 = (bf16[128,512]{1,0:T(8,128)(2,1)}, bf16[128,512]{1,0:T(8,128)(2,1)S(1)}, u32[]{:S(2)}) copy-start(bf16[128,512]{1,0:T(8,128)(2,1)S(1)} %collective-permute-done.w1) | copy-start | bytes 393220
  27.4 14.5 %copy-start.20 = (bf16[128,512]{1,0:T(8,128)(2,1)}, bf16[128,512]{1,0:T(8,128)(2,1)S(1)}, u32[]{:S(2)}) copy-start(bf16[128,512]{1,0:T(8,128)(2,1)S(1)} %collective-permute-done.1.w2) | copy-start | bytes 393220
  27.4 14.5 %copy-start.21 = (bf16[128,512]{1,0:T(8,128)(2,1)}, bf16[128,512]{1,0:T(8,128)(2,1)S(1)}, u32[]{:S(2)}) copy-start(bf16[128,512]{1,0:T(8,128)(2,1)S(1)} %collective-permute-done.2.w3) | copy-start | bytes 393220
  27.4 14.4 %collective-permute-start.7 = (bf16[512,512]{1,0:T(8,128)(2,1)S(1)}, bf16[512,512]{1,0:T(8,128)(2,1)S(1)}, u32[]{:S(2)}, u32[]{:S(2)}) collective-permute-start(bf16[512,512]{1,0:T(8,128)(2,1)S(1)} %copy-done.11), channel_id=1, source_target_pairs={{0,1},{1,0},{2,3},{3,2},{4,5},{5,4},{6,7},{7,6},{8,9},{9,8},{10,11... | collective-permute-start | bytes 1572872 | tf_op jit(solution)/shard_map/ppermute | solution.py:702
  27.9 14.0 %collective-permute-start.8 = (bf16[512,512]{1,0:T(8,128)(2,1)S(1)}, bf16[512,512]{1,0:T(8,128)(2,1)S(1)}, u32[]{:S(2)}, u32[]{:S(2)}) collective-permute-start(bf16[512,512]{1,0:T(8,128)(2,1)S(1)} %copy-done.12), channel_id=1, source_target_pairs={{0,1},{1,0},{2,3},{3,2},{4,5},{5,4},{6,7},{7,6},{8,9},{9,8},{10,11... | collective-permute-start | bytes 1572872 | tf_op jit(solution)/shard_map/ppermute | solution.py:702
  28.0 9.3 %collective-permute-start.5 = (bf16[1024,128]{1,0:T(8,128)(2,1)}, bf16[1024,128]{1,0:T(8,128)(2,1)S(1)}, u32[]{:S(2)}, u32[]{:S(2)}) collective-permute-start(bf16[1024,128]{1,0:T(8,128)(2,1)} %get-tuple-element.87.own_att), channel_id=1, source_target_pairs={{0,2},{1,3},{2,0},{3,1},{4,6},{5,7},{6,4},{7,5},{8,10},{9,11},{10,... | collective-permute-start | bytes 786440 | tf_op jit(solution)/shard_map/ppermute | solution.py:702
  30.0 7.4 %collective-permute-start.4 = (bf16[1024,128]{1,0:T(8,128)(2,1)}, bf16[1024,128]{1,0:T(8,128)(2,1)S(1)}, u32[]{:S(2)}, u32[]{:S(2)}) collective-permute-start(bf16[1024,128]{1,0:T(8,128)(2,1)} %get-tuple-element.88), channel_id=1, source_target_pairs={{0,1},{1,0},{2,3},{3,2},{4,5},{5,4},{6,7},{7,6},{8,9},{9,8},{10,11... | collective-permute-start | bytes 786440 | tf_op jit(solution)/shard_map/ppermute | solution.py:702
  30.0 11.9 %collective-permute-start.6 = (bf16[1024,128]{1,0:T(8,128)(2,1)}, bf16[1024,128]{1,0:T(8,128)(2,1)S(1)}, u32[]{:S(2)}, u32[]{:S(2)}) collective-permute-start(bf16[1024,128]{1,0:T(8,128)(2,1)} %get-tuple-element.88), channel_id=1, source_target_pairs={{0,3},{1,2},{2,1},{3,0},{4,7},{5,6},{6,5},{7,4},{8,11},{9,10},{10,... | collective-permute-start | bytes 786440 | tf_op jit(solution)/shard_map/ppermute | solution.py:702
  58.3 3.0 %collective-permute-start.18 = (bf16[8,128,512]{2,1,0:T(8,128)(2,1)}, bf16[8,128,512]{2,1,0:T(8,128)(2,1)S(1)}, u32[]{:S(2)}, u32[]{:S(2)}) collective-permute-start(bf16[8,128,512]{2,1,0:T(8,128)(2,1)} %get-tuple-element.129), channel_id=1, source_target_pairs={{0,1},{1,0},{2,3},{3,2},{4,5},{5,4},{6,7},{7,6},{8,9},{9,8},{10,11... | collective-permute-start | bytes 3145736 | tf_op jit(solution)/shard_map/ppermute | solution.py:702
  58.7 14.1 %collective-permute-start.9 = (bf16[512,512]{1,0:T(8,128)(2,1)}, bf16[512,512]{1,0:T(8,128)(2,1)S(1)}, u32[]{:S(2)}, u32[]{:S(2)}) collective-permute-start(bf16[512,512]{1,0:T(8,128)(2,1)} %get-tuple-element.98), channel_id=1, source_target_pairs={{0,2},{1,3},{2,0},{3,1},{4,6},{5,7},{6,4},{7,5},{8,10},{9,11},{10,... | collective-permute-start | bytes 1572872 | tf_op jit(solution)/shard_map/ppermute | solution.py:702
  63.8 53.5 %all-to-all-start = ((bf16[8,128,512]{2,1,0:T(8,128)(2,1)}), bf16[8,128,512]{2,1,0:T(8,128)(2,1)S(1)}, u32[]{:S(2)}, u32[]{:S(2)}) async-start(bf16[8,128,512]{2,1,0:T(8,128)(2,1)} %add_convert_fusion.1), calls=%async_computation | async-start | bytes 2097152 | tf_op jit(solution)/shard_map/all_to_all | solution.py:731
  73.7 7.3 %copy-start.4 = (bf16[1024,512]{1,0:T(8,128)(2,1)S(1)}, bf16[1024,512]{1,0:T(8,128)(2,1)}, u32[]{:S(2)}) copy-start(bf16[1024,512]{1,0:T(8,128)(2,1)} %get-tuple-element.127) | copy-start | bytes 3145732
  78.7 2.2 %collective-permute-start.10 = (bf16[512,128]{1,0:T(8,128)(2,1)}, bf16[512,128]{1,0:T(8,128)(2,1)S(1)}, u32[]{:S(2)}, u32[]{:S(2)}) collective-permute-start(bf16[512,128]{1,0:T(8,128)(2,1)} %get-tuple-element.101), channel_id=1, source_target_pairs={{0,1},{1,0},{2,3},{3,2},{4,5},{5,4},{6,7},{7,6},{8,9},{9,8},{10,11... | collective-permute-start | bytes 393224 | tf_op jit(solution)/shard_map/ppermute | solution.py:702
  78.8 3.7 %collective-permute-start.13 = (f32[1,512]{1,0:T(1,128)S(1)}, f32[1,512]{1,0:T(1,128)S(1)}, u32[]{:S(2)}, u32[]{:S(2)}) collective-permute-start(f32[1,512]{1,0:T(1,128)S(1)} %slice.86), channel_id=1, source_target_pairs={{0,1},{1,0},{2,3},{3,2},{4,5},{5,4},{6,7},{7,6},{8,9},{9,8},{10,11... | collective-permute-start | bytes 6152 | tf_op jit(solution)/shard_map/ppermute | solution.py:702
  79.2 6.5 %collective-permute-start.11 = (bf16[512,128]{1,0:T(8,128)(2,1)}, bf16[512,128]{1,0:T(8,128)(2,1)S(1)}, u32[]{:S(2)}, u32[]{:S(2)}) collective-permute-start(bf16[512,128]{1,0:T(8,128)(2,1)} %get-tuple-element.102), channel_id=1, source_target_pairs={{0,2},{1,3},{2,0},{3,1},{4,6},{5,7},{6,4},{7,5},{8,10},{9,11},{10,... | collective-permute-start | bytes 393224 | tf_op jit(solution)/shard_map/ppermute | solution.py:702
  80.9 7.0 %collective-permute-start.12 = (bf16[512,128]{1,0:T(8,128)(2,1)}, bf16[512,128]{1,0:T(8,128)(2,1)S(1)}, u32[]{:S(2)}, u32[]{:S(2)}) collective-permute-start(bf16[512,128]{1,0:T(8,128)(2,1)} %get-tuple-element.103), channel_id=1, source_target_pairs={{0,3},{1,2},{2,1},{3,0},{4,7},{5,6},{6,5},{7,4},{8,11},{9,10},{10,... | collective-permute-start | bytes 393224 | tf_op jit(solution)/shard_map/ppermute | solution.py:702
  81.0 36.3 %collective-permute-start.17 = (bf16[1024,512]{1,0:T(8,128)(2,1)S(1)}, bf16[1024,512]{1,0:T(8,128)(2,1)}, u32[]{:S(2)}, u32[]{:S(2)}) collective-permute-start(bf16[1024,512]{1,0:T(8,128)(2,1)S(1)} %copy-done.4), channel_id=1, source_target_pairs={{0,2},{1,3},{2,0},{3,1},{4,6},{5,7},{6,4},{7,5},{8,10},{9,11},{10,... | collective-permute-start | bytes 3145736 | tf_op jit(solution)/shard_map/ppermute | solution.py:702
  83.8 33.5 %collective-permute-start.14 = (bf16[128,512]{1,0:T(8,128)(2,1)}, bf16[128,512]{1,0:T(8,128)(2,1)S(1)}, u32[]{:S(2)}, u32[]{:S(2)}) collective-permute-start(bf16[128,512]{1,0:T(8,128)(2,1)} %get-tuple-element.123), channel_id=1, source_target_pairs={{0,1},{1,0},{2,3},{3,2},{4,5},{5,4},{6,7},{7,6},{8,9},{9,8},{10,11... | collective-permute-start | bytes 393224 | tf_op jit(solution)/shard_map/ppermute | solution.py:702
  84.2 33.1 %collective-permute-start.15 = (bf16[128,512]{1,0:T(8,128)(2,1)}, bf16[128,512]{1,0:T(8,128)(2,1)S(1)}, u32[]{:S(2)}, u32[]{:S(2)}) collective-permute-start(bf16[128,512]{1,0:T(8,128)(2,1)} %get-tuple-element.124), channel_id=1, source_target_pairs={{0,2},{1,3},{2,0},{3,1},{4,6},{5,7},{6,4},{7,5},{8,10},{9,11},{10,... | collective-permute-start | bytes 393224 | tf_op jit(solution)/shard_map/ppermute | solution.py:702
  85.7 31.5 %collective-permute-start.16 = (bf16[128,512]{1,0:T(8,128)(2,1)}, bf16[128,512]{1,0:T(8,128)(2,1)S(1)}, u32[]{:S(2)}, u32[]{:S(2)}) collective-permute-start(bf16[128,512]{1,0:T(8,128)(2,1)} %get-tuple-element.125), channel_id=1, source_target_pairs={{0,3},{1,2},{2,1},{3,0},{4,7},{5,6},{6,5},{7,4},{8,11},{9,10},{10,... | collective-permute-start | bytes 393224 | tf_op jit(solution)/shard_map/ppermute | solution.py:702
  118.0 3.6 %collective-permute-start.20 = (bf16[1024,512]{1,0:T(8,128)(2,1)}, bf16[1024,512]{1,0:T(8,128)(2,1)S(1)}, u32[]{:S(2)}, u32[]{:S(2)}) collective-permute-start(bf16[1024,512]{1,0:T(8,128)(2,1)} %get-tuple-element.137), channel_id=1, source_target_pairs={{0,1},{1,0},{2,3},{3,2},{4,5},{5,4},{6,7},{7,6},{8,9},{9,8},{10,11... | collective-permute-start | bytes 3145736 | tf_op jit(solution)/shard_map/ppermute | solution.py:702
  121.6 12.4 %copy-start.3 = (bf16[1024,512]{1,0:T(8,128)(2,1)}, bf16[1024,512]{1,0:T(8,128)(2,1)S(1)}, u32[]{:S(2)}) copy-start(bf16[1024,512]{1,0:T(8,128)(2,1)S(1)} %collective-permute-done.20.near0.near1) | copy-start | bytes 3145732
  122.8 9.2 %collective-permute-start.32 = (bf16[128,512]{1,0:T(8,128)(2,1)S(1)}, bf16[128,512]{1,0:T(8,128)(2,1)S(1)}, u32[]{:S(2)}, u32[]{:S(2)}) collective-permute-start(bf16[128,512]{1,0:T(8,128)(2,1)S(1)} %reduce_sum.12), channel_id=1, source_target_pairs={{0,16},{4,20},{8,24},{12,28},{16,0},{20,4},{24,8},{28,12},{1,17},{... | collective-permute-start | bytes 393224 | tf_op jit(solution)/shard_map/ppermute | solution.py:702
  122.9 16.6 %collective-permute-start.19 = (bf16[336,512]{1,0:T(8,128)(2,1)}, bf16[336,512]{1,0:T(8,128)(2,1)S(1)}, u32[]{:S(2)}, u32[]{:S(2)}) collective-permute-start(bf16[336,512]{1,0:T(8,128)(2,1)} %add_convert_fusion.3), channel_id=1, source_target_pairs={{0,4},{4,0},{8,12},{12,8},{16,20},{20,16},{24,28},{28,24},{1,5},{5... | collective-permute-start | bytes 1032200 | tf_op jit(solution)/shard_map/ppermute | solution.py:702
  126.9 13.5 %collective-permute-start.21 = (bf16[512,512]{1,0:T(8,128)(2,1)}, bf16[512,512]{1,0:T(8,128)(2,1)S(1)}, u32[]{:S(2)}, u32[]{:S(2)}) collective-permute-start(bf16[512,512]{1,0:T(8,128)(2,1)} %bitcast.50), channel_id=1, source_target_pairs={{0,2},{1,3},{2,0},{3,1},{4,6},{5,7},{6,4},{7,5},{8,10},{9,11},{10,... | collective-permute-start | bytes 1572872 | tf_op jit(solution)/shard_map/ppermute | solution.py:702
  132.0 8.5 %copy-start.9 = (bf16[16,512]{1,0:T(8,128)(2,1)S(1)}, bf16[16,512]{1,0:T(8,128)(2,1)}, u32[]{:S(2)}) copy-start(bf16[16,512]{1,0:T(8,128)(2,1)} %get-tuple-element.139) | copy-start | bytes 49156
  132.0 8.5 %copy-start.6 = (bf16[320,512]{1,0:T(8,128)(2,1)S(1)}, bf16[320,512]{1,0:T(8,128)(2,1)}, u32[]{:S(2)}) copy-start(bf16[320,512]{1,0:T(8,128)(2,1)} %get-tuple-element.130) | copy-start | bytes 983044
  132.0 7.4 %collective-permute-start.33 = (bf16[256,512]{1,0:T(8,128)(2,1)S(1)}, bf16[256,512]{1,0:T(8,128)(2,1)S(1)}, u32[]{:S(2)}, u32[]{:S(2)}) collective-permute-start(bf16[256,512]{1,0:T(8,128)(2,1)S(1)} %pad_maximum_fusion.3), channel_id=1, source_target_pairs={{0,8},{4,12},{8,0},{12,4},{16,24},{20,28},{24,16},{28,20},{1,9},{5... | collective-permute-start | bytes 786440 | tf_op jit(solution)/shard_map/ppermute | solution.py:702
  134.0 35.9 %collective-permute-start.26 = (bf16[1024,512]{1,0:T(8,128)(2,1)S(1)}, bf16[1024,512]{1,0:T(8,128)(2,1)S(1)}, u32[]{:S(2)}, u32[]{:S(2)}) collective-permute-start(bf16[1024,512]{1,0:T(8,128)(2,1)S(1)} %add_convert_fusion.m0), channel_id=1, source_target_pairs={{0,1},{1,0},{2,3},{3,2},{4,5},{5,4},{6,7},{7,6},{8,9},{9,8},{10,11... | collective-permute-start | bytes 3145736 | tf_op jit(solution)/shard_map/ppermute | solution.py:702
  140.7 5.6 %collective-permute-start.22 = (bf16[176,512]{1,0:T(8,128)(2,1)S(1)}, bf16[176,512]{1,0:T(8,128)(2,1)S(1)}, u32[]{:S(2)}, u32[]{:S(2)}) collective-permute-start(bf16[176,512]{1,0:T(8,128)(2,1)S(1)} %pad_maximum_fusion.4), channel_id=1, source_target_pairs={{0,8},{4,12},{8,0},{12,4},{16,24},{20,28},{24,16},{28,20},{1,9},{5... | collective-permute-start | bytes 540680 | tf_op jit(solution)/shard_map/ppermute | solution.py:702
  142.8 12.6 %collective-permute-start.34 = (bf16[512,512]{1,0:T(8,128)(2,1)S(1)}, bf16[512,512]{1,0:T(8,128)(2,1)S(1)}, u32[]{:S(2)}, u32[]{:S(2)}) collective-permute-start(bf16[512,512]{1,0:T(8,128)(2,1)S(1)} %pad_maximum_fusion.1), channel_id=1, source_target_pairs={{0,4},{4,0},{8,12},{12,8},{16,20},{20,16},{24,28},{28,24},{1,5},{5... | collective-permute-start | bytes 1572872 | tf_op jit(solution)/shard_map/ppermute | solution.py:702
  146.4 8.8 %collective-permute-start.23 = (bf16[176,512]{1,0:T(8,128)(2,1)S(1)}, bf16[176,512]{1,0:T(8,128)(2,1)S(1)}, u32[]{:S(2)}, u32[]{:S(2)}) collective-permute-start(bf16[176,512]{1,0:T(8,128)(2,1)S(1)} %pad_maximum_fusion.5), channel_id=1, source_target_pairs={{0,16},{4,20},{8,24},{12,28},{16,0},{20,4},{24,8},{28,12},{1,17},{... | collective-permute-start | bytes 540680 | tf_op jit(solution)/shard_map/ppermute | solution.py:702
  151.0 14.2 %collective-permute-start.28 = (bf16[512,512]{1,0:T(8,128)(2,1)}, bf16[512,512]{1,0:T(8,128)(2,1)S(1)}, u32[]{:S(2)}, u32[]{:S(2)}) collective-permute-start(bf16[512,512]{1,0:T(8,128)(2,1)} %close.1.g0), channel_id=1, source_target_pairs={{0,2},{1,3},{2,0},{3,1},{4,6},{5,7},{6,4},{7,5},{8,10},{9,11},{10,... | collective-permute-start | bytes 1572872 | tf_op jit(solution)/shard_map/ppermute | solution.py:702
  152.6 17.4 %collective-permute-start.27 = (bf16[512,512]{1,0:T(8,128)(2,1)}, bf16[512,512]{1,0:T(8,128)(2,1)S(1)}, u32[]{:S(2)}, u32[]{:S(2)}) collective-permute-start(bf16[512,512]{1,0:T(8,128)(2,1)} %close.1.g0), channel_id=1, source_target_pairs={{0,1},{1,0},{2,3},{3,2},{4,5},{5,4},{6,7},{7,6},{8,9},{9,8},{10,11... | collective-permute-start | bytes 1572872 | tf_op jit(solution)/shard_map/ppermute | solution.py:702
  155.3 5.4 %collective-permute-start.24 = (bf16[160,512]{1,0:T(8,128)(2,1)S(1)}, bf16[160,512]{1,0:T(8,128)(2,1)S(1)}, u32[]{:S(2)}, u32[]{:S(2)}) collective-permute-start(bf16[160,512]{1,0:T(8,128)(2,1)S(1)} %fusion.1), channel_id=1, source_target_pairs={{0,8},{4,12},{8,0},{12,4},{16,24},{20,28},{24,16},{28,20},{1,9},{5... | collective-permute-start | bytes 491528 | tf_op jit(solution)/shard_map/ppermute | solution.py:702
  160.7 4.8 %collective-permute-start.30 = (f32[5,512]{1,0:T(8,128)S(1)}, f32[5,512]{1,0:T(8,128)S(1)}, u32[]{:S(2)}, u32[]{:S(2)}) collective-permute-start(f32[5,512]{1,0:T(8,128)S(1)} %slice.119), channel_id=1, source_target_pairs={{0,1},{1,0},{2,3},{3,2},{4,5},{5,4},{6,7},{7,6},{8,9},{9,8},{10,11... | collective-permute-start | bytes 30728 | tf_op jit(solution)/shard_map/ppermute | solution.py:702
  160.8 9.1 %copy-start = (bf16[512,512]{1,0:T(8,128)(2,1)S(1)}, bf16[512,512]{1,0:T(8,128)(2,1)}, u32[]{:S(2)}) copy-start(bf16[512,512]{1,0:T(8,128)(2,1)} %close.1.g0) | copy-start | bytes 1572868
  160.8 9.1 %copy-start.1 = (s32[4]{0:T(128)S(1)}, s32[4]{0:T(128)}, u32[]{:S(2)}) copy-start(s32[4]{0:T(128)} %pad_add_fusion.place) | copy-start | bytes 52
  162.4 11.2 %collective-permute-start.25 = (bf16[320,512]{1,0:T(8,128)(2,1)S(1)}, bf16[320,512]{1,0:T(8,128)(2,1)S(1)}, u32[]{:S(2)}, u32[]{:S(2)}) collective-permute-start(bf16[320,512]{1,0:T(8,128)(2,1)S(1)} %pad_maximum_fusion.2), channel_id=1, source_target_pairs={{0,4},{4,0},{8,12},{12,8},{16,20},{20,16},{24,28},{28,24},{1,5},{5... | collective-permute-start | bytes 983048 | tf_op jit(solution)/shard_map/ppermute | solution.py:702
  165.3 4.7 %collective-permute-start.29 = (bf16[512,512]{1,0:T(8,128)(2,1)S(1)}, bf16[512,512]{1,0:T(8,128)(2,1)S(1)}, u32[]{:S(2)}, u32[]{:S(2)}) collective-permute-start(bf16[512,512]{1,0:T(8,128)(2,1)S(1)} %collective-permute-done.28.g2), channel_id=1, source_target_pairs={{0,1},{1,0},{2,3},{3,2},{4,5},{5,4},{6,7},{7,6},{8,9},{9,8},{10,11... | collective-permute-start | bytes 1572872 | tf_op jit(solution)/shard_map/ppermute | solution.py:702
  165.5 3.8 %collective-permute-start.31 = (f32[5,512]{1,0:T(8,128)S(1)}, f32[5,512]{1,0:T(8,128)S(1)}, u32[]{:S(2)}, u32[]{:S(2)}) collective-permute-start(f32[5,512]{1,0:T(8,128)S(1)} %slice_add_fusion.7), channel_id=1, source_target_pairs={{0,2},{1,3},{2,0},{3,1},{4,6},{5,7},{6,4},{7,5},{8,10},{9,11},{10,... | collective-permute-start | bytes 30728 | tf_op jit(solution)/shard_map/ppermute | solution.py:702
  (14 other events, 35.5 us)
